TPU v7x, 32 devices: a whole 2x2x4 slice. The times are simulated.
32 devices in a mesh: dp: 8 (over z, x), group: 4 (over y, core).
Axes of the slice: x: 2, y: 2, z: 4, core: 2. Of those that a mesh axis runs over, the one named last changes fastest.
Arguments:
- hidden_in: bfloat16 [16, 1024, 1024], P('dp', 'group'), may hold values from -6 to 6
- out_grad: bfloat16 [16, 1024, 1024], P('dp', 'group'), may hold values from -6 to 6
- stretch_order: int32 [8], replicated, may hold values from 0 to 7, as said below
- positions: int32 [16, 1024], P('dp', 'group'), may hold values from 0 to 5118, as said below
- qkv_weight: float32 [1024, 4096], P('group'), may hold values from -0.1875 to 0.1875
- qkv_moment: float32 [1024, 4096], P('group'), may hold values from -128 to 128
- qkv_square: float32 [1024, 4096], P('group'), may hold values from 861.7984 to 13762.56
- out_weight: float32 [2048, 1024], P('group'), may hold values from -1.5 to 1.5
- out_moment: float32 [2048, 1024], P('group'), may hold values from -6 to 6
- out_square: float32 [2048, 1024], P('group'), may hold values from 2.944 to 47.2
- gateup_weight: float32 [1024, 6144], P('group'), may hold values from -0.1875 to 0.1875
- gateup_moment: float32 [1024, 6144], P('group'), may hold values from -48 to 48
- gateup_square: float32 [1024, 6144], P('group'), may hold values from 129.4336 to 2064.384
- down_weight: float32 [3072, 1024], P('group'), may hold values from -0.109375 to 0.109375
- down_moment: float32 [3072, 1024], P('group'), may hold values from -48 to 48
- down_square: float32 [3072, 1024], P('group'), may hold values from 155.648 to 2490.368
- gain_weight: float32 [2304], P('group'), may hold values from 0.5 to 1.5
- gain_moment: float32 [2304], P('group'), may hold values from -246.1863 to 246.1863
- gain_square: float32 [2304], P('group'), may hold values from 655.36 to 221184
Outputs:
- layer_out: bfloat16 [16, 1024, 1024], P('dp', 'group')
- input_grad: bfloat16 [16, 1024, 1024], P('dp', 'group')
- qkv_new: float32 [1024, 4096], P('group')
- qkv_moment_new: float32 [1024, 4096], P('group')
- qkv_square_new: float32 [1024, 4096], P('group')
- out_new: float32 [2048, 1024], P('group')
- out_moment_new: float32 [2048, 1024], P('group')
- out_square_new: float32 [2048, 1024], P('group')
- gateup_new: float32 [1024, 6144], P('group')
- gateup_moment_new: float32 [1024, 6144], P('group')
- gateup_square_new: float32 [1024, 6144], P('group')
- down_new: float32 [3072, 1024], P('group')
- down_moment_new: float32 [3072, 1024], P('group')
- down_square_new: float32 [3072, 1024], P('group')
- gain_new: float32 [2304], P('group')
- gain_moment_new: float32 [2304], P('group')
- gain_square_new: float32 [2304], P('group')
Inputs may be any that keep to these rules, and one draw needn't show every extreme that they name: `stretch_order`: A permutation in which stored pieces 2 i and 2 i + 1 hold pieces that add up to 7. positions[b, p] = start of sequence b plus the place of stored token p; starts are below 4096, one sequence starts at 0 and one at 4095.
All inputs are finite; a program needn't handle non-finite values.
Results may differ from a plain program's by a relative error of at most 0.02.
Values may be sent and summed in bfloat16 or wider, within the bound.
No kernel may reach another device: no remote copies, remote signals or barrier semaphores. Data moves between devices by JAX's collectives and lax.ppermute only.
A program may use at most 256 MiB of HBM per device.

v0:
```python
import jax
import jax.numpy as jnp
from jax import lax
from jax.sharding import PartitionSpec as P

D = 1024
H = 16
KV = 8
HD = 128
FF = 3072
STEP = 10


EPSILON = 1e-06
ROPE_BASE = 1000000.0
BETA_ONE = 0.9
BETA_TWO = 0.95
ADAM_EPSILON = 1e-08
DECAY = 0.1
LR_MULT = 3.0
GAIN_RATE = 0.3
MASKED = -1e30
START_TOP = -1e29


def rms_scale(values, gain):
    mean_square = jnp.mean(values * values, axis=-1, keepdims=True)
    return values * lax.rsqrt(mean_square + EPSILON) * gain


def rotate(values, cosine, sine):
    half = values.shape[-1] // 2
    turned = jnp.concatenate([-values[..., half:], values[..., :half]], axis=-1)
    return values * cosine + turned * sine


def rope_tables(places):
    exponent = jnp.arange(HD // 2, dtype=jnp.float32) * (2.0 / HD)
    inverse = jnp.power(jnp.float32(ROPE_BASE), -exponent)
    angle = places.astype(jnp.float32)[:, None] * inverse[None, :]
    angle = jnp.concatenate([angle, angle], axis=-1)
    return (jnp.cos(angle), jnp.sin(angle))


def split_heads(mixed, query_gain, key_gain, cosine, sine):
    row_count = mixed.shape[0]
    query = mixed[:, : H * HD].reshape(row_count, H, HD)
    keys = mixed[:, H * HD : (H + KV) * HD].reshape(row_count, KV, HD)
    values = mixed[:, (H + KV) * HD :].reshape(row_count, KV, HD)
    query = rotate(rms_scale(query, query_gain), cosine[:, None, :], sine[:, None, :])
    keys = rotate(rms_scale(keys, key_gain), cosine[:, None, :], sine[:, None, :])
    return (query, keys, values)


def gated(gate_up):
    half = gate_up.shape[1] // 2
    return jax.nn.silu(gate_up[:, :half]) * gate_up[:, half:]


def real_places(stretch_list, start, count, half_stretch):
    stored = start + jnp.arange(count, dtype=jnp.int32)
    piece_index = stored // half_stretch
    table = jnp.arange(stretch_list.shape[0], dtype=jnp.int32)
    picked = jnp.sum(
        jnp.where(piece_index[:, None] == table[None, :], stretch_list[None, :], 0), axis=1
    )
    return picked * half_stretch + stored % half_stretch


def by_blocks(block_fn, carry, piece, width):
    count = piece[0].shape[1]

    def advance(state, number):
        sliced = tuple(
            (lax.dynamic_slice_in_dim(member, number * width, width, 1) for member in piece)
        )
        return (block_fn(state, sliced, number * width), None)

    state, unused = lax.scan(advance, carry, jnp.arange(count // width, dtype=jnp.int32))
    return state


def adam_step(weight, moment, square, grad, rate, decay):
    moment_new = BETA_ONE * moment + (1.0 - BETA_ONE) * grad
    square_new = BETA_TWO * square + (1.0 - BETA_TWO) * grad * grad
    ratio = (
        moment_new
        / (1.0 - BETA_ONE**STEP)
        / (jnp.sqrt(square_new / (1.0 - BETA_TWO**STEP)) + ADAM_EPSILON)
    )
    return (weight - rate * (ratio + decay * weight), moment_new, square_new)


def shards(
    hidden_in,
    out_grad,
    stretch_order,
    positions,
    qkv_weight,
    qkv_moment,
    qkv_square,
    out_weight,
    out_moment,
    out_square,
    gateup_weight,
    gateup_moment,
    gateup_square,
    down_weight,
    down_moment,
    down_square,
    gain_weight,
    gain_moment,
    gain_square,
):
    groups = lax.axis_size("group")
    sequences, local_len, width = hidden_in.shape
    half_stretch = local_len // 2
    seq_len = local_len * groups
    ratio = H // KV
    row_count = sequences * local_len
    scale = HD ** (-0.5)
    bf16 = jnp.bfloat16
    f32 = jnp.float32
    w_qkv, w_out, w_gateup, w_down, gains_low = (
        lax.all_gather(qkv_weight.astype(bf16), "group", axis=0, tiled=True),
        lax.all_gather(out_weight.astype(bf16), "group", axis=0, tiled=True),
        lax.all_gather(gateup_weight.astype(bf16), "group", axis=0, tiled=True),
        lax.all_gather(down_weight.astype(bf16), "group", axis=0, tiled=True),
        lax.all_gather(gain_weight.astype(bf16), "group", axis=0, tiled=True),
    )
    gains = gains_low.astype(f32)
    gain_one = gains[:D]
    gain_two = gains[D : 2 * D]
    gain_query = gains[2 * D : 2 * D + HD]
    gain_key = gains[2 * D + HD :]
    member = lax.axis_index("group")
    query_places = real_places(stretch_order, member * local_len, local_len, half_stretch)
    cosine, sine = rope_tables(positions.reshape(row_count))
    tokens = hidden_in.reshape(row_count, width).astype(f32)
    normed, pull_one = jax.vjp(rms_scale, tokens, gain_one)
    normed_low = normed.astype(bf16)
    mixed = jnp.dot(normed_low, w_qkv, preferred_element_type=f32)

    def heads_of(mixed_rows, query_gain, key_gain):
        return split_heads(mixed_rows, query_gain, key_gain, cosine, sine)

    (query, keys, values), pull_heads = jax.vjp(heads_of, mixed, gain_query, gain_key)
    query_low = query.astype(bf16).reshape(sequences, local_len, KV, ratio, HD)
    keys_low = keys.astype(bf16).reshape(sequences, local_len, KV, HD)
    values_low = values.astype(bf16).reshape(sequences, local_len, KV, HD)

    def scores_for(keys_piece, start):
        count = keys_piece.shape[1]
        key_places = real_places(stretch_order, start, count, half_stretch)
        allowed = key_places[None, :] <= query_places[:, None]
        raw_scores = (
            jnp.einsum("sqkrd,spkd->skrqp", query_low, keys_piece, preferred_element_type=f32)
            * scale
        )
        return jnp.where(allowed, raw_scores, MASKED)

    def forward_block(carry, piece, start):
        top_old, total_old, accum_old = carry
        scores = scores_for(piece[0], start)
        top_new = jnp.maximum(top_old, jnp.max(scores, axis=-1))
        factor = jnp.exp(top_old - top_new)
        exp_terms = jnp.exp(scores - top_new[..., None])
        total_new = total_old * factor + jnp.sum(exp_terms, axis=-1)
        update = jnp.einsum(
            "skrqp,spkd->skrqd", exp_terms.astype(bf16), piece[1], preferred_element_type=f32
        )
        return (top_new, total_new, accum_old * factor[..., None] + update)

    start_state = (
        jnp.full((sequences, KV, ratio, local_len), START_TOP, f32),
        jnp.zeros((sequences, KV, ratio, local_len), f32),
        jnp.zeros((sequences, KV, ratio, local_len, HD), f32),
    )
    top, total, accum = by_blocks(
        forward_block,
        start_state,
        (
            lax.all_gather(keys_low, "group", axis=1, tiled=True),
            lax.all_gather(values_low, "group", axis=1, tiled=True),
        ),
        local_len,
    )
    attended = accum / total[..., None]
    log_total = top + jnp.log(total)
    attended_low = jnp.transpose(attended, (0, 3, 1, 2, 4)).reshape(row_count, H * HD).astype(bf16)
    middle = tokens + jnp.dot(attended_low, w_out, preferred_element_type=f32)
    second, pull_two = jax.vjp(rms_scale, middle, gain_two)
    second_low = second.astype(bf16)
    gate_up = jnp.dot(second_low, w_gateup, preferred_element_type=f32)
    inner, pull_gate = jax.vjp(gated, gate_up)
    inner_low = inner.astype(bf16)
    result = middle + jnp.dot(inner_low, w_down, preferred_element_type=f32)
    layer_out = result.astype(bf16).reshape(sequences, local_len, width)
    grad_result_low = out_grad.reshape(row_count, width)
    grad_down = jnp.einsum("ti,to->io", inner_low, grad_result_low, preferred_element_type=f32)
    grad_inner = jnp.einsum("to,io->ti", grad_result_low, w_down, preferred_element_type=f32)
    (grad_gate_up,) = pull_gate(grad_inner)
    grad_gate_low = grad_gate_up.astype(bf16)
    grad_gateup = jnp.einsum("td,tf->df", second_low, grad_gate_low, preferred_element_type=f32)
    grad_second = jnp.einsum("tf,df->td", grad_gate_low, w_gateup, preferred_element_type=f32)
    grad_mid_part, grad_gain_two = pull_two(grad_second)
    grad_middle = grad_result_low.astype(f32) + grad_mid_part
    grad_branch_low = grad_middle.astype(bf16)
    grad_out = jnp.einsum("ta,td->ad", attended_low, grad_branch_low, preferred_element_type=f32)
    grad_att = jnp.einsum("td,ad->ta", grad_branch_low, w_out, preferred_element_type=f32).astype(
        bf16
    )
    grad_att_heads = jnp.transpose(
        grad_att.reshape(sequences, local_len, KV, ratio, HD), (0, 2, 3, 1, 4)
    )
    delta = jnp.sum(grad_att_heads.astype(f32) * attended, axis=-1)

    def backward_block(carry, piece, start):
        grad_query, grad_pairs = carry
        keys_piece, values_piece = piece
        count = keys_piece.shape[1]
        scores = scores_for(keys_piece, start)
        probs = jnp.exp(scores - log_total[..., None])
        grad_values = jnp.einsum(
            "skrqp,skrqd->spkd", probs.astype(bf16), grad_att_heads, preferred_element_type=f32
        )
        grad_probs = jnp.einsum(
            "skrqd,spkd->skrqp", grad_att_heads, values_piece, preferred_element_type=f32
        )
        grad_scores = (probs * (grad_probs - delta[..., None])).astype(bf16)
        grad_query = (
            grad_query
            + jnp.einsum("skrqp,spkd->skrqd", grad_scores, keys_piece, preferred_element_type=f32)
            * scale
        )
        grad_keys = (
            jnp.einsum("skrqp,sqkrd->spkd", grad_scores, query_low, preferred_element_type=f32)
            * scale
        )
        current = lax.dynamic_slice_in_dim(grad_pairs, start, count, 1)
        joined = current + jnp.concatenate([grad_keys, grad_values], axis=-1)
        return (grad_query, lax.dynamic_update_slice_in_dim(grad_pairs, joined, start, 1))

    back_state = (
        jnp.zeros((sequences, KV, ratio, local_len, HD), f32),
        jnp.zeros((sequences, seq_len, KV, 2 * HD), f32),
    )
    grad_query, grad_pairs = by_blocks(
        backward_block,
        back_state,
        (
            lax.all_gather(keys_low, "group", axis=1, tiled=True),
            lax.all_gather(values_low, "group", axis=1, tiled=True),
        ),
        local_len,
    )
    grad_local = lax.psum_scatter(
        grad_pairs.astype(jnp.bfloat16), "group", scatter_dimension=1, tiled=True
    ).astype(jnp.float32)
    grad_keys = grad_local[..., :HD].reshape(row_count, KV, HD)
    grad_values = grad_local[..., HD:].reshape(row_count, KV, HD)
    grad_query = jnp.transpose(grad_query, (0, 3, 1, 2, 4)).reshape(row_count, H, HD)
    grad_mixed, grad_gain_query, grad_gain_key = pull_heads((grad_query, grad_keys, grad_values))
    grad_mixed_low = grad_mixed.astype(bf16)
    grad_qkv = jnp.einsum("td,tc->dc", normed_low, grad_mixed_low, preferred_element_type=f32)
    grad_normed = jnp.einsum("tc,dc->td", grad_mixed_low, w_qkv, preferred_element_type=f32)
    grad_token_part, grad_gain_one = pull_one(grad_normed)
    input_grad = (grad_middle + grad_token_part).astype(bf16).reshape(sequences, local_len, width)
    grad_gains = jnp.concatenate([grad_gain_one, grad_gain_two, grad_gain_query, grad_gain_key])
    part_qkv, part_out, part_gateup, part_down, part_gain = (
        lax.psum_scatter(
            grad_qkv.astype(jnp.bfloat16), "group", scatter_dimension=0, tiled=True
        ).astype(jnp.float32),
        lax.psum_scatter(
            grad_out.astype(jnp.bfloat16), "group", scatter_dimension=0, tiled=True
        ).astype(jnp.float32),
        lax.psum_scatter(
            grad_gateup.astype(jnp.bfloat16), "group", scatter_dimension=0, tiled=True
        ).astype(jnp.float32),
        lax.psum_scatter(
            grad_down.astype(jnp.bfloat16), "group", scatter_dimension=0, tiled=True
        ).astype(jnp.float32),
        lax.psum_scatter(
            grad_gains.astype(jnp.bfloat16), "group", scatter_dimension=0, tiled=True
        ).astype(jnp.float32),
    )
    total_qkv, total_out, total_gateup, total_down, total_gain = (
        lax.psum(part_qkv.astype(jnp.bfloat16), "dp").astype(jnp.float32),
        lax.psum(part_out.astype(jnp.bfloat16), "dp").astype(jnp.float32),
        lax.psum(part_gateup.astype(jnp.bfloat16), "dp").astype(jnp.float32),
        lax.psum(part_down.astype(jnp.bfloat16), "dp").astype(jnp.float32),
        lax.psum(part_gain.astype(jnp.bfloat16), "dp").astype(jnp.float32),
    )
    out_fan = H * HD * 8 // seq_len
    qkv_new = adam_step(qkv_weight, qkv_moment, qkv_square, total_qkv, LR_MULT * D ** (-0.5), DECAY)
    out_new = adam_step(
        out_weight, out_moment, out_square, total_out, LR_MULT * out_fan ** (-0.5), DECAY
    )
    gateup_new = adam_step(
        gateup_weight, gateup_moment, gateup_square, total_gateup, LR_MULT * D ** (-0.5), DECAY
    )
    down_new = adam_step(
        down_weight, down_moment, down_square, total_down, LR_MULT * FF ** (-0.5), DECAY
    )
    gain_new = adam_step(gain_weight, gain_moment, gain_square, total_gain, GAIN_RATE, 0.0)
    return (
        layer_out,
        input_grad,
        qkv_new[0],
        qkv_new[1],
        qkv_new[2],
        out_new[0],
        out_new[1],
        out_new[2],
        gateup_new[0],
        gateup_new[1],
        gateup_new[2],
        down_new[0],
        down_new[1],
        down_new[2],
        gain_new[0],
        gain_new[1],
        gain_new[2],
    )


def solution(mesh):
    return jax.shard_map(
        shards,
        mesh=mesh,
        in_specs=(
            P("dp", "group", None),
            P("dp", "group", None),
            P(),
            P("dp", "group"),
            P("group", None),
            P("group", None),
            P("group", None),
            P("group", None),
            P("group", None),
            P("group", None),
            P("group", None),
            P("group", None),
            P("group", None),
            P("group", None),
            P("group", None),
            P("group", None),
            P("group"),
            P("group"),
            P("group"),
        ),
        out_specs=(
            P("dp", "group", None),
            P("dp", "group", None),
            P("group", None),
            P("group", None),
            P("group", None),
            P("group", None),
            P("group", None),
            P("group", None),
            P("group", None),
            P("group", None),
            P("group", None),
            P("group", None),
            P("group", None),
            P("group", None),
            P("group"),
            P("group"),
            P("group"),
        ),
        check_vma=False,
    )
```

profile of v0, /device:TPU:0, one launch (start us, length us, event | category | flops | bytes accessed | tf_op | source)
XLA Modules:
  0.0 1248.0 jit_solution(3180055452354994773)
XLA Ops:
  13.2 8.5 all-reduce.9
  27.7 44.6 %all-gather.7.cloned.1.call-done = bf16[1024,4096]{1,0:T(8,128)(2,1)} async-done(((bf16[256,4096]{1,0:T(8,128)(2,1)}), bf16[1024,4096]{1,0:T(8,128)(2,1)}) %all-gather.7.cloned.1.call-update) | async-done | bytes 8388624 | tf_op jit(solution)/shard_map/all_gather | solution.py:125
  72.3 6.9 fusion.113
  126.3 11.2 copy.188
  165.9 11.2 copy.190
  177.1 56.1 %while.32 = (s32[]{:T(128)}, f32[2,8,2,256]{3,2,1,0:T(2,128)S(1)}, f32[2,8,2,256]{3,2,1,0:T(2,128)S(1)}, f32[2,8,2,256,128]{4,3,2,1,0:T(8,128)}, s32[4]{0:T(128)...) while((s32[]{:T(128)}, f32[2,8,2,256]{3,2,1,0:T(2,128)S(1)}, ...), condition=%wide.region_8.9_spmd.clone, body=%wide.region_4.8_spmd.clone.sunk | while | flops 1100076288 | bytes 72097080 | solution.py:79
  260.4 29.3 %all-gather.15.cloned.1.call-done = bf16[1024,6144]{1,0:T(8,128)(2,1)} async-done(((bf16[256,6144]{1,0:T(8,128)(2,1)}), bf16[1024,6144]{1,0:T(8,128)(2,1)}) %all-gather.15.cloned.1.call-update) | async-done | bytes 12582928 | tf_op jit(solution)/shard_map/all_gather | solution.py:127
  289.7 14.7 %fusion.95 = f32[512,6144]{1,0:T(8,128)} fusion(bf16[1024,6144]{1,0:T(8,128)(2,1)} %all-gather.15.cloned.1.call-done, f32[512,1024]{1,0:T(8,128)} %get-tuple-element.602, f32[1024]{0:T(1024)S(1)} %get-tuple-element.593, f32[512]{0:T(512)S(1)} %fusion.90), kind=kOutput, calls=%fused_computation.211 | convolution fusion | flops 6444023808 | bytes 27269120 | tf_op jit(solution)/shard_map/dot_general | solution.py:194
  304.4 33.7 %all-gather.17.cloned.1.call-done = bf16[3072,1024]{1,0:T(8,128)(2,1)} async-done(((bf16[768,1024]{1,0:T(8,128)(2,1)}), bf16[3072,1024]{1,0:T(8,128)(2,1)}) %all-gather.17.cloned.1.call-update) | async-done | bytes 6291472 | tf_op jit(solution)/shard_map/all_gather | solution.py:128
  338.1 13.6 %fusion.79 = (f32[512,3072]{1,0:T(8,128)}, f32[512,3072]{1,0:T(8,128)}, bf16[512,3072]{1,0:T(8,128)(2,1)}) fusion(f32[512,6144]{1,0:T(8,128)} %fusion.95, bf16[512,1024]{1,0:T(8,128)(2,1)S(1)} %bitcast.244, bf16[3072,1024]{1,0:T(8,128)(2,1)} %all-gather.17.cloned.1.call-done), kind=kOutput, calls=%fused_computation.166 | convolution fusion | flops 3243245568 | bytes 35651584 | tf_op jit(solution)/shard_map/to,io->ti/dot_general | solution.py:201
  351.7 15.5 %multiply_reduce_fusion.5 = (bf16[1024]{0:T(1024)(128)(2,1)}, f32[512]{0:T(512)S(1)}, f32[512,1024]{1,0:T(8,128)}) fusion(f32[512,1024]{1,0:T(8,128)} %get-tuple-element.602, f32[512]{0:T(512)S(1)} %fusion.90, f32[1024]{0:T(1024)S(1)} %get-tuple-element.593, bf16[1024,6144]{1,0:T(8,128)(2,1)} %all-gather.15.cloned.1.call-done, ...), kind=kOutput, calls=%fused_computation.148 | convolution fusion | flops 6451886592 | bytes 29370368 | tf_op jit(solution)/shard_map/tf,df->td/dot_general | solution.py:205
  389.5 6.9 broadcast_in_dim.124.clone
  396.4 161.2 %while.33 = (s32[]{:T(128)}, f32[2,8,2,256,128]{4,3,2,1,0:T(8,128)}, f32[2,1024,8,256]{3,2,1,0:T(8,128)}, s32[4]{0:T(128)S(1)}, s32[8]{0:T(128)S(1)}, /*index=5*...) while((s32[]{:T(128)}, ...), condition=%wide.region_14.15_spmd.clone, body=%wide.region_12.14_spmd.clone.sunk | while | flops 2711172352 | bytes 133471576 | solution.py:79
  557.6 9.3 convert_element_type.180
  566.9 7.4 copy.220
  574.3 12.3 copy.254
  595.6 7.9 convolution_convert_fusion.2
  605.1 14.6 %convolution_convert_fusion = bf16[1024,6144]{1,0:T(8,128)(2,1)} fusion(f32[512,3072]{1,0:T(8,128)} %get-tuple-element.575, f32[512,3072]{1,0:T(8,128)} %get-tuple-element.574, f32[512,1024]{1,0:T(8,128)S(1)} %copy-done.15, f32[1024]{0:T(1024)S(1)} %copy-done.34, f32[512]{0:T(512)S(1)} %copy-done.40), kind=kOutput, calls=%fused_computation.81 | convolution fusion | flops 6456606720 | bytes 27269120 | tf_op jit(solution)/shard_map/td,tf->df/dot_general | solution.py:204
  649.2 9.2 reduce-scatter.17.cloned.1.call-done
  671.8 10.5 convolution_convert_fusion.1
  682.4 23.3 %reduce-scatter.11.cloned.1.call-done = bf16[512,1024]{1,0:T(8,128)(2,1)} async-done(((bf16[2048,1024]{1,0:T(8,128)(2,1)}), bf16[512,1024]{1,0:T(8,128)(2,1)}) %reduce-scatter.11.cloned.1.call-update) | async-done | bytes 1048592 | tf_op jit(solution)/shard_map/reduce_scatter | solution.py:274
  705.7 61.5 %reduce-scatter.15.cloned.1.call-done = bf16[768,1024]{1,0:T(8,128)(2,1)} async-done(((bf16[3072,1024]{1,0:T(8,128)(2,1)}), bf16[768,1024]{1,0:T(8,128)(2,1)}) %reduce-scatter.15.cloned.1.call-update) | async-done | bytes 1572880 | tf_op jit(solution)/shard_map/reduce_scatter | solution.py:280
  767.2 101.7 %reduce-scatter.13.cloned.1.call-done = bf16[256,6144]{1,0:T(8,128)(2,1)} async-done(((bf16[1024,6144]{1,0:T(8,128)(2,1)}), bf16[256,6144]{1,0:T(8,128)(2,1)}) %reduce-scatter.13.cloned.1.call-update) | async-done | bytes 3145744 | tf_op jit(solution)/shard_map/reduce_scatter | solution.py:277
  868.9 74.5 %reduce-scatter.9.cloned.1.call-done = bf16[256,4096]{1,0:T(8,128)(2,1)} async-done(((bf16[1024,4096]{1,0:T(8,128)(2,1)}), bf16[256,4096]{1,0:T(8,128)(2,1)}) %reduce-scatter.9.cloned.1.call-update) | async-done | bytes 2097168 | tf_op jit(solution)/shard_map/reduce_scatter | solution.py:271
  944.1 8.2 add_convert_fusion.2
  952.4 12.8 %fusion.74 = (bf16[1024]{0:T(1024)(128)(2,1)S(1)}, f32[512]{0:T(512)S(1)}, f32[512,1024]{1,0:T(8,128)}) fusion(bf16[2,256,1024]{2,1,0:T(8,128)(2,1)S(1)} %copy-done.13, f32[512]{0:T(512)S(1)} %copy-done.47, f32[1024]{0:T(1024)S(1)} %copy-done.45, bf16[1024,4096]{1,0:T(8,128)(2,1)} %all-gather.7.cloned.1.call-done, f32[512,2048]{1,0:T(8,128)} %copy.207, ...), kind=kOutput, calls=%fused_computation.144 | convolution fusion | flops 4304927232 | bytes 19933184 | tf_op jit(solution)/shard_map/tc,dc->td/dot_general | solution.py:266
  971.6 23.2 %psum.39 = bf16[576]{0:T(1024)(128)(2,1)S(1)} all-reduce(bf16[576]{0:T(1024)(128)(2,1)S(1)} %dynamic-slice.2), channel_id=1, replica_groups=mesh['dp'=8,'group'=4] {'dp'}, use_global_device_ids=true, to_apply=%region_32.33 | all-reduce | flops 576 | bytes 2304 | tf_op jit(solution)/shard_map/psum | solution.py:292
  999.3 206.1 %all-reduce.14.cloned.1.call-done = (bf16[256,4096]{1,0:T(8,128)(2,1)}, bf16[512,1024]{1,0:T(8,128)(2,1)}, bf16[256,6144]{1,0:T(8,128)(2,1)}, bf16[768,1024]{1,0:T(8,128)(2,1)}) async-done(((bf16[256,4096]{1,0:T(8,128)(2,1)}, bf16[512,1024]{1,0:T(8,128)(2,1)}, bf16[256,6144]{1,0:T(8,128)(2,1)}, bf16[768,1024]{1,0:T(8,128)(2,1)}), (bf16[256,4096]{1,0:T(8,128)(2,1)}, bf16[512,1024]{1,0:T(8,128)(2,1)}, ...) | async-done | bytes 7864336 | tf_op jit(solution)/shard_map/psum | solution.py:288
  1205.3 6.7 multiply_subtract_fusion.3
  1212.1 6.9 multiply_subtract_fusion.2
  1219.0 9.7 multiply_subtract_fusion.1
  1230.5 10.3 multiply_subtract_fusion
  (393 shorter events, 413.2 us)
Async XLA Ops:
  7.2 14.5 %copy-start.61 = (s32[2,256]{1,0:T(2,128)S(1)}, s32[2,256]{1,0:T(2,128)}, u32[]{:S(2)}) copy-start(s32[2,256]{1,0:T(2,128)} %param.26) | copy-start | bytes 6148
  7.2 65.1 %all-gather.7.cloned.1.call-start = ((), (), s32[]{:S(2)}) async-start(), calls=%async_computation.5 | async-start | bytes 10485760 | tf_op jit(solution)/shard_map/all_gather | solution.py:125
  11.2 154.7 %all-gather.9.cloned.1.call-start = ((), (), s32[]{:S(2)}) async-start(), calls=%async_computation.6 | async-start | bytes 5242880 | tf_op jit(solution)/shard_map/all_gather | solution.py:183
  11.6 67.6 %copy-start.46 = (f32[512]{0:T(512)}, f32[512]{0:T(512)S(1)}, u32[]{:S(2)}) copy-start(f32[512]{0:T(512)S(1)} %rsqrt.48) | copy-start | bytes 6148
  27.4 64.1 %copy-start.52 = (f32[128]{0:T(128)}, f32[128]{0:T(128)S(1)}, u32[]{:S(2)}) copy-start(f32[128]{0:T(128)S(1)} %get-tuple-element.596) | copy-start | bytes 1540
  27.4 125.1 %copy-start.54 = (f32[128]{0:T(128)}, f32[128]{0:T(128)S(1)}, u32[]{:S(2)}) copy-start(f32[128]{0:T(128)S(1)} %get-tuple-element.595) | copy-start | bytes 1540
  27.4 51.9 %copy-start.44 = (f32[1024]{0:T(1024)}, f32[1024]{0:T(1024)S(1)}, u32[]{:S(2)}) copy-start(f32[1024]{0:T(1024)S(1)} %get-tuple-element.594) | copy-start | bytes 12292
  27.4 339.9 %copy-start.33 = (f32[1024]{0:T(1024)}, f32[1024]{0:T(1024)S(1)}, u32[]{:S(2)}) copy-start(f32[1024]{0:T(1024)S(1)} %get-tuple-element.593) | copy-start | bytes 12292
  27.7 51.5 %copy-start.27 = (bf16[512,1024]{1,0:T(8,128)(2,1)}, bf16[512,1024]{1,0:T(8,128)(2,1)S(1)}, u32[]{:S(2)}) copy-start(bf16[512,1024]{1,0:T(8,128)(2,1)S(1)} %fusion.73) | copy-start | bytes 3145732
  97.2 79.8 %all-gather.11.cloned.1.call-start = ((), (), s32[]{:S(2)}) async-start(), calls=%async_computation.7 | async-start | bytes 5242880 | tf_op jit(solution)/shard_map/all_gather | solution.py:184
  100.7 153.1 %all-gather.13.cloned.1.call-start = ((), (), s32[]{:S(2)}) async-start(), calls=%async_computation.8 | async-start | bytes 5242880 | tf_op jit(solution)/shard_map/all_gather | solution.py:126
  101.9 187.8 %all-gather.15.cloned.1.call-start = ((), (), s32[]{:S(2)}) async-start(), calls=%async_computation.9 | async-start | bytes 15728640 | tf_op jit(solution)/shard_map/all_gather | solution.py:127
  107.6 230.5 %all-gather.17.cloned.1.call-start = ((), (), s32[]{:S(2)}) async-start(), calls=%async_computation.10 | async-start | bytes 7864320 | tf_op jit(solution)/shard_map/all_gather | solution.py:128
  109.1 549.4 %reduce-scatter.17.cloned.1.call-start = ((), (), s32[]{:S(2)}) async-start(), calls=%async_computation.15 | async-start | bytes 10485760
  243.0 10.7 copy-start.12
  260.4 106.9 %copy-start.39 = (f32[512]{0:T(512)}, f32[512]{0:T(512)S(1)}, u32[]{:S(2)}) copy-start(f32[512]{0:T(512)S(1)} %fusion.90) | copy-start | bytes 6148
  289.7 48.4 %copy-start.29 = (bf16[2,256,1024]{2,1,0:T(8,128)(2,1)S(1)}, bf16[2,256,1024]{2,1,0:T(8,128)(2,1)}, u32[]{:S(2)}) copy-start(bf16[2,256,1024]{2,1,0:T(8,128)(2,1)} %param.24) | copy-start | bytes 3145732
  586.6 119.1 %reduce-scatter.11.cloned.1.call-start = ((), (), s32[]{:S(2)}) async-start(), calls=%async_computation.12 | async-start | bytes 5242880 | tf_op jit(solution)/shard_map/reduce_scatter | solution.py:274
  594.1 173.1 %reduce-scatter.15.cloned.1.call-start = ((), (), s32[]{:S(2)}) async-start(), calls=%async_computation.14 | async-start | bytes 7864320 | tf_op jit(solution)/shard_map/reduce_scatter | solution.py:280
  603.6 265.3 %reduce-scatter.13.cloned.1.call-start = ((), (), s32[]{:S(2)}) async-start(), calls=%async_computation.13 | async-start | bytes 15728640 | tf_op jit(solution)/shard_map/reduce_scatter | solution.py:277
  619.8 323.6 %reduce-scatter.9.cloned.1.call-start = ((), (), s32[]{:S(2)}) async-start(), calls=%async_computation.11 | async-start | bytes 10485760 | tf_op jit(solution)/shard_map/reduce_scatter | solution.py:271
  682.3 261.8 %copy-start.16 = (f32[512,1024]{1,0:T(8,128)S(1)}, f32[512,1024]{1,0:T(8,128)}, u32[]{:S(2)}) copy-start(f32[512,1024]{1,0:T(8,128)} %get-tuple-element.602) | copy-start | bytes 6291460
  682.3 523.0 %all-reduce.14.cloned.1.call-start = ((), (), s32[]{:S(2)}) async-start(), calls=%async_computation.16 | async-start | bytes 15728640 | tf_op jit(solution)/shard_map/psum | solution.py:288
  952.3 12.9 %copy-start.63 = (bf16[1024]{0:T(1024)(128)(2,1)S(1)}, bf16[1024]{0:T(1024)(128)(2,1)}, u32[]{:S(2)}) copy-start(bf16[1024]{0:T(1024)(128)(2,1)} %get-tuple-element.497) | copy-start | bytes 6148
  952.3 42.4 %copy-start.49 = (f32[1,2,2,128]{3,1,2,0:T(2,128)S(1)}, f32[1,2,2,128]{3,1,2,0:T(2,128)}, u32[]{:S(2)}) copy-start(f32[1,2,2,128]{3,1,2,0:T(2,128)} %copy-done.48) | copy-start | bytes 6148
  952.3 42.4 %copy-start.51 = (f32[576]{0:T(1024)S(1)}, f32[576]{0:T(1024)}, u32[]{:S(2)}) copy-start(f32[576]{0:T(1024)} %param.39) | copy-start | bytes 6916
  952.3 42.4 %copy-start.57 = (f32[576]{0:T(1024)S(1)}, f32[576]{0:T(1024)}, u32[]{:S(2)}) copy-start(f32[576]{0:T(1024)} %param.40) | copy-start | bytes 6916
  952.4 42.4 %copy-start.58 = (f32[576]{0:T(1024)S(1)}, f32[576]{0:T(1024)}, u32[]{:S(2)}) copy-start(f32[576]{0:T(1024)} %param.41) | copy-start | bytes 6916
  965.2 240.1 %copy-start.18 = (f32[512,1024]{1,0:T(8,128)S(1)}, f32[512,1024]{1,0:T(8,128)}, u32[]{:S(2)}) copy-start(f32[512,1024]{1,0:T(8,128)} %param.30) | copy-start | bytes 6291460
  1212.0 16.7 %slice-start = ((s8[6291456]{0:T(1024)(128)(4,1)}), s8[4194304]{0:T(1024)(128)(4,1)S(1)}, s32[]{:S(2)}) async-start(s8[6291456]{0:T(1024)(128)(4,1)} %bitcast.226), calls=%async_computation.17 | async-start | bytes 8388608
  1212.0 16.7 %slice-start.2 = ((s8[6291456]{0:T(1024)(128)(4,1)}), s8[4194304]{0:T(1024)(128)(4,1)S(1)}, s32[]{:S(2)}) async-start(s8[6291456]{0:T(1024)(128)(4,1)} %bitcast.236), calls=%async_computation.19 | async-start | bytes 8388608
  1219.0 11.4 copy-start.24
  (61 other events, 202.3 us)
Sparse Core Ops, SparseCore 0:
  11.3 60.9 all-gather.6
  97.3 35.0 all-gather.8
  134.5 34.4 all-gather.10
  171.1 34.4 all-gather.12
  207.5 82.0 all-gather.14
  291.7 46.3 all-gather.16
  586.7 71.7 reduce-scatter.16
  661.1 44.5 reduce-scatter.10
  708.8 58.3 reduce-scatter.14
  769.8 99.0 reduce-scatter.12
  871.7 71.6 reduce-scatter.8
  947.7 257.5 all-reduce.13
where the time goes:
time: 1260 us; the launch traced here: 1250 us
  waiting for transfers between devices  584 us (46%)
  local copies, waits for them, and re-layouts  253 us (20%)
  matrix products  218 us (17%)
  other arithmetic  132 us (10%)
  blocking collectives  38 us (3%)
  between operations  17 us (1%)
    psum x1, waiting for transfers between devices, shards(): lax.psum(part_qkv.astype(jnp.bfloat16), 'dp').astype(jnp.float32)  206 us
    reduce_scatter x1, waiting for transfers between devices, shards(): lax.psum_scatter(grad_gateup.astype(jnp.bfloat16), 'group', scatter_dimen...  102 us
    reduce_scatter x1, waiting for transfers between devices, shards(): lax.psum_scatter(grad_qkv.astype(jnp.bfloat16), 'group', scatter_dimensio...  74.5 us
    unnamed x147, local copies, waits for them, and re-layouts  62.1 us
    reduce_scatter x1, waiting for transfers between devices, shards(): lax.psum_scatter(grad_down.astype(jnp.bfloat16), 'group', scatter_dimensi...  61.5 us
    all_gather x1, waiting for transfers between devices, shards(): lax.all_gather(qkv_weight.astype(bf16), 'group', axis=0, tiled=True)  44.6 us
    dynamic_update_slice x8, local copies, waits for them, and re-layouts, backward_block(): lax.dynamic_update_slice_in_dim(grad_pairs, joined, start, 1)  39.5 us
    dynamic_slice x8, local copies, waits for them, and re-layouts, backward_block(): current = lax.dynamic_slice_in_dim(grad_pairs, start, count, 1)  38.8 us
  transfers between devices with their start and end apart: 12, of which 9 were waited for; matrix products, arithmetic and copies ran while one was open for 22% of the time, Pallas kernels for 0%

commit v1 on v0

--- a/solution.py
+++ b/solution.py
@@ -1,6 +1,8 @@
 import jax
 import jax.numpy as jnp
 from jax import lax
+from jax.experimental import pallas as pl
+from jax.experimental.pallas import tpu as pltpu
 from jax.sharding import PartitionSpec as P
 
 D = 1024
@@ -91,7 +93,7 @@
     return (weight - rate * (ratio + decay * weight), moment_new, square_new)
 
 
-def shards(
+def general_shards(
     hidden_in,
     out_grad,
     stretch_order,
@@ -324,6 +326,648 @@
     )
 
 
+ALL = ("dp", "group")
+LOG2E = 1.4426950408889634
+
+
+def tie(value, *others):
+    return lax.optimization_barrier((value, *others))[0]
+
+
+def split_product(left, right, left_dim, right_dim):
+    return lax.dot_general(
+        left, right, (((left_dim,), (right_dim,)), ((), ())), preferred_element_type=jnp.float32
+    )
+
+
+def place_rows(pieces, targets, chunk):
+    count = targets.shape[0]
+    per_piece = count // len(pieces)
+    width = pieces[0].shape[1]
+
+    def kernel(targets_ref, *refs):
+        sources = refs[: len(pieces)]
+        placed, sems = refs[len(pieces) :]
+        copies = []
+        for number in range(count):
+            row = pl.multiple_of(targets_ref[number] * chunk, chunk)
+            copies.append(
+                pltpu.make_async_copy(
+                    sources[number // per_piece].at[pl.ds((number % per_piece) * chunk, chunk)],
+                    placed.at[pl.ds(row, chunk)],
+                    sems.at[number],
+                )
+            )
+        for copy in copies:
+            copy.start()
+        for copy in copies:
+            copy.wait()
+
+    return pl.pallas_call(
+        kernel,
+        out_shape=jax.ShapeDtypeStruct((count * chunk, width), pieces[0].dtype),
+        grid_spec=pltpu.PrefetchScalarGridSpec(
+            num_scalar_prefetch=1,
+            grid=(1,),
+            in_specs=[pl.BlockSpec(memory_space=pl.ANY)] * len(pieces),
+            out_specs=pl.BlockSpec(memory_space=pl.ANY),
+            scratch_shapes=[pltpu.SemaphoreType.DMA((count,))],
+        ),
+        cost_estimate=pl.CostEstimate(
+            flops=0, bytes_accessed=4 * count * chunk * width, transcendentals=0
+        ),
+        name="place_rows",
+    )(targets, *pieces)
+
+
+def take_rows(rows, sources, chunk):
+    return jnp.concatenate(
+        [
+            lax.dynamic_slice_in_dim(rows, sources[number] * chunk, chunk, 0)
+            for number in range(sources.shape[0])
+        ],
+        axis=0,
+    )
+
+
+def normal_rope(raw, gain, cosine, sine):
+    inverse = lax.rsqrt(jnp.mean(raw * raw, axis=-1, keepdims=True) + EPSILON)
+    scaled = raw * inverse * gain
+    return scaled * cosine + pltpu.roll(scaled, HD // 2, 1) * sine, inverse
+
+
+def normal_rope_back(grad, raw, inverse, gain, cosine, sine):
+    grad_scaled = grad * cosine + pltpu.roll(grad * sine, HD // 2, 1)
+    unit = raw * inverse
+    grad_gain = jnp.sum(grad_scaled * unit, axis=0, keepdims=True)
+    weighted = grad_scaled * gain
+    shift = jnp.mean(weighted * unit, axis=-1, keepdims=True)
+    return inverse * (weighted - unit * shift), grad_gain
+
+
+def causal_mask(block, ratio):
+    row = lax.broadcasted_iota(jnp.int32, (ratio * block, block), 0) % block
+    column = lax.broadcasted_iota(jnp.int32, (ratio * block, block), 1)
+    return column <= row
+
+
+def attend_forward(mixed, cosine, sine, gain_query, gain_key, heads, ratio, block):
+    rows = mixed.shape[0]
+    wide = (ratio + 2) * HD
+    factor = HD ** (-0.5) * LOG2E
+    bf16 = jnp.bfloat16
+    f32 = jnp.float32
+
+    def kernel(mixed_ref, cos_ref, sin_ref, gq_ref, gk_ref, att_ref, total_ref):
+        cos = cos_ref[...]
+        sin = sin_ref[...]
+        query = [
+            normal_rope(mixed_ref[:, r * HD : (r + 1) * HD], gq_ref[...], cos, sin)[0].astype(bf16)
+            for r in range(ratio)
+        ]
+        keys = normal_rope(mixed_ref[:, ratio * HD : (ratio + 1) * HD], gk_ref[...], cos, sin)[0]
+        keys = keys.astype(bf16)
+        values = mixed_ref[:, (ratio + 1) * HD :].astype(bf16)
+        values = jnp.concatenate([values, jnp.ones((rows, HD), bf16)], axis=1)
+        allowed = causal_mask(block, ratio)
+        lane = lax.broadcasted_iota(jnp.int32, (block, HD), 1)
+        for number in range(rows // block):
+            low, high = number * block, (number + 1) * block
+            stacked = jnp.concatenate([part[low:high] for part in query], axis=0)
+            scores = split_product(stacked, keys[low:high], 1, 1)
+            terms = jnp.where(allowed, jnp.exp2(scores * factor), 0.0).astype(bf16)
+            joined = split_product(terms, values[low:high], 1, 0)
+            if low:
+                scores = split_product(stacked, keys[:low], 1, 1)
+                terms = jnp.exp2(scores * factor).astype(bf16)
+                joined = joined + split_product(terms, values[:low], 1, 0)
+            total = joined[:, HD:]
+            result = (joined[:, :HD] / total).astype(bf16)
+            kept = total[:block]
+            for r in range(ratio):
+                att_ref[low:high, r * HD : (r + 1) * HD] = result[r * block : (r + 1) * block]
+                if r:
+                    kept = jnp.where(
+                        lane >= r * (HD // ratio), total[r * block : (r + 1) * block], kept
+                    )
+            total_ref[low:high, :] = kept
+
+    work = heads * ratio * rows * rows * HD * 4 * 5 // 8
+    return pl.pallas_call(
+        kernel,
+        grid=(heads,),
+        in_specs=[
+            pl.BlockSpec((rows, wide), lambda i: (0, i)),
+            pl.BlockSpec((rows, HD), lambda i: (0, 0)),
+            pl.BlockSpec((rows, HD), lambda i: (0, 0)),
+            pl.BlockSpec((1, HD), lambda i: (0, 0)),
+            pl.BlockSpec((1, HD), lambda i: (0, 0)),
+        ],
+        out_specs=[
+            pl.BlockSpec((rows, ratio * HD), lambda i: (0, i)),
+            pl.BlockSpec((rows, HD), lambda i: (0, i)),
+        ],
+        out_shape=[
+            jax.ShapeDtypeStruct((rows, heads * ratio * HD), bf16),
+            jax.ShapeDtypeStruct((rows, heads * HD), f32),
+        ],
+        compiler_params=pltpu.CompilerParams(vmem_limit_bytes=48 * 1024 * 1024),
+        cost_estimate=pl.CostEstimate(
+            flops=work,
+            bytes_accessed=heads * rows * (wide * 4 + ratio * HD * 2 + HD * 4),
+            transcendentals=heads * ratio * rows * rows * 5 // 8,
+        ),
+        name="attend_forward",
+    )(mixed, cosine, sine, gain_query, gain_key)
+
+
+def attend_backward(
+    mixed, cosine, sine, gain_query, gain_key, attended, totals, grad_att, heads, ratio, block
+):
+    rows = mixed.shape[0]
+    wide = (ratio + 2) * HD
+    scale = HD ** (-0.5)
+    factor = scale * LOG2E
+    bf16 = jnp.bfloat16
+    f32 = jnp.float32
+
+    def kernel(
+        mixed_ref, cos_ref, sin_ref, gq_ref, gk_ref, att_ref, total_ref, grad_ref,
+        out_ref, dgq_ref, dgk_ref, key_sum, value_sum,
+    ):
+        cos = cos_ref[...]
+        sin = sin_ref[...]
+        gain_q = gq_ref[...]
+        query = []
+        query_inverse = []
+        for r in range(ratio):
+            turned, inverse = normal_rope(mixed_ref[:, r * HD : (r + 1) * HD], gain_q, cos, sin)
+            query.append(turned.astype(bf16))
+            query_inverse.append(inverse)
+        raw_keys = mixed_ref[:, ratio * HD : (ratio + 1) * HD]
+        keys, key_inverse = normal_rope(raw_keys, gk_ref[...], cos, sin)
+        keys = keys.astype(bf16)
+        values = mixed_ref[:, (ratio + 1) * HD :].astype(bf16)
+        allowed = causal_mask(block, ratio)
+        grad_gain = jnp.zeros((1, HD), f32)
+
+        @pl.when(pl.program_id(0) == 0)
+        def _():
+            dgq_ref[...] = jnp.zeros_like(dgq_ref)
+            dgk_ref[...] = jnp.zeros_like(dgk_ref)
+
+        for number in reversed(range(rows // block)):
+            low, high = number * block, (number + 1) * block
+            stacked = jnp.concatenate([part[low:high] for part in query], axis=0)
+            grads = []
+            deltas = []
+            for r in range(ratio):
+                lane = r * (HD // ratio)
+                inverse = 1.0 / total_ref[low:high, lane : lane + 1]
+                columns = slice(r * HD, (r + 1) * HD)
+                part = (grad_ref[low:high, columns].astype(f32) * inverse).astype(bf16)
+                grads.append(part)
+                deltas.append(
+                    jnp.sum(
+                        part.astype(f32) * att_ref[low:high, columns].astype(f32),
+                        axis=-1,
+                        keepdims=True,
+                    )
+                )
+            grad = jnp.concatenate(grads, axis=0)
+            delta = jnp.concatenate(deltas, axis=0)
+            grad_query = None
+            for start, end, masked in ((low, high, True), (0, low, False)):
+                if end == start:
+                    continue
+                scores = split_product(stacked, keys[start:end], 1, 1)
+                terms = jnp.exp2(scores * factor)
+                if masked:
+                    terms = jnp.where(allowed, terms, 0.0)
+                grad_terms = split_product(grad, values[start:end], 1, 1)
+                grad_scores = (terms * (grad_terms - delta)).astype(bf16)
+                grad_values = split_product(terms.astype(bf16), grad, 0, 0)
+                grad_keys = split_product(grad_scores, stacked, 0, 0)
+                part = split_product(grad_scores, keys[start:end], 1, 0)
+                grad_query = part if grad_query is None else grad_query + part
+                if number == rows // block - 1:
+                    value_sum[start:end, :] = grad_values
+                    key_sum[start:end, :] = grad_keys
+                else:
+                    value_sum[start:end, :] += grad_values
+                    key_sum[start:end, :] += grad_keys
+            for r in range(ratio):
+                columns = slice(r * HD, (r + 1) * HD)
+                back, gain_part = normal_rope_back(
+                    grad_query[r * block : (r + 1) * block] * scale,
+                    mixed_ref[low:high, columns],
+                    query_inverse[r][low:high],
+                    gain_q,
+                    cos[low:high],
+                    sin[low:high],
+                )
+                out_ref[low:high, columns] = back.astype(bf16)
+                grad_gain = grad_gain + gain_part
+        dgq_ref[...] += grad_gain
+        back, gain_part = normal_rope_back(
+            key_sum[...] * scale, raw_keys, key_inverse, gk_ref[...], cos, sin
+        )
+        dgk_ref[...] += gain_part
+        out_ref[:, ratio * HD : (ratio + 1) * HD] = back.astype(bf16)
+        out_ref[:, (ratio + 1) * HD :] = value_sum[...].astype(bf16)
+
+    work = heads * ratio * rows * rows * HD * 10 * 5 // 8
+    return pl.pallas_call(
+        kernel,
+        grid=(heads,),
+        in_specs=[
+            pl.BlockSpec((rows, wide), lambda i: (0, i)),
+            pl.BlockSpec((rows, HD), lambda i: (0, 0)),
+            pl.BlockSpec((rows, HD), lambda i: (0, 0)),
+            pl.BlockSpec((1, HD), lambda i: (0, 0)),
+            pl.BlockSpec((1, HD), lambda i: (0, 0)),
+            pl.BlockSpec((rows, ratio * HD), lambda i: (0, i)),
+            pl.BlockSpec((rows, HD), lambda i: (0, i)),
+            pl.BlockSpec((rows, ratio * HD), lambda i: (0, i)),
+        ],
+        out_specs=[
+            pl.BlockSpec((rows, wide), lambda i: (0, i)),
+            pl.BlockSpec((1, HD), lambda i: (0, 0)),
+            pl.BlockSpec((1, HD), lambda i: (0, 0)),
+        ],
+        out_shape=[
+            jax.ShapeDtypeStruct((rows, heads * wide), bf16),
+            jax.ShapeDtypeStruct((1, HD), f32),
+            jax.ShapeDtypeStruct((1, HD), f32),
+        ],
+        scratch_shapes=[pltpu.VMEM((rows, HD), f32), pltpu.VMEM((rows, HD), f32)],
+        compiler_params=pltpu.CompilerParams(vmem_limit_bytes=48 * 1024 * 1024),
+        cost_estimate=pl.CostEstimate(
+            flops=work,
+            bytes_accessed=heads * rows * (wide * 6 + ratio * HD * 4 + HD * 4),
+            transcendentals=heads * ratio * rows * rows * 5 // 8,
+        ),
+        name="attend_backward",
+    )(mixed, cosine, sine, gain_query, gain_key, attended, totals, grad_att)
+
+
+def paired_shards(
+    hidden_in,
+    out_grad,
+    stretch_order,
+    positions,
+    qkv_weight,
+    qkv_moment,
+    qkv_square,
+    out_weight,
+    out_moment,
+    out_square,
+    gateup_weight,
+    gateup_moment,
+    gateup_square,
+    down_weight,
+    down_moment,
+    down_square,
+    gain_weight,
+    gain_moment,
+    gain_square,
+):
+    groups = lax.axis_size("group")
+    copies = lax.axis_size("dp")
+    sequences, local_len, width = hidden_in.shape
+    seq_len = local_len * groups
+    pieces = stretch_order.shape[0]
+    chunk = seq_len // pieces
+    held = pieces // groups
+    ratio = H // KV
+    heads = 2 * KV // groups
+    ff = FF // groups
+    bf16 = jnp.bfloat16
+    f32 = jnp.float32
+    member = lax.axis_index("group")
+    copy = lax.axis_index("dp")
+    half = member // 2
+    rank = member % 2
+    side = copy % 2
+
+    def permute(value, target):
+        pairs = []
+        for d in range(copies):
+            for g in range(groups):
+                to_d, to_g = target(d, g)
+                pairs.append((d * groups + g, to_d * groups + to_g))
+        return lax.ppermute(value, ALL, pairs)
+
+    def over_core(value):
+        return permute(value, lambda d, g: (d, g ^ 1))
+
+    def over_chip(value):
+        return permute(value, lambda d, g: (d, g ^ 2))
+
+    def over_side(value):
+        return permute(value, lambda d, g: (d ^ 1, g))
+
+    def block_of(far, other_rank):
+        at = half if not far else 1 - half
+        return at * 2 + (rank if not other_rank else 1 - rank)
+
+    def pick(array, index):
+        return lax.dynamic_index_in_dim(array, index, 0, keepdims=False)
+
+    gains = lax.all_gather(gain_weight.astype(bf16), "group", axis=0, tiled=True).astype(f32)
+    gain_one = gains[:D]
+    gain_two = gains[D : 2 * D]
+    gain_query = gains[2 * D : 2 * D + HD].reshape(1, HD)
+    gain_key = gains[2 * D + HD :].reshape(1, HD)
+
+    first_piece = pick(stretch_order, member * held)
+    start = pick(positions, half)[0] - first_piece * chunk
+    exponent = jnp.arange(HD // 2, dtype=f32) * (2.0 / HD)
+    inverse = jnp.power(jnp.float32(ROPE_BASE), -exponent)
+    places = (start + jnp.arange(seq_len, dtype=jnp.int32)).astype(f32)
+    angle = places[:, None] * inverse[None, :]
+    cosine_half, sine_half = jnp.cos(angle), jnp.sin(angle)
+    cosine = jnp.concatenate([cosine_half, cosine_half], axis=-1)
+    sine = jnp.concatenate([-sine_half, sine_half], axis=-1)
+
+    def piece_targets(other_rank):
+        return [
+            stretch_order[block_of(far, other_rank) * held + number]
+            for far in (False, True)
+            for number in range(held)
+        ]
+
+    own_targets = jnp.stack(piece_targets(False))
+    peer_targets = jnp.stack(piece_targets(True))
+    all_targets = jnp.concatenate([own_targets, peer_targets])
+
+    def whole_sequence(array, far_part):
+        near_part = pick(array, half)
+        mine = jnp.concatenate([near_part, far_part], axis=0)
+        theirs = over_core(mine)
+        return place_rows([mine, theirs], all_targets, chunk)
+
+    def by_heads(array):
+        lead = array.shape[0]
+        query = array[:, : H * HD].reshape(lead, KV, ratio * HD)
+        keys = array[:, H * HD : (H + KV) * HD].reshape(lead, KV, HD)
+        values = array[:, (H + KV) * HD :].reshape(lead, KV, HD)
+        return jnp.concatenate([query, keys, values], axis=2).reshape(lead, groups, -1)
+
+    def by_units(array):
+        lead = array.shape[0]
+        gate = array[:, :FF].reshape(lead, groups, ff)
+        up = array[:, FF:].reshape(lead, groups, ff)
+        return jnp.concatenate([gate, up], axis=2)
+
+    def column_blocks(blocked, other_rank):
+        parts = []
+        for far in (False, True):
+            parts.append(
+                lax.dynamic_index_in_dim(blocked, block_of(far, other_rank), 1, keepdims=False)
+            )
+        return jnp.concatenate(parts, axis=1)
+
+    def chip_columns(blocked):
+        mine = column_blocks(blocked, False)
+        theirs = over_core(column_blocks(blocked, True))
+        lead, cols = mine.shape
+        chip = jnp.zeros((2 * lead, cols), bf16)
+        chip = lax.dynamic_update_slice(chip, mine, (rank * lead, 0))
+        return lax.dynamic_update_slice(chip, theirs, ((1 - rank) * lead, 0))
+
+    def columns_payload(chip):
+        lead, cols = chip.shape
+        return lax.dynamic_slice(chip, (0, (1 - side) * (cols // 2)), (lead, cols // 2))
+
+    def columns_join(chip, from_chip, from_side):
+        lead, cols = chip.shape
+        whole = jnp.zeros((2 * lead, cols), bf16)
+        whole = lax.dynamic_update_slice(whole, chip, (half * lead, 0))
+        whole = lax.dynamic_update_slice(
+            whole, from_chip, ((1 - half) * lead, side * (cols // 2))
+        )
+        return lax.dynamic_update_slice(
+            whole, from_side, ((1 - half) * lead, (1 - side) * (cols // 2))
+        )
+
+    def rows_payload(own):
+        return lax.dynamic_slice_in_dim(own, side * (own.shape[0] // 2), own.shape[0] // 2, 0)
+
+    def rows_join(own, from_chip, from_side):
+        lead, cols = own.shape
+        whole = jnp.zeros((2 * lead, cols), bf16)
+        whole = lax.dynamic_update_slice(whole, own, (0, 0))
+        whole = lax.dynamic_update_slice(whole, from_chip, (lead + side * (lead // 2), 0))
+        return lax.dynamic_update_slice(whole, from_side, (lead + (1 - side) * (lead // 2), 0))
+
+    hidden_far = over_chip(pick(hidden_in, 1 - half))
+    qkv_chip = chip_columns(by_heads(qkv_weight.astype(bf16)))
+    qkv_y = over_chip(columns_payload(qkv_chip))
+    qkv_x = over_side(qkv_y)
+    out_own = out_weight.astype(bf16)
+    out_y = over_chip(tie(rows_payload(out_own), hidden_far))
+    out_x = over_side(out_y)
+    gateup_chip = chip_columns(by_units(gateup_weight.astype(bf16)))
+    gateup_y = over_chip(tie(columns_payload(gateup_chip), qkv_y))
+    gateup_x = over_side(gateup_y)
+    down_own = down_weight.astype(bf16)
+    down_y = over_chip(tie(rows_payload(down_own), out_y))
+    down_x = over_side(down_y)
+    grad_far = over_chip(tie(pick(out_grad, 1 - half), gateup_y))
+
+    hidden = whole_sequence(hidden_in, hidden_far)
+    tokens = hidden.astype(f32)
+    normed_low = rms_scale(tokens, gain_one).astype(bf16)
+    w_qkv = columns_join(qkv_chip, qkv_y, qkv_x)
+    mixed = split_product(normed_low, w_qkv, 1, 0)
+    block = min(256, seq_len)
+    attended, totals = attend_forward(
+        mixed, cosine, sine, gain_query, gain_key, heads, ratio, block
+    )
+    w_out = rows_join(out_own, out_y, out_x)
+    branch = split_product(attended, w_out, 1, 0).astype(bf16)
+    middle = tokens + (branch.astype(f32) + over_core(branch).astype(f32))
+    second, pull_two = jax.vjp(rms_scale, middle, gain_two)
+    second_low = second.astype(bf16)
+    w_gateup = columns_join(gateup_chip, gateup_y, gateup_x)
+    gate_up = split_product(second_low, w_gateup, 1, 0)
+
+    def gated_pairs(values):
+        return jnp.concatenate(
+            [
+                jax.nn.silu(values[:, far * 2 * ff : far * 2 * ff + ff])
+                * values[:, far * 2 * ff + ff : (far + 1) * 2 * ff]
+                for far in range(2)
+            ],
+            axis=1,
+        )
+
+    inner, pull_gate = jax.vjp(gated_pairs, gate_up)
+    inner_low = inner.astype(bf16)
+    grad_result = whole_sequence(out_grad, grad_far)
+
+    def near_far(grad_fn, swapped=False):
+        far = grad_fn(True)
+        from_far = over_chip(far)
+        near = grad_fn(False)
+        if swapped:
+            size = from_far.shape[1] // 2
+            from_far = jnp.concatenate([from_far[:, size:], from_far[:, :size]], axis=1)
+        return (near.astype(f32) + from_far.astype(f32)).astype(bf16)
+
+    def unit_rows(array, far):
+        size = array.shape[1] // 2
+        return array[:, size:] if far else array[:, :size]
+
+    def chip_rows(array, far):
+        size = array.shape[1] // 2
+        at = (1 - half) if far else half
+        return lax.dynamic_slice_in_dim(array, at * size, size, 1)
+
+    sum_down = near_far(
+        lambda far: split_product(unit_rows(inner_low, far), grad_result, 0, 0).astype(bf16)
+    )
+    w_down = rows_join(down_own, down_y, down_x)
+    result_part = split_product(inner_low, w_down, 1, 0).astype(bf16)
+    grad_inner = split_product(grad_result, w_down, 1, 1)
+    (grad_gate_up,) = pull_gate(grad_inner)
+    grad_gate_low = grad_gate_up.astype(bf16)
+    sum_gateup = near_far(
+        lambda far: split_product(chip_rows(second_low, far), grad_gate_low, 0, 0).astype(bf16),
+        True,
+    )
+    second_part = split_product(grad_gate_low, w_gateup, 1, 1).astype(bf16)
+    grad_second = second_part.astype(f32) + over_core(second_part).astype(f32)
+    grad_mid_part, grad_gain_two = pull_two(grad_second)
+    grad_middle = grad_result.astype(f32) + grad_mid_part
+    grad_branch_low = grad_middle.astype(bf16)
+    sum_out = near_far(
+        lambda far: split_product(unit_rows(attended, far), grad_branch_low, 0, 0).astype(bf16)
+    )
+    grad_att = split_product(grad_branch_low, w_out, 1, 1).astype(bf16)
+    grad_mixed_low, grad_gain_query, grad_gain_key = attend_backward(
+        mixed, cosine, sine, gain_query, gain_key, attended, totals, grad_att, heads, ratio, block
+    )
+    sum_qkv = near_far(
+        lambda far: split_product(chip_rows(normed_low, far), grad_mixed_low, 0, 0).astype(bf16),
+        True,
+    )
+    normed_part = split_product(grad_mixed_low, w_qkv, 1, 1).astype(bf16)
+
+    def share_rows(part):
+        return take_rows(part, own_targets, chunk).astype(f32) + over_core(
+            take_rows(part, peer_targets, chunk)
+        ).astype(f32)
+
+    def to_stored(rows_here):
+        stored = rows_here.astype(bf16).reshape(2, local_len, width)
+        from_far = over_chip(stored[1])
+        first = jnp.where(half == 0, stored[0], from_far)
+        last = jnp.where(half == 0, from_far, stored[0])
+        return jnp.stack([first, last])
+
+    layer_out = to_stored(take_rows(middle, own_targets, chunk) + share_rows(result_part))
+    grad_normed = share_rows(normed_part)
+    own_tokens = take_rows(hidden, own_targets, chunk).astype(f32)
+    unused, pull_one = jax.vjp(rms_scale, own_tokens, gain_one)
+    grad_token_part, grad_gain_one = pull_one(grad_normed)
+    input_grad = to_stored(take_rows(grad_middle, own_targets, chunk) + grad_token_part)
+
+    def swap_rows(chip_sum):
+        lead = chip_sum.shape[0] // 2
+        mine = lax.dynamic_slice_in_dim(chip_sum, rank * lead, lead, 0)
+        theirs = lax.dynamic_slice_in_dim(chip_sum, (1 - rank) * lead, lead, 0)
+        return jnp.concatenate([mine, over_core(theirs)], axis=0)
+
+    bits = []
+    step = 1
+    while step < copies:
+        bits.append(step)
+        step *= 2
+
+    def dp_sum(value):
+        for bit in bits:
+            size = value.shape[0] // 2
+            at = (copy // bit) % 2
+            sent = lax.dynamic_slice_in_dim(value, (1 - at) * size, size, 0)
+            kept = lax.dynamic_slice_in_dim(value, at * size, size, 0)
+            received = permute(sent, lambda d, g: (d ^ bit, g))
+            value = (kept.astype(f32) + received.astype(f32)).astype(bf16)
+        for bit in reversed(bits):
+            size = value.shape[0]
+            at = (copy // bit) % 2
+            received = permute(value, lambda d, g: (d ^ bit, g))
+            whole = jnp.zeros((2 * size, value.shape[1]), bf16)
+            whole = lax.dynamic_update_slice(whole, value, (at * size, 0))
+            value = lax.dynamic_update_slice(whole, received, ((1 - at) * size, 0))
+        return value
+
+    total_down = dp_sum(sum_down).astype(f32)
+    total_gateup = dp_sum(swap_rows(sum_gateup))
+    total_out = dp_sum(sum_out).astype(f32)
+    total_qkv = dp_sum(swap_rows(sum_qkv))
+
+    def owner_blocks(total):
+        lead = total.shape[0] // 2
+        cols = total.shape[1] // 2
+        blocks = []
+        for block_number in range(groups):
+            far = (block_number // 2) ^ half
+            peer = (block_number % 2) ^ rank
+            blocks.append(lax.dynamic_slice(total, (peer * lead, far * cols), (lead, cols)))
+        return blocks
+
+    gateup_blocks = owner_blocks(total_gateup)
+    total_gateup = jnp.concatenate(
+        [blocked[:, :ff] for blocked in gateup_blocks]
+        + [blocked[:, ff:] for blocked in gateup_blocks],
+        axis=1,
+    ).astype(f32)
+    wide = (ratio + 2) * HD
+    head_blocks = [
+        blocked[:, number * wide : (number + 1) * wide]
+        for blocked in owner_blocks(total_qkv)
+        for number in range(blocked.shape[1] // wide)
+    ]
+    total_qkv = jnp.concatenate(
+        [blocked[:, : ratio * HD] for blocked in head_blocks]
+        + [blocked[:, ratio * HD : (ratio + 1) * HD] for blocked in head_blocks]
+        + [blocked[:, (ratio + 1) * HD :] for blocked in head_blocks],
+        axis=1,
+    ).astype(f32)
+    counted = jnp.where(rank == 0, 1.0, 0.0).astype(f32)
+    grad_gains = jnp.concatenate(
+        [grad_gain_one, grad_gain_two * counted, grad_gain_query[0], grad_gain_key[0]]
+    )
+    total_gains = lax.psum(grad_gains, ALL)
+    gain_rows = gain_weight.shape[0]
+    total_gain = lax.dynamic_slice_in_dim(total_gains, member * gain_rows, gain_rows, 0)
+
+    out_fan = H * HD * 8 // seq_len
+    qkv_new = adam_step(qkv_weight, qkv_moment, qkv_square, total_qkv, LR_MULT * D ** (-0.5), DECAY)
+    out_new = adam_step(
+        out_weight, out_moment, out_square, total_out, LR_MULT * out_fan ** (-0.5), DECAY
+    )
+    gateup_new = adam_step(
+        gateup_weight, gateup_moment, gateup_square, total_gateup, LR_MULT * D ** (-0.5), DECAY
+    )
+    down_new = adam_step(
+        down_weight, down_moment, down_square, total_down, LR_MULT * FF ** (-0.5), DECAY
+    )
+    gain_new = adam_step(gain_weight, gain_moment, gain_square, total_gain, GAIN_RATE, 0.0)
+    return (layer_out, input_grad, *qkv_new, *out_new, *gateup_new, *down_new, *gain_new)
+
+
+def shards(hidden_in, *others):
+    groups = lax.axis_size("group")
+    copies = lax.axis_size("dp")
+    two_ranks = hidden_in.shape[0] == 2 and groups == 4
+    if two_ranks and copies % 2 == 0 and copies & (copies - 1) == 0:
+        return paired_shards(hidden_in, *others)
+    return general_shards(hidden_in, *others)
+
+
 def solution(mesh):
     return jax.shard_map(
         shards,

time: 1260 us -> 913 us (0.72)
  waiting for transfers between devices: 584 us -> 262 us
  Pallas kernels: 0 us -> 188 us
  matrix products: 218 us -> 91 us
  local copies, waits for them, and re-layouts: 253 us -> 128 us
  starting transfers between devices: 0.72 us -> 60.2 us
  other arithmetic: 132 us -> 93.9 us
  blocking collectives: 38 us -> 73.4 us
    ppermute x0 -> x50, waiting for transfers between devices: none -> 262 us  [permute(): return lax.ppermute(value, ALL, pairs)]
    reduce_scatter x4 -> x0, waiting for transfers between devices: 261 us -> none  [the longest x1 102 us: shards(): lax.psum_scatter(grad_gateup.astype(jnp.bfloat16), 'group', scatter_dimen...]
    psum x1 -> x0, waiting for transfers between devices: 206 us -> none  [shards(): lax.psum(part_qkv.astype(jnp.bfloat16), 'dp').astype(jnp.float32)]
    pallas_call x0 -> x4, Pallas kernels: none -> 188 us  [the longest x2 131 us: place_rows(): pl.pallas_call(kernel, out_shape=jax.ShapeDtypeStruct((count * chunk, wid...]
    dot_general x40 -> x16, matrix products: 218 us -> 91 us  [split_product(): lax.dot_general(left, right, (((left_dim,), (right_dim,)), ((), ())), pre...]
    all_gather x6 -> x0, waiting for transfers between devices: 108 us -> none  [the longest x1 44.6 us: shards(): lax.all_gather(qkv_weight.astype(bf16), 'group', axis=0, tiled=True)]
    ppermute x0 -> x50, starting transfers between devices: none -> 60.2 us  [permute(): return lax.ppermute(value, ALL, pairs)]
    unnamed x147 -> x212, local copies, waits for them, and re-layouts: 62.1 us -> 13.8 us
  transfers between devices with their start and end apart: 12 -> 50, of which waited for: 9 -> 24; matrix products, arithmetic and copies ran while one was open for 22% -> 28% of each run, Pallas kernels for 0% -> 13%
where the time goes in v1:
time: 913 us; the launch traced here: 907 us
  waiting for transfers between devices  262 us (29%)
  Pallas kernels  188 us (21%)
  local copies, waits for them, and re-layouts  128 us (14%)
  other arithmetic  93.9 us (10%)
  matrix products  91 us (10%)
  blocking collectives  73.4 us (8%)
  starting transfers between devices  60.2 us (7%)
  between operations  10.6 us (1%)
    ppermute x50, waiting for transfers between devices, permute(): return lax.ppermute(value, ALL, pairs)  262 us
    pallas_call x2, Pallas kernels, place_rows(): pl.pallas_call(kernel, out_shape=jax.ShapeDtypeStruct((count * chunk, wid...  131 us
    dot_general x16, matrix products, split_product(): lax.dot_general(left, right, (((left_dim,), (right_dim,)), ((), ())), pre...  91 us
    ppermute x50, starting transfers between devices, permute(): return lax.ppermute(value, ALL, pairs)  60.2 us
    psum x1, blocking collectives, paired_shards(): total_gains = lax.psum(grad_gains, ALL)  59.9 us
    pallas_call x1, Pallas kernels, attend_backward(): pl.pallas_call(kernel, grid=(heads,), in_specs=[pl.BlockSpec((rows, wide)...  34.9 us
    dynamic_update_slice x2, local copies, waits for them, and re-layouts, columns_join(): lax.dynamic_update_slice(whole, from_chip, ((1 - half) * lead, side * (co...  31.1 us
    sub x5, other arithmetic, adam_step(): return (weight - rate * (ratio + decay * weight), moment_new, square_new)  29.2 us
  transfers between devices with their start and end apart: 50, of which 24 were waited for; matrix products, arithmetic and copies ran while one was open for 28% of the time, Pallas kernels for 13%

profile of v1, /device:TPU:0, one launch (start us, length us, event | category | flops | bytes accessed | tf_op | source)
XLA Modules:
  0.0 907.4 jit_solution(10104133682458715486)
XLA Ops:
  23.3 13.5 %all-reduce.6 = bf16[2304]{0:T(1024)(128)(2,1)S(1)} all-reduce(bf16[2304]{0:T(1024)(128)(2,1)S(1)} %dynamic-update-slice), channel_id=1, replica_groups=mesh['dp'=8,'group'=4] {'group'}, use_global_device_ids=true, to_apply=%add.6 | all-reduce | flops 2304 | bytes 9216
  71.0 65.4 %place_rows.2 = bf16[1024,1024]{1,0:T(8,128)(2,1)} custom-call(s32[8]{0:T(128)} %concatenate.79.targets_ref, bf16[512,1024]{1,0:T(8,128)(2,1)} %pad_maximum_fusion.2.refs_0_, bf16[512,1024]{1,0:T(8,128)(2,1)} %collective-permute-done.1.refs_1_), custom_call_target="tpu_custom_call" | custom-call | bytes 4194304 | tf_op jit(solution)/shard_map/place_rows/pallas_call | solution.py:366
  147.2 13.2 %dynamic_update_slice.123 = bf16[1024,2048]{1,0:T(8,128)(2,1)S(1)} dynamic-update-slice(bf16[1024,2048]{1,0:T(8,128)(2,1)S(1)} %copy-done.34, bf16[512,1024]{1,0:T(8,128)(2,1)} %collective-permute-done.3, s32[]{:T(128)S(6)} %select_n.397, s32[]{:T(128)S(6)} %select_n.398) | dynamic-update-slice | bytes 2097156 | tf_op jit(solution)/shard_map/dynamic_update_slice | solution.py:747
  163.0 8.5 dynamic_update_slice.124
  178.2 22.1 %attend_forward.1 = (bf16[1024,1024]{1,0:T(8,128)(2,1)S(1)}, f32[1024,512]{1,0:T(8,128)S(1)}) custom-call(f32[1024,2048]{1,0:T(8,128)} %fusion.75.mixed_ref, f32[1024,128]{1,0:T(8,128)S(1)} %get-tuple-element.142.cos_ref, f32[1024,128]{1,0:T(8,128)S(1)} %get-tuple-element.143.sin_ref, f32[1,128]{1,0:T(1,128)S(1)} %get-tuple-element.127.gq_ref, ...), custom_call_target="tpu_custom_call" | custom-call | flops 2684354560 | bytes 12582912 | tf_op jit(solution)/shard_map/attend_forward/pallas_call | solution.py:456
  221.1 8.5 collective-permute-done.11
  239.4 13.0 %collective-permute-done.12 = bf16[384,1024]{1,0:T(8,128)(2,1)S(1)} collective-permute-done((bf16[384,1024]{1,0:T(8,128)(2,1)}, bf16[384,1024]{1,0:T(8,128)(2,1)S(1)}, u32[]{:S(2)}, u32[]{:S(2)}) %collective-permute-start.12) | collective-permute-done | bytes 786464 | tf_op jit(solution)/shard_map/ppermute | solution.py:659
  253.4 17.9 %dynamic_update_slice.131 = bf16[1024,3072]{1,0:T(8,128)(2,1)S(1)} dynamic-update-slice(bf16[1024,3072]{1,0:T(8,128)(2,1)S(1)} %constant_dynamic-update-slice_fusion.42, bf16[512,1536]{1,0:T(8,128)(2,1)} %collective-permute-done.9, s32[]{:T(128)S(6)} %select_n.397, s32[]{:T(128)S(6)} %select_n.408) | dynamic-update-slice | bytes 3145732 | tf_op jit(solution)/shard_map/dynamic_update_slice | solution.py:747
  277.0 8.2 collective-permute-done.10
  285.2 12.7 %dynamic_update_slice.132 = bf16[1024,3072]{1,0:T(8,128)(2,1)S(1)} dynamic-update-slice(bf16[1024,3072]{1,0:T(8,128)(2,1)S(1)} %dynamic_update_slice.131, bf16[512,1536]{1,0:T(8,128)(2,1)S(1)} %collective-permute-done.10, s32[]{:T(128)S(6)} %select_n.397, s32[]{:T(128)S(6)} %select_n.407) | dynamic-update-slice | bytes 3145732 | tf_op jit(solution)/shard_map/dynamic_update_slice | solution.py:750
  297.9 9.1 fusion.76
  307.0 65.4 %place_rows.3 = bf16[1024,1024]{1,0:T(8,128)(2,1)} custom-call(s32[8]{0:T(128)} %concatenate.79.targets_ref, bf16[512,1024]{1,0:T(8,128)(2,1)} %copy-done.24, bf16[512,1024]{1,0:T(8,128)(2,1)} %collective-permute-done.16.refs_1_), custom_call_target="tpu_custom_call" | custom-call | bytes 4194304 | tf_op jit(solution)/shard_map/place_rows/pallas_call | solution.py:366
  386.0 12.6 %convolution_convert_fusion.7 = bf16[1024,1024]{1,0:T(8,128)(2,1)} fusion(bf16[1024,3072]{1,0:T(8,128)(2,1)} %copy-done.20, f32[1024,768]{1,0:T(8,128)} %get-tuple-element.66, f32[1024,768]{1,0:T(8,128)} %get-tuple-element.67, f32[1024,768]{1,0:T(8,128)} %get-tuple-element.65, f32[1024,768]{1,0:T(8,128)} %get-tuple-element.64), kind=kOutput, calls=%fused_computation.91 | convolution fusion | flops 6456082432 | bytes 20971520 | tf_op jit(solution)/shard_map/dot_general | solution.py:338
  411.4 10.2 %convolution_convert_fusion = bf16[512,3072]{1,0:T(8,128)(2,1)} fusion(bf16[1024,1024]{1,0:T(8,128)(2,1)} %copy-done.51, s32[]{:T(128)S(6)} %select_n.397, f32[1024,768]{1,0:T(8,128)} %get-tuple-element.66, f32[1024,768]{1,0:T(8,128)} %get-tuple-element.67, f32[1024,768]{1,0:T(8,128)} %get-tuple-element.65, f32[1024,768]{1,0:T(8,128)} %get-tuple-element.64), kind=kOutput, calls=%fused_computation.16 | convolution fusion | flops 3235381248 | bytes 16777220 | tf_op jit(solution)/shard_map/dot_general | solution.py:338
  429.4 11.9 %collective-permute-done.43 = bf16[768,1024]{1,0:T(8,128)(2,1)} collective-permute-done((bf16[768,1024]{1,0:T(8,128)(2,1)}, bf16[768,1024]{1,0:T(8,128)(2,1)}, u32[]{:S(2)}, u32[]{:S(2)}) %collective-permute-start.43) | collective-permute-done | bytes 1572896 | tf_op jit(solution)/shard_map/ppermute | solution.py:659
  444.3 7.7 collective-permute-start.44
  460.6 34.9 %attend_backward.1 = (bf16[1024,2048]{1,0:T(8,128)(2,1)}, f32[1,128]{1,0:T(1,128)S(1)}, f32[1,128]{1,0:T(1,128)S(1)}) custom-call(f32[1024,2048]{1,0:T(8,128)} %fusion.75.mixed_ref, f32[1024,128]{1,0:T(8,128)S(1)} %get-tuple-element.142.cos_ref, f32[1024,128]{1,0:T(8,128)S(1)} %get-tuple-element.143.sin_ref, f32[1,128]{1,0:T(1,128)S(1)} %get-tuple-element.127.gq_ref, ...), custom_call_target="tpu_custom_call" | custom-call | flops 6710886400 | bytes 18874368 | tf_op jit(solution)/shard_map/attend_backward/pallas_call | solution.py:580
  530.1 8.5 collective-permute-done.46
  544.1 10.2 %add_convert_fusion.1 = bf16[512,3072]{1,0:T(8,128)(2,1)} fusion(bf16[512,1536]{1,0:T(8,128)(2,1)} %get-tuple-element.81, bf16[512,1536]{1,0:T(8,128)(2,1)} %get-tuple-element.80, bf16[1024,1024]{1,0:T(8,128)(2,1)} %copy-done.51, s32[]{:T(128)S(6)} %select_n.394, f32[1024,768]{1,0:T(8,128)} %get-tuple-element.66, f32[1024,768]{1,0:T(8,128)} %get-tuple-element.67, ...), kind=kOutput, calls=%fused_computation.6 | convolution fusion | flops 3246391296 | bytes 19922948 | tf_op jit(solution)/shard_map/dot_general | solution.py:338
  560.3 8.1 collective-permute-start.29
  579.0 59.9 %psum.7 = f32[2304]{0:T(1024)S(1)} all-reduce(f32[2304]{0:T(1024)S(1)} %pad_maximum_fusion.13), channel_id=1, replica_groups=mesh['dp'=8,'group'=4] {'dp','group'}, use_global_device_ids=true, to_apply=%region_7.8 | all-reduce | flops 2304 | bytes 18432 | tf_op jit(solution)/shard_map/psum | solution.py:943
  644.8 8.6 collective-permute-done.48
  686.3 41.2 %collective-permute-done.34 = bf16[256,1024]{1,0:T(8,128)(2,1)S(1)} collective-permute-done((bf16[256,1024]{1,0:T(8,128)(2,1)S(1)}, bf16[256,1024]{1,0:T(8,128)(2,1)S(1)}, u32[]{:S(2)}, u32[]{:S(2)}) %collective-permute-start.34) | collective-permute-done | bytes 524320 | tf_op jit(solution)/shard_map/ppermute | solution.py:659
  733.5 20.0 %collective-permute-done.22 = bf16[256,2048]{1,0:T(8,128)(2,1)S(1)} collective-permute-done((bf16[256,2048]{1,0:T(8,128)(2,1)S(1)}, bf16[256,2048]{1,0:T(8,128)(2,1)S(1)}, u32[]{:S(2)}, u32[]{:S(2)}) %collective-permute-start.22) | collective-permute-done | bytes 1048608 | tf_op jit(solution)/shard_map/ppermute | solution.py:659
  770.9 19.3 %collective-permute-done.24 = bf16[64,2048]{1,0:T(8,128)(2,1)S(1)} collective-permute-done((bf16[64,2048]{1,0:T(8,128)(2,1)S(1)}, bf16[64,2048]{1,0:T(8,128)(2,1)S(1)}, u32[]{:S(2)}, u32[]{:S(2)}) %collective-permute-start.24) | collective-permute-done | bytes 262176 | tf_op jit(solution)/shard_map/ppermute | solution.py:659
  790.4 13.8 %collective-permute-done.39 = bf16[64,3072]{1,0:T(8,128)(2,1)S(1)} collective-permute-done((bf16[64,3072]{1,0:T(8,128)(2,1)S(1)}, bf16[64,3072]{1,0:T(8,128)(2,1)S(1)}, u32[]{:S(2)}, u32[]{:S(2)}) %collective-permute-start.39) | collective-permute-done | bytes 393248 | tf_op jit(solution)/shard_map/ppermute | solution.py:659
  804.5 13.8 %collective-permute-done.25 = bf16[64,2048]{1,0:T(8,128)(2,1)S(1)} collective-permute-done((bf16[64,2048]{1,0:T(8,128)(2,1)S(1)}, bf16[64,2048]{1,0:T(8,128)(2,1)S(1)}, u32[]{:S(2)}, u32[]{:S(2)}) %collective-permute-start.25) | collective-permute-done | bytes 262176 | tf_op jit(solution)/shard_map/ppermute | solution.py:659
  825.7 11.1 %collective-permute-done.26 = bf16[128,2048]{1,0:T(8,128)(2,1)S(1)} collective-permute-done((bf16[128,2048]{1,0:T(8,128)(2,1)S(1)}, bf16[128,2048]{1,0:T(8,128)(2,1)S(1)}, u32[]{:S(2)}, u32[]{:S(2)}) %collective-permute-start.26) | collective-permute-done | bytes 524320 | tf_op jit(solution)/shard_map/ppermute | solution.py:659
  838.6 15.0 %collective-permute-done.41 = bf16[128,3072]{1,0:T(8,128)(2,1)S(1)} collective-permute-done((bf16[128,3072]{1,0:T(8,128)(2,1)S(1)}, bf16[128,3072]{1,0:T(8,128)(2,1)S(1)}, u32[]{:S(2)}, u32[]{:S(2)}) %collective-permute-start.41) | collective-permute-done | bytes 786464 | tf_op jit(solution)/shard_map/ppermute | solution.py:659
  864.1 9.3 %multiply_subtract_fusion.1 = (f32[256,4096]{1,0:T(8,128)}, f32[256,4096]{1,0:T(8,128)}, f32[256,4096]{1,0:T(8,128)}) fusion(f32[256,4096]{1,0:T(8,128)S(1)} %copy-done.13, bf16[256,4096]{1,0:T(8,128)(2,1)S(1)} %constant_dynamic-update-slice_fusion, f32[256,4096]{1,0:T(8,128)} %param.24, f32[256,4096]{1,0:T(8,128)} %param.25), kind=kLoop, calls=%fused_computation.25 | loop fusion | flops 16777216 | bytes 27262976 | tf_op jit(solution)/shard_map/sub | solution.py:93
  873.4 22.3 %collective-permute-done.42 = bf16[256,3072]{1,0:T(8,128)(2,1)S(1)} collective-permute-done((bf16[256,3072]{1,0:T(8,128)(2,1)S(1)}, bf16[256,3072]{1,0:T(8,128)(2,1)S(1)}, u32[]{:S(2)}, u32[]{:S(2)}) %collective-permute-start.42) | collective-permute-done | bytes 1572896 | tf_op jit(solution)/shard_map/ppermute | solution.py:659
  896.3 10.6 %multiply_subtract_fusion = (f32[256,6144]{1,0:T(8,128)}, f32[256,6144]{1,0:T(8,128)}, f32[256,6144]{1,0:T(8,128)}) fusion(f32[256,6144]{1,0:T(8,128)S(1)} %bitcast.77, bf16[256,6144]{1,0:T(8,128)(2,1)S(1)} %dynamic-slice_dynamic-update-slice_fusion, f32[256,6144]{1,0:T(8,128)S(1)} %bitcast.80, f32[256,6144]{1,0:T(8,128)} %param.31), kind=kLoop, calls=%fused_computation.5 | loop fusion | flops 25165824 | bytes 40894464 | tf_op jit(solution)/shard_map/sub | solution.py:93
  (464 shorter events, 290.7 us)
Async XLA Ops:
  9.7 132.0 %collective-permute-start.8 = (bf16[256,3072]{1,0:T(8,128)(2,1)}, bf16[256,3072]{1,0:T(8,128)(2,1)}, u32[]{:S(2)}, u32[]{:S(2)}) collective-permute-start(bf16[256,3072]{1,0:T(8,128)(2,1)} %pad_maximum_fusion.1), channel_id=1, source_target_pairs={{0,1},{1,0},{2,3},{3,2},{4,5},{5,4},{6,7},{7,6},{8,9},{9,8},{10,11... | collective-permute-start | bytes 4718600 | tf_op jit(solution)/shard_map/ppermute | solution.py:659
  16.8 33.3 %collective-permute-start.2 = (bf16[256,2048]{1,0:T(8,128)(2,1)}, bf16[256,2048]{1,0:T(8,128)(2,1)}, u32[]{:S(2)}, u32[]{:S(2)}) collective-permute-start(bf16[256,2048]{1,0:T(8,128)(2,1)} %pad_maximum_fusion.3), channel_id=1, source_target_pairs={{0,1},{1,0},{2,3},{3,2},{4,5},{5,4},{6,7},{7,6},{8,9},{9,8},{10,11... | collective-permute-start | bytes 3145736 | tf_op jit(solution)/shard_map/ppermute | solution.py:659
  18.3 28.1 %collective-permute-start = (bf16[256,1024]{1,0:T(8,128)(2,1)}, bf16[256,1024]{1,0:T(8,128)(2,1)}, u32[]{:S(2)}, u32[]{:S(2)}) collective-permute-start(bf16[256,1024]{1,0:T(8,128)(2,1)} %get-tuple-element.125), channel_id=1, source_target_pairs={{0,2},{1,3},{2,0},{3,1},{4,6},{5,7},{6,4},{7,5},{8,10},{9,11},{10,... | collective-permute-start | bytes 1572872 | tf_op jit(solution)/shard_map/ppermute | solution.py:659
  52.4 86.1 %collective-permute-start.3 = (bf16[512,1024]{1,0:T(8,128)(2,1)}, bf16[512,1024]{1,0:T(8,128)(2,1)}, u32[]{:S(2)}, u32[]{:S(2)}) collective-permute-start(bf16[512,1024]{1,0:T(8,128)(2,1)} %constant_dynamic-slice_fusion.46), channel_id=1, source_target_pairs={{0,2},{1,3},{2,0},{3,1},{4,6},{5,7},{6,4},{7,5},{8,10},{9,11},{10,... | collective-permute-start | bytes 3145736 | tf_op jit(solution)/shard_map/ppermute | solution.py:659
  64.8 74.4 %collective-permute-start.6 = (bf16[256,1024]{1,0:T(8,128)(2,1)}, bf16[256,1024]{1,0:T(8,128)(2,1)}, u32[]{:S(2)}, u32[]{:S(2)}) collective-permute-start(bf16[256,1024]{1,0:T(8,128)(2,1)} %collective-permute-done.5), channel_id=1, source_target_pairs={{0,4},{1,5},{2,6},{3,7},{4,0},{5,1},{6,2},{7,3},{8,12},{9,13},{10,... | collective-permute-start | bytes 1572872 | tf_op jit(solution)/shard_map/ppermute | solution.py:659
  146.9 87.8 %collective-permute-start.9 = (bf16[512,1536]{1,0:T(8,128)(2,1)}, bf16[512,1536]{1,0:T(8,128)(2,1)}, u32[]{:S(2)}, u32[]{:S(2)}) collective-permute-start(bf16[512,1536]{1,0:T(8,128)(2,1)} %constant_dynamic-slice_fusion.39), channel_id=1, source_target_pairs={{0,2},{1,3},{2,0},{3,1},{4,6},{5,7},{6,4},{7,5},{8,10},{9,11},{10,... | collective-permute-start | bytes 4718600 | tf_op jit(solution)/shard_map/ppermute | solution.py:659
  204.0 67.5 %collective-permute-start.7 = (bf16[1024,1024]{1,0:T(8,128)(2,1)}, bf16[1024,1024]{1,0:T(8,128)(2,1)}, u32[]{:S(2)}, u32[]{:S(2)}) collective-permute-start(bf16[1024,1024]{1,0:T(8,128)(2,1)} %convolution_convert_fusion.6), channel_id=1, source_target_pairs={{0,1},{1,0},{2,3},{3,2},{4,5},{5,4},{6,7},{7,6},{8,9},{9,8},{10,11... | collective-permute-start | bytes 6291464 | tf_op jit(solution)/shard_map/ppermute | solution.py:659
  234.7 36.5 %collective-permute-start.15 = (bf16[256,1024]{1,0:T(8,128)(2,1)S(1)}, bf16[256,1024]{1,0:T(8,128)(2,1)S(1)}, u32[]{:S(2)}, u32[]{:S(2)}) collective-permute-start(bf16[256,1024]{1,0:T(8,128)(2,1)S(1)} %get-tuple-element.30), channel_id=1, source_target_pairs={{0,2},{1,3},{2,0},{3,1},{4,6},{5,7},{6,4},{7,5},{8,10},{9,11},{10,... | collective-permute-start | bytes 1572872 | tf_op jit(solution)/shard_map/ppermute | solution.py:659
  236.0 49.2 %collective-permute-start.10 = (bf16[512,1536]{1,0:T(8,128)(2,1)}, bf16[512,1536]{1,0:T(8,128)(2,1)S(1)}, u32[]{:S(2)}, u32[]{:S(2)}) collective-permute-start(bf16[512,1536]{1,0:T(8,128)(2,1)} %collective-permute-done.9), channel_id=1, source_target_pairs={{0,4},{1,5},{2,6},{3,7},{4,0},{5,1},{6,2},{7,3},{8,12},{9,13},{10,... | collective-permute-start | bytes 4718600 | tf_op jit(solution)/shard_map/ppermute | solution.py:659
  271.4 35.6 %collective-permute-start.16 = (bf16[512,1024]{1,0:T(8,128)(2,1)S(1)}, bf16[512,1024]{1,0:T(8,128)(2,1)}, u32[]{:S(2)}, u32[]{:S(2)}) collective-permute-start(bf16[512,1024]{1,0:T(8,128)(2,1)S(1)} %pad_maximum_fusion.6.refs_0_), channel_id=1, source_target_pairs={{0,1},{1,0},{2,3},{3,2},{4,5},{5,4},{6,7},{7,6},{8,9},{9,8},{10,11... | collective-permute-start | bytes 3145736 | tf_op jit(solution)/shard_map/ppermute | solution.py:659
  398.6 55.0 %collective-permute-start.17 = (bf16[1024,1024]{1,0:T(8,128)(2,1)}, bf16[1024,1024]{1,0:T(8,128)(2,1)S(1)}, u32[]{:S(2)}, u32[]{:S(2)}) collective-permute-start(bf16[1024,1024]{1,0:T(8,128)(2,1)} %convolution_convert_fusion.7), channel_id=1, source_target_pairs={{0,1},{1,0},{2,3},{3,2},{4,5},{5,4},{6,7},{7,6},{8,9},{9,8},{10,11... | collective-permute-start | bytes 6291464 | tf_op jit(solution)/shard_map/ppermute | solution.py:659
  403.8 37.5 %collective-permute-start.43 = (bf16[768,1024]{1,0:T(8,128)(2,1)}, bf16[768,1024]{1,0:T(8,128)(2,1)}, u32[]{:S(2)}, u32[]{:S(2)}) collective-permute-start(bf16[768,1024]{1,0:T(8,128)(2,1)} %convolution_convert_fusion.8), channel_id=1, source_target_pairs={{0,2},{1,3},{2,0},{3,1},{4,6},{5,7},{6,4},{7,5},{8,10},{9,11},{10,... | collective-permute-start | bytes 4718600 | tf_op jit(solution)/shard_map/ppermute | solution.py:659
  425.3 27.1 %collective-permute-start.14 = (bf16[256,1024]{1,0:T(8,128)(2,1)S(1)}, bf16[256,1024]{1,0:T(8,128)(2,1)S(1)}, u32[]{:S(2)}, u32[]{:S(2)}) collective-permute-start(bf16[256,1024]{1,0:T(8,128)(2,1)S(1)} %slice.285), channel_id=1, source_target_pairs={{0,2},{1,3},{2,0},{3,1},{4,6},{5,7},{6,4},{7,5},{8,10},{9,11},{10,... | collective-permute-start | bytes 1572872 | tf_op jit(solution)/shard_map/ppermute | solution.py:659
  427.8 112.4 %collective-permute-start.35 = (bf16[512,3072]{1,0:T(8,128)(2,1)}, bf16[512,3072]{1,0:T(8,128)(2,1)}, u32[]{:S(2)}, u32[]{:S(2)}) collective-permute-start(bf16[512,3072]{1,0:T(8,128)(2,1)} %convolution_convert_fusion), channel_id=1, source_target_pairs={{0,2},{1,3},{2,0},{3,1},{4,6},{5,7},{6,4},{7,5},{8,10},{9,11},{10,... | collective-permute-start | bytes 9437192 | tf_op jit(solution)/shard_map/ppermute | solution.py:659
  444.3 70.3 %collective-permute-start.44 = (bf16[384,1024]{1,0:T(8,128)(2,1)}, bf16[384,1024]{1,0:T(8,128)(2,1)}, u32[]{:S(2)}, u32[]{:S(2)}) collective-permute-start(bf16[384,1024]{1,0:T(8,128)(2,1)} %constant_dynamic-slice_fusion.2), channel_id=1, source_target_pairs={{0,4},{1,5},{2,6},{3,7},{4,0},{5,1},{6,2},{7,3},{8,12},{9,13},{10,... | collective-permute-start | bytes 2359304 | tf_op jit(solution)/shard_map/ppermute | solution.py:659
  507.0 61.3 %collective-permute-start.18 = (bf16[512,1024]{1,0:T(8,128)(2,1)}, bf16[512,1024]{1,0:T(8,128)(2,1)}, u32[]{:S(2)}, u32[]{:S(2)}) collective-permute-start(bf16[512,1024]{1,0:T(8,128)(2,1)} %pad_maximum_fusion.8), channel_id=1, source_target_pairs={{0,1},{1,0},{2,3},{3,2},{4,5},{5,4},{6,7},{7,6},{8,9},{9,8},{10,11... | collective-permute-start | bytes 3145736 | tf_op jit(solution)/shard_map/ppermute | solution.py:659
  507.1 50.7 %collective-permute-start.28 = (bf16[512,1024]{1,0:T(8,128)(2,1)}, bf16[512,1024]{1,0:T(8,128)(2,1)}, u32[]{:S(2)}, u32[]{:S(2)}) collective-permute-start(bf16[512,1024]{1,0:T(8,128)(2,1)} %convolution_convert_fusion.10), channel_id=1, source_target_pairs={{0,2},{1,3},{2,0},{3,1},{4,6},{5,7},{6,4},{7,5},{8,10},{9,11},{10,... | collective-permute-start | bytes 3145736 | tf_op jit(solution)/shard_map/ppermute | solution.py:659
  512.3 160.0 %collective-permute-start.20 = (bf16[512,2048]{1,0:T(8,128)(2,1)}, bf16[512,2048]{1,0:T(8,128)(2,1)}, u32[]{:S(2)}, u32[]{:S(2)}) collective-permute-start(bf16[512,2048]{1,0:T(8,128)(2,1)} %convolution_convert_fusion.2), channel_id=1, source_target_pairs={{0,2},{1,3},{2,0},{3,1},{4,6},{5,7},{6,4},{7,5},{8,10},{9,11},{10,... | collective-permute-start | bytes 6291464 | tf_op jit(solution)/shard_map/ppermute | solution.py:659
  540.2 99.3 %collective-permute-start.47 = (bf16[96,1024]{1,0:T(8,128)(2,1)}, bf16[96,1024]{1,0:T(8,128)(2,1)}, u32[]{:S(2)}, u32[]{:S(2)}) collective-permute-start(bf16[96,1024]{1,0:T(8,128)(2,1)} %get-tuple-element.46), channel_id=1, source_target_pairs={{0,16},{1,17},{2,18},{3,19},{4,20},{5,21},{6,22},{7,23},{8,24},{9,... | collective-permute-start | bytes 589832 | tf_op jit(solution)/shard_map/ppermute | solution.py:659
  557.7 119.7 %collective-permute-start.36 = (bf16[256,3072]{1,0:T(8,128)(2,1)}, bf16[256,3072]{1,0:T(8,128)(2,1)S(1)}, u32[]{:S(2)}, u32[]{:S(2)}) collective-permute-start(bf16[256,3072]{1,0:T(8,128)(2,1)} %get-tuple-element.78), channel_id=1, source_target_pairs={{0,1},{1,0},{2,3},{3,2},{4,5},{5,4},{6,7},{7,6},{8,9},{9,8},{10,11... | collective-permute-start | bytes 4718600 | tf_op jit(solution)/shard_map/ppermute | solution.py:659
  560.3 81.3 %collective-permute-start.29 = (bf16[256,1024]{1,0:T(8,128)(2,1)}, bf16[256,1024]{1,0:T(8,128)(2,1)}, u32[]{:S(2)}, u32[]{:S(2)}) collective-permute-start(bf16[256,1024]{1,0:T(8,128)(2,1)} %constant_dynamic-slice_fusion.9), channel_id=1, source_target_pairs={{0,4},{1,5},{2,6},{3,7},{4,0},{5,1},{6,2},{7,3},{8,12},{9,13},{10,... | collective-permute-start | bytes 1572872 | tf_op jit(solution)/shard_map/ppermute | solution.py:659
  578.1 79.6 %collective-permute-start.19 = (bf16[256,1024]{1,0:T(8,128)(2,1)}, bf16[256,1024]{1,0:T(8,128)(2,1)}, u32[]{:S(2)}, u32[]{:S(2)}) collective-permute-start(bf16[256,1024]{1,0:T(8,128)(2,1)} %slice.287), channel_id=1, source_target_pairs={{0,2},{1,3},{2,0},{3,1},{4,6},{5,7},{6,4},{7,5},{8,10},{9,11},{10,... | collective-permute-start | bytes 1572872 | tf_op jit(solution)/shard_map/ppermute | solution.py:659
  677.2 50.4 %collective-permute-start.21 = (bf16[256,2048]{1,0:T(8,128)(2,1)S(1)}, bf16[256,2048]{1,0:T(8,128)(2,1)S(1)}, u32[]{:S(2)}, u32[]{:S(2)}) collective-permute-start(bf16[256,2048]{1,0:T(8,128)(2,1)S(1)} %get-tuple-element.88), channel_id=1, source_target_pairs={{0,1},{1,0},{2,3},{3,2},{4,5},{5,4},{6,7},{7,6},{8,9},{9,8},{10,11... | collective-permute-start | bytes 3145736 | tf_op jit(solution)/shard_map/ppermute | solution.py:659
  678.8 51.5 %collective-permute-start.37 = (bf16[256,3072]{1,0:T(8,128)(2,1)S(1)}, bf16[256,3072]{1,0:T(8,128)(2,1)S(1)}, u32[]{:S(2)}, u32[]{:S(2)}) collective-permute-start(bf16[256,3072]{1,0:T(8,128)(2,1)S(1)} %fusion.34), channel_id=1, source_target_pairs={{0,4},{1,5},{2,6},{3,7},{4,0},{5,1},{6,2},{7,3},{8,12},{9,13},{10,... | collective-permute-start | bytes 4718600 | tf_op jit(solution)/shard_map/ppermute | solution.py:659
  681.2 46.3 %collective-permute-start.34 = (bf16[256,1024]{1,0:T(8,128)(2,1)S(1)}, bf16[256,1024]{1,0:T(8,128)(2,1)S(1)}, u32[]{:S(2)}, u32[]{:S(2)}) collective-permute-start(bf16[256,1024]{1,0:T(8,128)(2,1)S(1)} %constant_dynamic-update-slice_fusion.30), channel_id=1, source_target_pairs={{0,4},{1,5},{2,6},{3,7},{4,0},{5,1},{6,2},{7,3},{8,12},{9,13},{10,... | collective-permute-start | bytes 1572872 | tf_op jit(solution)/shard_map/ppermute | solution.py:659
  728.4 25.0 %collective-permute-start.22 = (bf16[256,2048]{1,0:T(8,128)(2,1)S(1)}, bf16[256,2048]{1,0:T(8,128)(2,1)S(1)}, u32[]{:S(2)}, u32[]{:S(2)}) collective-permute-start(bf16[256,2048]{1,0:T(8,128)(2,1)S(1)} %fusion.36), channel_id=1, source_target_pairs={{0,4},{1,5},{2,6},{3,7},{4,0},{5,1},{6,2},{7,3},{8,12},{9,13},{10,... | collective-permute-start | bytes 3145736 | tf_op jit(solution)/shard_map/ppermute | solution.py:659
  731.8 37.9 %collective-permute-start.38 = (bf16[128,3072]{1,0:T(8,128)(2,1)S(1)}, bf16[128,3072]{1,0:T(8,128)(2,1)S(1)}, u32[]{:S(2)}, u32[]{:S(2)}) collective-permute-start(bf16[128,3072]{1,0:T(8,128)(2,1)S(1)} %constant_dynamic-slice_fusion.4), channel_id=1, source_target_pairs={{0,8},{1,9},{2,10},{3,11},{4,12},{5,13},{6,14},{7,15},{8,0},{9,1},... | collective-permute-start | bytes 2359304 | tf_op jit(solution)/shard_map/ppermute | solution.py:659
  770.0 34.3 %collective-permute-start.39 = (bf16[64,3072]{1,0:T(8,128)(2,1)S(1)}, bf16[64,3072]{1,0:T(8,128)(2,1)S(1)}, u32[]{:S(2)}, u32[]{:S(2)}) collective-permute-start(bf16[64,3072]{1,0:T(8,128)(2,1)S(1)} %constant_dynamic-slice_fusion.3), channel_id=1, source_target_pairs={{0,16},{1,17},{2,18},{3,19},{4,20},{5,21},{6,22},{7,23},{8,24},{9,... | collective-permute-start | bytes 1179656 | tf_op jit(solution)/shard_map/ppermute | solution.py:659
  790.4 27.9 %collective-permute-start.25 = (bf16[64,2048]{1,0:T(8,128)(2,1)S(1)}, bf16[64,2048]{1,0:T(8,128)(2,1)S(1)}, u32[]{:S(2)}, u32[]{:S(2)}) collective-permute-start(bf16[64,2048]{1,0:T(8,128)(2,1)S(1)} %get-tuple-element.61), channel_id=1, source_target_pairs={{0,16},{1,17},{2,18},{3,19},{4,20},{5,21},{6,22},{7,23},{8,24},{9,... | collective-permute-start | bytes 786440 | tf_op jit(solution)/shard_map/ppermute | solution.py:659
  825.6 27.9 %collective-permute-start.41 = (bf16[128,3072]{1,0:T(8,128)(2,1)S(1)}, bf16[128,3072]{1,0:T(8,128)(2,1)S(1)}, u32[]{:S(2)}, u32[]{:S(2)}) collective-permute-start(bf16[128,3072]{1,0:T(8,128)(2,1)S(1)} %constant_dynamic-update-slice_fusion.26), channel_id=1, source_target_pairs={{0,8},{1,9},{2,10},{3,11},{4,12},{5,13},{6,14},{7,15},{8,0},{9,1},... | collective-permute-start | bytes 2359304 | tf_op jit(solution)/shard_map/ppermute | solution.py:659
  836.9 26.1 %collective-permute-start.27 = (bf16[256,2048]{1,0:T(8,128)(2,1)S(1)}, bf16[256,2048]{1,0:T(8,128)(2,1)S(1)}, u32[]{:S(2)}, u32[]{:S(2)}) collective-permute-start(bf16[256,2048]{1,0:T(8,128)(2,1)S(1)} %constant_dynamic-update-slice_fusion.36), channel_id=1, source_target_pairs={{0,4},{1,5},{2,6},{3,7},{4,0},{5,1},{6,2},{7,3},{8,12},{9,13},{10,... | collective-permute-start | bytes 3145736 | tf_op jit(solution)/shard_map/ppermute | solution.py:659
  853.7 42.0 %collective-permute-start.42 = (bf16[256,3072]{1,0:T(8,128)(2,1)S(1)}, bf16[256,3072]{1,0:T(8,128)(2,1)S(1)}, u32[]{:S(2)}, u32[]{:S(2)}) collective-permute-start(bf16[256,3072]{1,0:T(8,128)(2,1)S(1)} %constant_dynamic-update-slice_fusion.24), channel_id=1, source_target_pairs={{0,4},{1,5},{2,6},{3,7},{4,0},{5,1},{6,2},{7,3},{8,12},{9,13},{10,... | collective-permute-start | bytes 4718600 | tf_op jit(solution)/shard_map/ppermute | solution.py:659
  (108 other events, 1423.5 us)

commit v2 on v1

--- a/solution.py
+++ b/solution.py
@@ -340,44 +340,98 @@
     )
 
 
-def place_rows(pieces, targets, chunk):
+def place_rows(mine, theirs, targets, chunk, gain):
     count = targets.shape[0]
-    per_piece = count // len(pieces)
-    width = pieces[0].shape[1]
-
-    def kernel(targets_ref, *refs):
-        sources = refs[: len(pieces)]
-        placed, sems = refs[len(pieces) :]
-        copies = []
-        for number in range(count):
-            row = pl.multiple_of(targets_ref[number] * chunk, chunk)
-            copies.append(
-                pltpu.make_async_copy(
-                    sources[number // per_piece].at[pl.ds((number % per_piece) * chunk, chunk)],
-                    placed.at[pl.ds(row, chunk)],
-                    sems.at[number],
-                )
-            )
-        for copy in copies:
-            copy.start()
-        for copy in copies:
-            copy.wait()
-
+    width = mine.shape[1]
+    near = mine.shape[0] // chunk
+    with_norm = gain is not None
+
+    def kernel(targets_ref, mine_ref, theirs_ref, *refs):
+        step = pl.program_id(0)
+        rows = jnp.where(step < near, mine_ref[...], theirs_ref[...])
+        if with_norm:
+            gain_ref, placed, normed = refs
+            wide = rows.astype(jnp.float32)
+            normed[...] = rms_scale(wide, gain_ref[...]).astype(jnp.bfloat16)
+        else:
+            (placed,) = refs
+        placed[...] = rows
+
+    def target_row(i, targets_ref):
+        return (targets_ref[i], 0)
+
+    in_specs = [
+        pl.BlockSpec((chunk, width), lambda i, targets_ref: (jnp.minimum(i, near - 1), 0)),
+        pl.BlockSpec((chunk, width), lambda i, targets_ref: (jnp.maximum(i - near, 0), 0)),
+    ]
+    operands = [mine, theirs]
+    outputs = 1
+    if with_norm:
+        in_specs.append(pl.BlockSpec((1, width), lambda i, targets_ref: (0, 0)))
+        operands.append(gain.reshape(1, width))
+        outputs = 2
+    shape = jax.ShapeDtypeStruct((count * chunk, width), mine.dtype)
     return pl.pallas_call(
         kernel,
-        out_shape=jax.ShapeDtypeStruct((count * chunk, width), pieces[0].dtype),
+        out_shape=[shape] * outputs,
         grid_spec=pltpu.PrefetchScalarGridSpec(
             num_scalar_prefetch=1,
-            grid=(1,),
-            in_specs=[pl.BlockSpec(memory_space=pl.ANY)] * len(pieces),
-            out_specs=pl.BlockSpec(memory_space=pl.ANY),
-            scratch_shapes=[pltpu.SemaphoreType.DMA((count,))],
+            grid=(count,),
+            in_specs=in_specs,
+            out_specs=[pl.BlockSpec((chunk, width), target_row)] * outputs,
         ),
         cost_estimate=pl.CostEstimate(
-            flops=0, bytes_accessed=4 * count * chunk * width, transcendentals=0
+            flops=0, bytes_accessed=4 * outputs * count * chunk * width, transcendentals=0
         ),
         name="place_rows",
-    )(targets, *pieces)
+    )(targets, *operands)
+
+
+def join_columns(own_near, own_far, peer, chip, diagonal, chip_side, diagonal_side, where_at, parts):
+    lead, cols = own_near.shape
+    width = cols // parts
+
+    def kernel(
+        at_ref, near_ref, far_ref, peer_ref, chip_ref, diag_ref, chip_x_ref, diag_x_ref, out_ref
+    ):
+        step = pl.program_id(0)
+        same_half = step // 2 == at_ref[0]
+        same_rank = step % 2 == at_ref[1]
+        even = at_ref[2] == 0
+
+        def put(condition, first, second):
+            @pl.when(condition)
+            def _():
+                for part in range(parts):
+                    columns = slice(part * width, (part + 1) * width)
+                    low = 2 * part * width
+                    out_ref[:, low : low + width] = first[:, columns]
+                    out_ref[:, low + width : low + 2 * width] = second[:, columns]
+
+        put(same_half & same_rank, near_ref, far_ref)
+        put(same_half & ~same_rank, peer_ref.at[0], peer_ref.at[1])
+        put(~same_half & same_rank & even, chip_ref, chip_x_ref)
+        put(~same_half & same_rank & ~even, chip_x_ref, chip_ref)
+        put(~same_half & ~same_rank & even, diag_ref, diag_x_ref)
+        put(~same_half & ~same_rank & ~even, diag_x_ref, diag_ref)
+
+    flat = pl.BlockSpec((lead, cols), lambda i, at_ref: (0, 0))
+    pair = pl.BlockSpec((2, lead, cols), lambda i, at_ref: (0, 0, 0))
+    return pl.pallas_call(
+        kernel,
+        out_shape=jax.ShapeDtypeStruct((4 * lead, 2 * cols), own_near.dtype),
+        grid_spec=pltpu.PrefetchScalarGridSpec(
+            num_scalar_prefetch=1,
+            grid=(4,),
+            in_specs=[flat, flat, pair, flat, flat, flat, flat],
+            out_specs=pl.BlockSpec((lead, 2 * cols), lambda i, at_ref: (i, 0)),
+        ),
+        compiler_params=pltpu.CompilerParams(vmem_limit_bytes=48 * 1024 * 1024),
+        cost_estimate=pl.CostEstimate(
+            flops=0, bytes_accessed=32 * lead * cols, transcendentals=0
+        ),
+        name="join_columns",
+    )(where_at, own_near, own_far, peer, chip, diagonal, chip_side, diagonal_side)
 
 
 def take_rows(rows, sources, chunk):
@@ -464,7 +518,7 @@
             pl.BlockSpec((1, HD), lambda i: (0, 0)),
         ],
         out_specs=[
-            pl.BlockSpec((rows, ratio * HD), lambda i: (0, i)),
+            pl.BlockSpec((rows, ratio * HD), lambda i: (0, i % 2 * (heads // 2) + i // 2)),
             pl.BlockSpec((rows, HD), lambda i: (0, i)),
         ],
         out_shape=[
@@ -482,8 +536,9 @@
 
 
 def attend_backward(
-    mixed, cosine, sine, gain_query, gain_key, attended, totals, grad_att, heads, ratio, block
+    mixed, cosine, sine, gain_query, gain_key, attended, totals, grad_att, part, parts, ratio, block
 ):
+    heads = 2
     rows = mixed.shape[0]
     wide = (ratio + 2) * HD
     scale = HD ** (-0.5)
@@ -518,18 +573,18 @@
 
         for number in reversed(range(rows // block)):
             low, high = number * block, (number + 1) * block
-            stacked = jnp.concatenate([part[low:high] for part in query], axis=0)
+            stacked = jnp.concatenate([turned[low:high] for turned in query], axis=0)
             grads = []
             deltas = []
             for r in range(ratio):
                 lane = r * (HD // ratio)
                 inverse = 1.0 / total_ref[low:high, lane : lane + 1]
                 columns = slice(r * HD, (r + 1) * HD)
-                part = (grad_ref[low:high, columns].astype(f32) * inverse).astype(bf16)
-                grads.append(part)
+                scaled = (grad_ref[low:high, columns].astype(f32) * inverse).astype(bf16)
+                grads.append(scaled)
                 deltas.append(
                     jnp.sum(
-                        part.astype(f32) * att_ref[low:high, columns].astype(f32),
+                        scaled.astype(f32) * att_ref[low:high, columns].astype(f32),
                         axis=-1,
                         keepdims=True,
                     )
@@ -548,8 +603,8 @@
                 grad_scores = (terms * (grad_terms - delta)).astype(bf16)
                 grad_values = split_product(terms.astype(bf16), grad, 0, 0)
                 grad_keys = split_product(grad_scores, stacked, 0, 0)
-                part = split_product(grad_scores, keys[start:end], 1, 0)
-                grad_query = part if grad_query is None else grad_query + part
+                added = split_product(grad_scores, keys[start:end], 1, 0)
+                grad_query = added if grad_query is None else grad_query + added
                 if number == rows // block - 1:
                     value_sum[start:end, :] = grad_values
                     key_sum[start:end, :] = grad_keys
@@ -581,14 +636,14 @@
         kernel,
         grid=(heads,),
         in_specs=[
-            pl.BlockSpec((rows, wide), lambda i: (0, i)),
+            pl.BlockSpec((rows, wide), lambda i: (0, part * 2 + i)),
             pl.BlockSpec((rows, HD), lambda i: (0, 0)),
             pl.BlockSpec((rows, HD), lambda i: (0, 0)),
             pl.BlockSpec((1, HD), lambda i: (0, 0)),
             pl.BlockSpec((1, HD), lambda i: (0, 0)),
-            pl.BlockSpec((rows, ratio * HD), lambda i: (0, i)),
-            pl.BlockSpec((rows, HD), lambda i: (0, i)),
-            pl.BlockSpec((rows, ratio * HD), lambda i: (0, i)),
+            pl.BlockSpec((rows, ratio * HD), lambda i: (0, i * parts + part)),
+            pl.BlockSpec((rows, HD), lambda i: (0, part * 2 + i)),
+            pl.BlockSpec((rows, ratio * HD), lambda i: (0, i * parts + part)),
         ],
         out_specs=[
             pl.BlockSpec((rows, wide), lambda i: (0, i)),
@@ -649,6 +704,8 @@
     half = member // 2
     rank = member % 2
     side = copy % 2
+    depth = copies // 2
+    deep = copy // 2
 
     def permute(value, target):
         pairs = []
@@ -664,8 +721,14 @@
     def over_chip(value):
         return permute(value, lambda d, g: (d, g ^ 2))
 
+    def over_diagonal(value):
+        return permute(value, lambda d, g: (d, g ^ 3))
+
     def over_side(value):
         return permute(value, lambda d, g: (d ^ 1, g))
+
+    def over_depth(value, shift):
+        return permute(value, lambda d, g: ((d // 2 + shift) % depth * 2 + d % 2, g))
 
     def block_of(far, other_rank):
         at = half if not far else 1 - half
@@ -674,7 +737,14 @@
     def pick(array, index):
         return lax.dynamic_index_in_dim(array, index, 0, keepdims=False)
 
-    gains = lax.all_gather(gain_weight.astype(bf16), "group", axis=0, tiled=True).astype(f32)
+    def ordered(first_side, mine, theirs):
+        return jnp.concatenate(
+            [jnp.where(first_side, mine, theirs), jnp.where(first_side, theirs, mine)]
+        )
+
+    gain_low = gain_weight.astype(bf16)
+    gain_pair = ordered(rank == 0, gain_low, over_core(gain_low))
+    gains = ordered(half == 0, gain_pair, over_chip(gain_pair)).astype(f32)
     gain_one = gains[:D]
     gain_two = gains[D : 2 * D]
     gain_query = gains[2 * D : 2 * D + HD].reshape(1, HD)
@@ -701,159 +771,229 @@
     peer_targets = jnp.stack(piece_targets(True))
     all_targets = jnp.concatenate([own_targets, peer_targets])
 
-    def whole_sequence(array, far_part):
-        near_part = pick(array, half)
-        mine = jnp.concatenate([near_part, far_part], axis=0)
-        theirs = over_core(mine)
-        return place_rows([mine, theirs], all_targets, chunk)
+    def whole_sequence(array, far_part, gain):
+        mine = jnp.concatenate([pick(array, half), far_part], axis=0)
+        return place_rows(mine, over_core(mine), all_targets, chunk, gain)
+
+    parts = 2
+    wide = (ratio + 2) * HD
+    some = ff // parts
 
     def by_heads(array):
-        lead = array.shape[0]
-        query = array[:, : H * HD].reshape(lead, KV, ratio * HD)
-        keys = array[:, H * HD : (H + KV) * HD].reshape(lead, KV, HD)
-        values = array[:, (H + KV) * HD :].reshape(lead, KV, HD)
-        return jnp.concatenate([query, keys, values], axis=2).reshape(lead, groups, -1)
+        blocks = []
+        for head in range(KV):
+            blocks.append(array[:, head * ratio * HD : (head + 1) * ratio * HD])
+            blocks.append(array[:, (H + head) * HD : (H + head + 1) * HD])
+            blocks.append(array[:, (H + KV + head) * HD : (H + KV + head + 1) * HD])
+        size = 3 * KV // groups
+        return jnp.stack(
+            [
+                jnp.concatenate(blocks[number * size : (number + 1) * size], axis=1)
+                for number in range(groups)
+            ]
+        )
 
     def by_units(array):
-        lead = array.shape[0]
-        gate = array[:, :FF].reshape(lead, groups, ff)
-        up = array[:, FF:].reshape(lead, groups, ff)
-        return jnp.concatenate([gate, up], axis=2)
-
-    def column_blocks(blocked, other_rank):
-        parts = []
-        for far in (False, True):
-            parts.append(
-                lax.dynamic_index_in_dim(blocked, block_of(far, other_rank), 1, keepdims=False)
+        stacked = []
+        for number in range(groups):
+            blocks = []
+            for part in range(parts):
+                low = number * ff + part * some
+                blocks.append(array[:, low : low + some])
+                blocks.append(array[:, FF + low : FF + low + some])
+            stacked.append(jnp.concatenate(blocks, axis=1))
+        return jnp.stack(stacked)
+
+    where_at = jnp.stack([half, rank, side]).astype(jnp.int32)
+
+    class Columns:
+        def __init__(self, blocked):
+            sent_half = jnp.where(side == 0, 1 - half, half)
+            self.to_chip = pick(blocked, sent_half * 2 + rank)
+            self.to_diagonal = pick(blocked, sent_half * 2 + 1 - rank)
+            self.to_core = jnp.stack(
+                [pick(blocked, block_of(False, True)), pick(blocked, block_of(True, True))]
             )
-        return jnp.concatenate(parts, axis=1)
-
-    def chip_columns(blocked):
-        mine = column_blocks(blocked, False)
-        theirs = over_core(column_blocks(blocked, True))
-        lead, cols = mine.shape
-        chip = jnp.zeros((2 * lead, cols), bf16)
-        chip = lax.dynamic_update_slice(chip, mine, (rank * lead, 0))
-        return lax.dynamic_update_slice(chip, theirs, ((1 - rank) * lead, 0))
-
-    def columns_payload(chip):
-        lead, cols = chip.shape
-        return lax.dynamic_slice(chip, (0, (1 - side) * (cols // 2)), (lead, cols // 2))
-
-    def columns_join(chip, from_chip, from_side):
-        lead, cols = chip.shape
-        whole = jnp.zeros((2 * lead, cols), bf16)
-        whole = lax.dynamic_update_slice(whole, chip, (half * lead, 0))
-        whole = lax.dynamic_update_slice(
-            whole, from_chip, ((1 - half) * lead, side * (cols // 2))
-        )
-        return lax.dynamic_update_slice(
-            whole, from_side, ((1 - half) * lead, (1 - side) * (cols // 2))
-        )
-
-    def rows_payload(own):
-        return lax.dynamic_slice_in_dim(own, side * (own.shape[0] // 2), own.shape[0] // 2, 0)
-
-    def rows_join(own, from_chip, from_side):
-        lead, cols = own.shape
-        whole = jnp.zeros((2 * lead, cols), bf16)
-        whole = lax.dynamic_update_slice(whole, own, (0, 0))
-        whole = lax.dynamic_update_slice(whole, from_chip, (lead + side * (lead // 2), 0))
-        return lax.dynamic_update_slice(whole, from_side, (lead + (1 - side) * (lead // 2), 0))
+            self.near = pick(blocked, block_of(False, False))
+            self.far = pick(blocked, block_of(True, False))
+
+        def send(self):
+            self.chip = over_chip(self.to_chip)
+            self.diagonal = over_diagonal(self.to_diagonal)
+            self.peer = over_core(self.to_core)
+            self.chip_side = over_side(self.chip)
+            self.diagonal_side = over_side(self.diagonal)
+
+        def joined(self):
+            return join_columns(
+                self.near, self.far, self.peer, self.chip, self.diagonal,
+                self.chip_side, self.diagonal_side, where_at, parts,
+            )
+
+    class Rows:
+        def __init__(self, own):
+            self.own = own
+            self.payload = pick(own.reshape(2, own.shape[0] // 2, own.shape[1]), side)
+
+        def send(self):
+            self.chip = over_chip(self.payload)
+            self.side = over_side(self.chip)
+
+        def joined(self):
+            return jnp.concatenate([self.own, ordered(side == 0, self.chip, self.side)], axis=0)
 
     hidden_far = over_chip(pick(hidden_in, 1 - half))
-    qkv_chip = chip_columns(by_heads(qkv_weight.astype(bf16)))
-    qkv_y = over_chip(columns_payload(qkv_chip))
-    qkv_x = over_side(qkv_y)
-    out_own = out_weight.astype(bf16)
-    out_y = over_chip(tie(rows_payload(out_own), hidden_far))
-    out_x = over_side(out_y)
-    gateup_chip = chip_columns(by_units(gateup_weight.astype(bf16)))
-    gateup_y = over_chip(tie(columns_payload(gateup_chip), qkv_y))
-    gateup_x = over_side(gateup_y)
-    down_own = down_weight.astype(bf16)
-    down_y = over_chip(tie(rows_payload(down_own), out_y))
-    down_x = over_side(down_y)
-    grad_far = over_chip(tie(pick(out_grad, 1 - half), gateup_y))
-
-    hidden = whole_sequence(hidden_in, hidden_far)
+    qkv = Columns(by_heads(qkv_weight.astype(bf16)))
+    qkv.send()
+    out = Rows(tie(out_weight, qkv.to_chip, qkv.to_diagonal, qkv.to_core).astype(bf16))
+    out.payload = tie(out.payload, hidden_far)
+    out.send()
+    gateup = Columns(by_units(tie(gateup_weight, qkv.to_chip, out.payload).astype(bf16)))
+    gateup.to_chip = tie(gateup.to_chip, qkv.chip)
+    gateup.to_diagonal = tie(gateup.to_diagonal, qkv.diagonal)
+    gateup.send()
+    down = Rows(tie(down_weight, gateup.to_chip, gateup.to_diagonal).astype(bf16))
+    down.payload = tie(down.payload, out.chip, gateup.chip)
+    down.send()
+    grad_far = over_chip(tie(pick(out_grad, 1 - half), gateup.diagonal))
+
+    hidden, normed_low = whole_sequence(hidden_in, hidden_far, gain_one)
     tokens = hidden.astype(f32)
-    normed_low = rms_scale(tokens, gain_one).astype(bf16)
-    w_qkv = columns_join(qkv_chip, qkv_y, qkv_x)
+    w_qkv = qkv.joined()
     mixed = split_product(normed_low, w_qkv, 1, 0)
     block = min(256, seq_len)
     attended, totals = attend_forward(
         mixed, cosine, sine, gain_query, gain_key, heads, ratio, block
     )
-    w_out = rows_join(out_own, out_y, out_x)
+    w_out = out.joined()
     branch = split_product(attended, w_out, 1, 0).astype(bf16)
     middle = tokens + (branch.astype(f32) + over_core(branch).astype(f32))
     second, pull_two = jax.vjp(rms_scale, middle, gain_two)
     second_low = second.astype(bf16)
-    w_gateup = columns_join(gateup_chip, gateup_y, gateup_x)
+    w_gateup = gateup.joined()
     gate_up = split_product(second_low, w_gateup, 1, 0)
 
-    def gated_pairs(values):
+    def gated_part(values, part):
+        pieces_here = []
+        for far in range(2):
+            low = (part * 2 + far) * 2 * some
+            pieces_here.append(
+                jax.nn.silu(values[:, low : low + some]) * values[:, low + some : low + 2 * some]
+            )
+        return pieces_here
+
+    def gated_all(values):
+        found = [gated_part(values, part) for part in range(parts)]
         return jnp.concatenate(
-            [
-                jax.nn.silu(values[:, far * 2 * ff : far * 2 * ff + ff])
-                * values[:, far * 2 * ff + ff : (far + 1) * 2 * ff]
-                for far in range(2)
-            ],
-            axis=1,
+            [found[part][far] for far in range(2) for part in range(parts)], axis=1
         )
 
-    inner, pull_gate = jax.vjp(gated_pairs, gate_up)
+    inner, pull_gate = jax.vjp(gated_all, gate_up)
     inner_low = inner.astype(bf16)
-    grad_result = whole_sequence(out_grad, grad_far)
-
-    def near_far(grad_fn, swapped=False):
-        far = grad_fn(True)
-        from_far = over_chip(far)
-        near = grad_fn(False)
-        if swapped:
-            size = from_far.shape[1] // 2
-            from_far = jnp.concatenate([from_far[:, size:], from_far[:, :size]], axis=1)
-        return (near.astype(f32) + from_far.astype(f32)).astype(bf16)
-
-    def unit_rows(array, far):
+    (grad_result,) = whole_sequence(out_grad, grad_far, None)
+
+    def half_columns(array, far):
+        size = array.shape[1] // 2
+        near_side = half == (1 if far else 0)
+        return jnp.where(near_side, array[:, :size], array[:, size:])
+
+    def far_columns(array, far):
         size = array.shape[1] // 2
         return array[:, size:] if far else array[:, :size]
 
-    def chip_rows(array, far):
+    def far_first(array):
         size = array.shape[1] // 2
-        at = (1 - half) if far else half
-        return lax.dynamic_slice_in_dim(array, at * size, size, 1)
-
-    sum_down = near_far(
-        lambda far: split_product(unit_rows(inner_low, far), grad_result, 0, 0).astype(bf16)
-    )
-    w_down = rows_join(down_own, down_y, down_x)
-    result_part = split_product(inner_low, w_down, 1, 0).astype(bf16)
+        return jnp.concatenate([array[:, size:], array[:, :size]], axis=1)
+
+    def exchange(left_far, left_near, right):
+        far = split_product(left_far, right, 0, 0).astype(bf16)
+        received = over_chip(far)
+        near = split_product(left_near, right, 0, 0).astype(bf16)
+        return near, received
+
+    def add(first, *others):
+        total = first.astype(f32)
+        for other in others:
+            total = total + other.astype(f32)
+        return total.astype(bf16)
+
+    def swap_rows(near, received):
+        received = far_first(received)
+        lead = near.shape[0] // 2
+        near = near.reshape(2, lead, -1)
+        received = received.reshape(2, lead, -1)
+        theirs = add(pick(near, 1 - rank), pick(received, 1 - rank))
+        mine = add(pick(near, rank), pick(received, rank))
+        return jnp.stack([mine, over_core(theirs)])
+
+    def side_sum(value):
+        value = value.reshape(2, depth, -1, value.shape[-1])
+        return add(pick(value, side), over_side(pick(value, 1 - side)))
+
+    def depth_sum(value):
+        received = [
+            over_depth(pick(value, (deep + shift) % depth), shift) for shift in range(1, depth)
+        ]
+        return add(pick(value, deep), *received)
+
+    def depth_gather(value):
+        whole = jnp.zeros((depth, *value.shape), bf16)
+        for shift in range(depth):
+            piece = value if shift == 0 else over_depth(value, shift)
+            whole = lax.dynamic_update_index_in_dim(whole, piece, (deep - shift) % depth, 0)
+        return whole
+
+    def side_gather(value):
+        flat = value.reshape(-1, value.shape[-1])
+        return ordered(side == 0, flat, over_side(flat))
+
+    down_near, down_received = exchange(
+        far_columns(inner_low, True), far_columns(inner_low, False), grad_result
+    )
+    w_down = down.joined()
     grad_inner = split_product(grad_result, w_down, 1, 1)
     (grad_gate_up,) = pull_gate(grad_inner)
     grad_gate_low = grad_gate_up.astype(bf16)
-    sum_gateup = near_far(
-        lambda far: split_product(chip_rows(second_low, far), grad_gate_low, 0, 0).astype(bf16),
-        True,
-    )
+    second_near, second_far = half_columns(second_low, False), half_columns(second_low, True)
+    part_cols = grad_gate_low.shape[1] // parts
+    gateup_sent = [
+        exchange(second_far, second_near, grad_gate_low[:, part * part_cols : (part + 1) * part_cols])
+        for part in range(parts)
+    ]
     second_part = split_product(grad_gate_low, w_gateup, 1, 1).astype(bf16)
     grad_second = second_part.astype(f32) + over_core(second_part).astype(f32)
+    result_part = split_product(inner_low, w_down, 1, 0).astype(bf16)
     grad_mid_part, grad_gain_two = pull_two(grad_second)
     grad_middle = grad_result.astype(f32) + grad_mid_part
     grad_branch_low = grad_middle.astype(bf16)
-    sum_out = near_far(
-        lambda far: split_product(unit_rows(attended, far), grad_branch_low, 0, 0).astype(bf16)
+    out_near, out_received = exchange(
+        far_columns(attended, True), far_columns(attended, False), grad_branch_low
     )
     grad_att = split_product(grad_branch_low, w_out, 1, 1).astype(bf16)
-    grad_mixed_low, grad_gain_query, grad_gain_key = attend_backward(
-        mixed, cosine, sine, gain_query, gain_key, attended, totals, grad_att, heads, ratio, block
-    )
-    sum_qkv = near_far(
-        lambda far: split_product(chip_rows(normed_low, far), grad_mixed_low, 0, 0).astype(bf16),
-        True,
-    )
-    normed_part = split_product(grad_mixed_low, w_qkv, 1, 1).astype(bf16)
+    normed_near, normed_far = half_columns(normed_low, False), half_columns(normed_low, True)
+    grad_parts = []
+    qkv_sent = []
+    gain_parts = []
+    for part in range(parts):
+        grad_part, grad_query_part, grad_key_part = attend_backward(
+            mixed, cosine, sine, gain_query, gain_key, attended, totals, grad_att,
+            part, parts, ratio, block,
+        )
+        grad_parts.append(grad_part)
+        gain_parts.append((grad_query_part[0], grad_key_part[0]))
+        qkv_sent.append(exchange(normed_far, normed_near, grad_part))
+    normed_part = sum(
+        split_product(grad_parts[part], w_qkv[:, part * 2 * wide : (part + 1) * 2 * wide], 1, 1)
+        for part in range(parts)
+    ).astype(bf16)
+
+    down_sum = side_sum(add(down_near, tie(down_received, grad_att)))
+    down_sum = depth_sum(tie(down_sum, grad_parts[0]))
+    down_sum = side_gather(depth_gather(tie(down_sum, grad_parts[1])))
+    gateup_swapped = []
+    for part in range(parts):
+        near, received = gateup_sent[part]
+        gateup_swapped.append(swap_rows(near, tie(received, grad_parts[part])))
 
     def share_rows(part):
         return take_rows(part, own_targets, chunk).astype(f32) + over_core(
@@ -874,62 +1014,35 @@
     grad_token_part, grad_gain_one = pull_one(grad_normed)
     input_grad = to_stored(take_rows(grad_middle, own_targets, chunk) + grad_token_part)
 
-    def swap_rows(chip_sum):
-        lead = chip_sum.shape[0] // 2
-        mine = lax.dynamic_slice_in_dim(chip_sum, rank * lead, lead, 0)
-        theirs = lax.dynamic_slice_in_dim(chip_sum, (1 - rank) * lead, lead, 0)
-        return jnp.concatenate([mine, over_core(theirs)], axis=0)
-
-    bits = []
-    step = 1
-    while step < copies:
-        bits.append(step)
-        step *= 2
-
-    def dp_sum(value):
-        for bit in bits:
-            size = value.shape[0] // 2
-            at = (copy // bit) % 2
-            sent = lax.dynamic_slice_in_dim(value, (1 - at) * size, size, 0)
-            kept = lax.dynamic_slice_in_dim(value, at * size, size, 0)
-            received = permute(sent, lambda d, g: (d ^ bit, g))
-            value = (kept.astype(f32) + received.astype(f32)).astype(bf16)
-        for bit in reversed(bits):
-            size = value.shape[0]
-            at = (copy // bit) % 2
-            received = permute(value, lambda d, g: (d ^ bit, g))
-            whole = jnp.zeros((2 * size, value.shape[1]), bf16)
-            whole = lax.dynamic_update_slice(whole, value, (at * size, 0))
-            value = lax.dynamic_update_slice(whole, received, ((1 - at) * size, 0))
-        return value
-
-    total_down = dp_sum(sum_down).astype(f32)
-    total_gateup = dp_sum(swap_rows(sum_gateup))
-    total_out = dp_sum(sum_out).astype(f32)
-    total_qkv = dp_sum(swap_rows(sum_qkv))
-
-    def owner_blocks(total):
-        lead = total.shape[0] // 2
-        cols = total.shape[1] // 2
+    def rest_of_sum(value):
+        return side_gather(depth_gather(depth_sum(side_sum(value))))
+
+    gateup_sums = [rest_of_sum(value) for value in gateup_swapped]
+    out_sum = rest_of_sum(add(out_near, out_received))
+    qkv_sums = [rest_of_sum(swap_rows(*sent)) for sent in qkv_sent]
+    total_down = down_sum.astype(f32)
+    total_out = out_sum.astype(f32)
+
+    def owner_blocks(totals_of_parts):
         blocks = []
         for block_number in range(groups):
             far = (block_number // 2) ^ half
             peer = (block_number % 2) ^ rank
-            blocks.append(lax.dynamic_slice(total, (peer * lead, far * cols), (lead, cols)))
+            for total in totals_of_parts:
+                lead = total.shape[0] // 2
+                cols = total.shape[1] // 2
+                stacked = total.reshape(2, lead, 2 * cols)
+                rows_here = pick(stacked, peer)
+                blocks.append(jnp.where(far == 0, rows_here[:, :cols], rows_here[:, cols:]))
         return blocks
 
-    gateup_blocks = owner_blocks(total_gateup)
+    gateup_blocks = owner_blocks(gateup_sums)
     total_gateup = jnp.concatenate(
-        [blocked[:, :ff] for blocked in gateup_blocks]
-        + [blocked[:, ff:] for blocked in gateup_blocks],
+        [blocked[:, :some] for blocked in gateup_blocks]
+        + [blocked[:, some:] for blocked in gateup_blocks],
         axis=1,
     ).astype(f32)
-    wide = (ratio + 2) * HD
-    head_blocks = [
-        blocked[:, number * wide : (number + 1) * wide]
-        for blocked in owner_blocks(total_qkv)
-        for number in range(blocked.shape[1] // wide)
-    ]
+    head_blocks = owner_blocks(qkv_sums)
     total_qkv = jnp.concatenate(
         [blocked[:, : ratio * HD] for blocked in head_blocks]
         + [blocked[:, ratio * HD : (ratio + 1) * HD] for blocked in head_blocks]
@@ -937,10 +1050,18 @@
         axis=1,
     ).astype(f32)
     counted = jnp.where(rank == 0, 1.0, 0.0).astype(f32)
-    grad_gains = jnp.concatenate(
-        [grad_gain_one, grad_gain_two * counted, grad_gain_query[0], grad_gain_key[0]]
-    )
-    total_gains = lax.psum(grad_gains, ALL)
+    total_gains = jnp.concatenate(
+        [
+            grad_gain_one,
+            grad_gain_two * counted,
+            sum(pair[0] for pair in gain_parts),
+            sum(pair[1] for pair in gain_parts),
+        ]
+    )
+    total_gains = total_gains + over_core(total_gains)
+    total_gains = total_gains + over_chip(total_gains)
+    total_gains = total_gains + over_side(total_gains)
+    total_gains = total_gains + sum(over_depth(total_gains, shift) for shift in range(1, depth))
     gain_rows = gain_weight.shape[0]
     total_gain = lax.dynamic_slice_in_dim(total_gains, member * gain_rows, gain_rows, 0)
 
@@ -963,7 +1084,7 @@
     groups = lax.axis_size("group")
     copies = lax.axis_size("dp")
     two_ranks = hidden_in.shape[0] == 2 and groups == 4
-    if two_ranks and copies % 2 == 0 and copies & (copies - 1) == 0:
+    if two_ranks and copies % 2 == 0:
         return paired_shards(hidden_in, *others)
     return general_shards(hidden_in, *others)
 

time: 913 us -> 690 us (0.76)
  Pallas kernels: 188 us -> 82.7 us
  local copies, waits for them, and re-layouts: 128 us -> 50.7 us
  blocking collectives: 73.4 us -> 0 us
  starting transfers between devices: 60.2 us -> 115 us
  matrix products: 91 us -> 80.7 us
  waiting for transfers between devices: 262 us -> 252 us
    pallas_call x2 -> x4, Pallas kernels: 131 us -> 23.9 us  [the longest x2 13.5 us: place_rows(): pl.pallas_call(kernel, out_shape=[shape] * outputs, grid_spec=pltpu.Prefe...]
    dynamic_update_slice x34 -> x19, local copies, waits for them, and re-layouts: 70.6 us -> 4.19 us  [depth_gather(): lax.dynamic_update_index_in_dim(whole, piece, (deep - shift) % depth, 0)]
    psum x1 -> x0, blocking collectives: 59.9 us -> none  [paired_shards(): total_gains = lax.psum(grad_gains, ALL)]
    ppermute x50 -> x90, starting transfers between devices: 60.2 us -> 115 us  [permute(): return lax.ppermute(value, ALL, pairs)]
    unnamed x1 -> x0, blocking collectives: 13.5 us -> none
    dynamic_slice x21 -> x0, local copies, waits for them, and re-layouts: 12 us -> none  [the longest x2 3.5 us: swap_rows(): theirs = lax.dynamic_slice_in_dim(chip_sum, (1 - rank) * lead, lead, 0)]
    ppermute x50 -> x90, waiting for transfers between devices: 262 us -> 252 us  [permute(): return lax.ppermute(value, ALL, pairs)]
    dot_general x16 -> x21, matrix products: 91 us -> 80.7 us  [split_product(): lax.dot_general(left, right, (((left_dim,), (right_dim,)), ((), ())), pre...]
  transfers between devices with their start and end apart: 50 -> 90, of which waited for: 24 -> 38; matrix products, arithmetic and copies ran while one was open for 28% -> 22% of each run, Pallas kernels for 13% -> 12%
where the time goes in v2:
time: 690 us; the launch traced here: 686 us
  waiting for transfers between devices  252 us (37%)
  starting transfers between devices  115 us (17%)
  other arithmetic  96.3 us (14%)
  Pallas kernels  82.7 us (12%)
  matrix products  80.7 us (12%)
  local copies, waits for them, and re-layouts  50.7 us (7%)
  between operations  9.49 us (1%)
    ppermute x90, waiting for transfers between devices, permute(): return lax.ppermute(value, ALL, pairs)  252 us
    ppermute x90, starting transfers between devices, permute(): return lax.ppermute(value, ALL, pairs)  115 us
    dot_general x21, matrix products, split_product(): lax.dot_general(left, right, (((left_dim,), (right_dim,)), ((), ())), pre...  80.7 us
    pallas_call x2, Pallas kernels, attend_backward(): pl.pallas_call(kernel, grid=(heads,), in_specs=[pl.BlockSpec((rows, wide)...  36.3 us
    sub x5, other arithmetic, adam_step(): return (weight - rate * (ratio + decay * weight), moment_new, square_new)  25.1 us
    pallas_call x1, Pallas kernels, attend_forward(): pl.pallas_call(kernel, grid=(heads,), in_specs=[pl.BlockSpec((rows, wide)...  22.6 us
    unnamed x189, local copies, waits for them, and re-layouts  18.3 us
  transfers between devices with their start and end apart: 90, of which 38 were waited for; matrix products, arithmetic and copies ran while one was open for 22% of the time, Pallas kernels for 12%

profile of v2, /device:TPU:0, one launch (start us, length us, event | category | flops | bytes accessed | tf_op | source)
XLA Modules:
  0.0 686.4 jit_solution(1807024389698684354)
XLA Ops:
  33.1 5.6 concatenate.125.targets_ref
  59.4 9.6 %collective-permute-done.7.chip_x_ref = bf16[256,1024]{1,0:T(8,128)(2,1)S(1)} collective-permute-done((bf16[256,1024]{1,0:T(8,128)(2,1)S(1)}, bf16[256,1024]{1,0:T(8,128)(2,1)S(1)}, u32[]{:S(2)}, u32[]{:S(2)}) %collective-permute-start.7) | collective-permute-done | bytes 524320 | tf_op jit(solution)/shard_map/ppermute | solution.py:716
  69.0 8.9 %collective-permute-done.8.diag_x_ref = bf16[256,1024]{1,0:T(8,128)(2,1)S(1)} collective-permute-done((bf16[256,1024]{1,0:T(8,128)(2,1)}, bf16[256,1024]{1,0:T(8,128)(2,1)S(1)}, u32[]{:S(2)}, u32[]{:S(2)}) %collective-permute-start.8) | collective-permute-done | bytes 524320 | tf_op jit(solution)/shard_map/ppermute | solution.py:716
  89.0 7.0 %place_rows.2 = (bf16[1024,1024]{1,0:T(8,128)(2,1)}, bf16[1024,1024]{1,0:T(8,128)(2,1)}) custom-call(s32[8]{0:T(128)} %concatenate.125.targets_ref, bf16[512,1024]{1,0:T(8,128)(2,1)} %copy-done.31, bf16[512,1024]{1,0:T(8,128)(2,1)} %copy-done.51, f32[1,1024]{1,0:T(1,128)} %bitcast.343), custom_call_target="tpu_custom_call" | custom-call | bytes 8388608 | tf_op jit(solution)/shard_map/place_rows/pallas_call | solution.py:374
  96.0 10.6 %fusion.138.mixed_ref = f32[1024,2048]{1,0:T(8,128)} fusion(bf16[1024,1024]{1,0:T(8,128)(2,1)} %get-tuple-element.41, bf16[1024,2048]{1,0:T(8,128)(2,1)} %join_columns.2), kind=kOutput, calls=%fused_computation.478 | convolution fusion | flops 4294967296 | bytes 14680064 | tf_op jit(solution)/shard_map/dot_general | solution.py:338
  107.9 22.6 %attend_forward.1 = (bf16[1024,1024]{1,0:T(8,128)(2,1)S(1)}, f32[1024,512]{1,0:T(8,128)S(1)}) custom-call(f32[1024,2048]{1,0:T(8,128)} %fusion.138.mixed_ref, f32[1024,128]{1,0:T(8,128)S(1)} %pad_maximum_fusion.28.cos_ref, f32[1024,128]{1,0:T(8,128)S(1)} %pad_maximum_fusion.29.sin_ref, f32[1,128]{1,0:T(1,128)S(1)} %get-tuple-element.269.gq_ref, ...), custom_call_target="tpu_custom_call" | custom-call | flops 2684354560 | bytes 12582912 | tf_op jit(solution)/shard_map/attend_forward/pallas_call | solution.py:510
  149.7 6.7 collective-permute-done.15.chip_x_ref
  156.4 16.9 %collective-permute-done.16.diag_x_ref = bf16[256,1536]{1,0:T(8,128)(2,1)} collective-permute-done((bf16[256,1536]{1,0:T(8,128)(2,1)}, bf16[256,1536]{1,0:T(8,128)(2,1)}, u32[]{:S(2)}, u32[]{:S(2)}) %collective-permute-start.16) | collective-permute-done | bytes 786464 | tf_op jit(solution)/shard_map/ppermute | solution.py:716
  173.3 5.9 join_columns.3
  179.2 9.9 %collective-permute-done.18 = bf16[384,1024]{1,0:T(8,128)(2,1)} collective-permute-done((bf16[384,1024]{1,0:T(8,128)(2,1)}, bf16[384,1024]{1,0:T(8,128)(2,1)}, u32[]{:S(2)}, u32[]{:S(2)}) %collective-permute-start.18) | collective-permute-done | bytes 786464 | tf_op jit(solution)/shard_map/ppermute | solution.py:716
  191.8 6.5 place_rows.3
  198.2 6.2 fusion.60
  204.5 5.5 multiply_reduce_fusion.2
  210.4 9.5 %fusion.139 = f32[1024,3072]{1,0:T(8,128)S(1)} fusion(bf16[1024,1024]{1,0:T(8,128)(2,1)S(1)} %multiply_convert_fusion, bf16[1024,3072]{1,0:T(8,128)(2,1)} %join_columns.3), kind=kOutput, calls=%fused_computation.479 | convolution fusion | flops 6442450944 | bytes 20971520 | tf_op jit(solution)/shard_map/dot_general | solution.py:338
  223.0 7.2 %slice_multiply_fusion.3 = (f32[1024,384]{1,0:T(8,128)}, f32[1024,384]{1,0:T(8,128)}, f32[1024,384]{1,0:T(8,128)}, f32[1024,384]{1,0:T(8,128)}, f32[1024,384]{1,...) fusion(f32[1024,1536]{1,0:T(8,128)} %copy-done.8, f32[1024,3072]{1,0:T(8,128)S(1)} %fusion.139), kind=kLoop, calls=%fused_computation.141 | loop fusion | flops 18087936 | bytes 29884416 | tf_op jit(solution)/shard_map/transpose(jvp())/mul | solution.py:881
  244.7 11.5 %convolution_convert_fusion.6 = bf16[1024,1024]{1,0:T(8,128)(2,1)S(1)} fusion(bf16[1024,3072]{1,0:T(8,128)(2,1)} %add_convert_fusion, bf16[1024,3072]{1,0:T(8,128)(2,1)} %join_columns.3), kind=kOutput, calls=%fused_computation.79 | convolution fusion | flops 6443499520 | bytes 14680064 | tf_op jit(solution)/shard_map/dot_general | solution.py:338
  280.5 17.7 %attend_backward.2 = (bf16[1024,1024]{1,0:T(8,128)(2,1)S(1)}, f32[1,128]{1,0:T(1,128)S(1)}, f32[1,128]{1,0:T(1,128)S(1)}) custom-call(f32[1024,2048]{1,0:T(8,128)} %fusion.138.mixed_ref, f32[1024,128]{1,0:T(8,128)S(1)} %pad_maximum_fusion.28.cos_ref, f32[1024,128]{1,0:T(8,128)S(1)} %pad_maximum_fusion.29.sin_ref, f32[1,128]{1,0:T(1,128)S(1)} %get-tuple-element.269.gq_ref, ...), custom_call_target="tpu_custom_call" | custom-call | flops 3355443200 | bytes 9437184 | tf_op jit(solution)/shard_map/attend_backward/pallas_call | solution.py:635
  298.2 18.6 %attend_backward.3 = (bf16[1024,1024]{1,0:T(8,128)(2,1)S(1)}, f32[1,128]{1,0:T(1,128)S(1)}, f32[1,128]{1,0:T(1,128)S(1)}) custom-call(f32[1024,2048]{1,0:T(8,128)} %fusion.138.mixed_ref, f32[1024,128]{1,0:T(8,128)S(1)} %pad_maximum_fusion.28.cos_ref, f32[1024,128]{1,0:T(8,128)S(1)} %pad_maximum_fusion.29.sin_ref, f32[1,128]{1,0:T(1,128)S(1)} %get-tuple-element.269.gq_ref, ...), custom_call_target="tpu_custom_call" | custom-call | flops 3355443200 | bytes 9437184 | tf_op jit(solution)/shard_map/attend_backward/pallas_call | solution.py:635
  343.2 24.2 %collective-permute-done.55 = bf16[512,1536]{1,0:T(8,128)(2,1)} collective-permute-done((bf16[512,1536]{1,0:T(8,128)(2,1)}, bf16[512,1536]{1,0:T(8,128)(2,1)}, u32[]{:S(2)}, u32[]{:S(2)}) %collective-permute-start.55) | collective-permute-done | bytes 1572896 | tf_op jit(solution)/shard_map/ppermute | solution.py:716
  383.5 6.2 collective-permute-done.78
  397.1 55.5 %collective-permute-done.26 = bf16[512,1024]{1,0:T(8,128)(2,1)S(1)} collective-permute-done((bf16[512,1024]{1,0:T(8,128)(2,1)S(1)}, bf16[512,1024]{1,0:T(8,128)(2,1)S(1)}, u32[]{:S(2)}, u32[]{:S(2)}) %collective-permute-start.26) | collective-permute-done | bytes 1048608 | tf_op jit(solution)/shard_map/ppermute | solution.py:716
  487.2 12.0 %collective-permute-done.47 = bf16[4,64,1024]{2,1,0:T(8,128)(2,1)S(1)} collective-permute-done((bf16[4,64,1024]{2,1,0:T(8,128)(2,1)S(1)}, bf16[4,64,1024]{2,1,0:T(8,128)(2,1)S(1)}, u32[]{:S(2)}, u32[]{:S(2)}) %collective-permute-start.47) | collective-permute-done | bytes 524320 | tf_op jit(solution)/shard_map/ppermute | solution.py:716
  509.0 7.0 %collective-permute-done.57 = bf16[4,64,1536]{2,1,0:T(8,128)(2,1)S(1)} collective-permute-done((bf16[4,64,1536]{2,1,0:T(8,128)(2,1)S(1)}, bf16[4,64,1536]{2,1,0:T(8,128)(2,1)S(1)}, u32[]{:S(2)}, u32[]{:S(2)}) %collective-permute-start.57) | collective-permute-done | bytes 786464 | tf_op jit(solution)/shard_map/ppermute | solution.py:716
  523.2 5.1 collective-permute-done.68
  531.4 5.6 collective-permute-done.69
  537.1 5.1 collective-permute-start.60
  542.9 6.5 collective-permute-done.59
  575.5 12.0 %collective-permute-done.72 = bf16[64,1536]{1,0:T(8,128)(2,1)S(1)} collective-permute-done((bf16[64,1536]{1,0:T(8,128)(2,1)S(1)}, bf16[64,1536]{1,0:T(8,128)(2,1)S(1)}, u32[]{:S(2)}, u32[]{:S(2)}) %collective-permute-start.72) | collective-permute-done | bytes 196640 | tf_op jit(solution)/shard_map/ppermute | solution.py:716
  588.8 9.3 %collective-permute-done.62 = bf16[64,1536]{1,0:T(8,128)(2,1)S(1)} collective-permute-done((bf16[64,1536]{1,0:T(8,128)(2,1)S(1)}, bf16[64,1536]{1,0:T(8,128)(2,1)S(1)}, u32[]{:S(2)}, u32[]{:S(2)}) %collective-permute-start.62) | collective-permute-done | bytes 196640 | tf_op jit(solution)/shard_map/ppermute | solution.py:716
  608.8 5.0 collective-permute-done.40
  662.7 10.3 %multiply_subtract_fusion = (f32[256,6144]{1,0:T(8,128)}, f32[256,6144]{1,0:T(8,128)}, f32[256,6144]{1,0:T(8,128)}) fusion(f32[256,6144]{1,0:T(8,128)S(1)} %bitcast.298, bf16[256,6144]{1,0:T(8,128)(2,1)S(1)} %slice_dynamic-update-slice_fusion, f32[256,6144]{1,0:T(8,128)S(1)} %bitcast.304, f32[256,6144]{1,0:T(8,128)} %param.31), kind=kLoop, calls=%fused_computation.5 | loop fusion | flops 25165824 | bytes 40894464 | tf_op jit(solution)/shard_map/sub | solution.py:93
  680.4 5.8 multiply_subtract_fusion.1
  (529 shorter events, 320.9 us)
Async XLA Ops:
  2.9 36.2 %collective-permute-start = (bf16[256,1024]{1,0:T(8,128)(2,1)}, bf16[256,1024]{1,0:T(8,128)(2,1)}, u32[]{:S(2)}, u32[]{:S(2)}) collective-permute-start(bf16[256,1024]{1,0:T(8,128)(2,1)} %get-tuple-element.233), channel_id=1, source_target_pairs={{0,2},{1,3},{2,0},{3,1},{4,6},{5,7},{6,4},{7,5},{8,10},{9,11},{10,... | collective-permute-start | bytes 1572872 | tf_op jit(solution)/shard_map/ppermute | solution.py:716
  15.6 31.4 %collective-permute-start.5 = (bf16[256,1024]{1,0:T(8,128)(2,1)}, bf16[256,1024]{1,0:T(8,128)(2,1)S(1)}, u32[]{:S(2)}, u32[]{:S(2)}) collective-permute-start(bf16[256,1024]{1,0:T(8,128)(2,1)} %get-tuple-element.165), channel_id=1, source_target_pairs={{0,2},{1,3},{2,0},{3,1},{4,6},{5,7},{6,4},{7,5},{8,10},{9,11},{10,... | collective-permute-start | bytes 1572872 | tf_op jit(solution)/shard_map/ppermute | solution.py:716
  15.6 33.2 %collective-permute-start.6 = (bf16[256,1024]{1,0:T(8,128)(2,1)}, bf16[256,1024]{1,0:T(8,128)(2,1)}, u32[]{:S(2)}, u32[]{:S(2)}) collective-permute-start(bf16[256,1024]{1,0:T(8,128)(2,1)} %get-tuple-element.164), channel_id=1, source_target_pairs={{0,3},{1,2},{2,1},{3,0},{4,7},{5,6},{6,5},{7,4},{8,11},{9,10},{10,... | collective-permute-start | bytes 1572872 | tf_op jit(solution)/shard_map/ppermute | solution.py:716
  17.6 38.3 %collective-permute-start.4 = (bf16[2,256,1024]{2,1,0:T(8,128)(2,1)}, bf16[2,256,1024]{2,1,0:T(8,128)(2,1)}, u32[]{:S(2)}, u32[]{:S(2)}) collective-permute-start(bf16[2,256,1024]{2,1,0:T(8,128)(2,1)} %pad_maximum_fusion.13), channel_id=1, source_target_pairs={{0,1},{1,0},{2,3},{3,2},{4,5},{5,4},{6,7},{7,6},{8,9},{9,8},{10,11... | collective-permute-start | bytes 3145736 | tf_op jit(solution)/shard_map/ppermute | solution.py:716
  47.0 41.0 %collective-permute-start.1 = (bf16[512,1024]{1,0:T(8,128)(2,1)S(1)}, bf16[512,1024]{1,0:T(8,128)(2,1)S(1)}, u32[]{:S(2)}, u32[]{:S(2)}) collective-permute-start(bf16[512,1024]{1,0:T(8,128)(2,1)S(1)} %pad_maximum_fusion.12.mine_ref), channel_id=1, source_target_pairs={{0,1},{1,0},{2,3},{3,2},{4,5},{5,4},{6,7},{7,6},{8,9},{9,8},{10,11... | collective-permute-start | bytes 3145736 | tf_op jit(solution)/shard_map/ppermute | solution.py:716
  48.8 35.2 %collective-permute-start.13 = (bf16[256,1536]{1,0:T(8,128)(2,1)S(1)}, bf16[256,1536]{1,0:T(8,128)(2,1)}, u32[]{:S(2)}, u32[]{:S(2)}) collective-permute-start(bf16[256,1536]{1,0:T(8,128)(2,1)S(1)} %get-tuple-element.46), channel_id=1, source_target_pairs={{0,2},{1,3},{2,0},{3,1},{4,6},{5,7},{6,4},{7,5},{8,10},{9,11},{10,... | collective-permute-start | bytes 2359304 | tf_op jit(solution)/shard_map/ppermute | solution.py:716
  49.2 37.8 %collective-permute-start.14 = (bf16[256,1536]{1,0:T(8,128)(2,1)S(1)}, bf16[256,1536]{1,0:T(8,128)(2,1)}, u32[]{:S(2)}, u32[]{:S(2)}) collective-permute-start(bf16[256,1536]{1,0:T(8,128)(2,1)S(1)} %get-tuple-element.47), channel_id=1, source_target_pairs={{0,3},{1,2},{2,1},{3,0},{4,7},{5,6},{6,5},{7,4},{8,11},{9,10},{10,... | collective-permute-start | bytes 2359304 | tf_op jit(solution)/shard_map/ppermute | solution.py:716
  69.0 72.3 %collective-permute-start.12 = (bf16[2,256,1536]{2,1,0:T(8,128)(2,1)}, bf16[2,256,1536]{2,1,0:T(8,128)(2,1)}, u32[]{:S(2)}, u32[]{:S(2)}) collective-permute-start(bf16[2,256,1536]{2,1,0:T(8,128)(2,1)} %pad_maximum_fusion.4), channel_id=1, source_target_pairs={{0,1},{1,0},{2,3},{3,2},{4,5},{5,4},{6,7},{7,6},{8,9},{9,8},{10,11... | collective-permute-start | bytes 4718600 | tf_op jit(solution)/shard_map/ppermute | solution.py:716
  84.0 53.7 %collective-permute-start.17 = (bf16[384,1024]{1,0:T(8,128)(2,1)}, bf16[384,1024]{1,0:T(8,128)(2,1)}, u32[]{:S(2)}, u32[]{:S(2)}) collective-permute-start(bf16[384,1024]{1,0:T(8,128)(2,1)} %dynamic-slice_bitcast_fusion.5), channel_id=1, source_target_pairs={{0,2},{1,3},{2,0},{3,1},{4,6},{5,7},{6,4},{7,5},{8,10},{9,11},{10,... | collective-permute-start | bytes 2359304 | tf_op jit(solution)/shard_map/ppermute | solution.py:716
  87.0 50.2 %collective-permute-start.21 = (bf16[256,1024]{1,0:T(8,128)(2,1)}, bf16[256,1024]{1,0:T(8,128)(2,1)}, u32[]{:S(2)}, u32[]{:S(2)}) collective-permute-start(bf16[256,1024]{1,0:T(8,128)(2,1)} %get-tuple-element.50), channel_id=1, source_target_pairs={{0,2},{1,3},{2,0},{3,1},{4,6},{5,7},{6,4},{7,5},{8,10},{9,11},{10,... | collective-permute-start | bytes 1572872 | tf_op jit(solution)/shard_map/ppermute | solution.py:716
  134.3 70.2 %collective-permute-start.11 = (bf16[1024,1024]{1,0:T(8,128)(2,1)}, bf16[1024,1024]{1,0:T(8,128)(2,1)}, u32[]{:S(2)}, u32[]{:S(2)}) collective-permute-start(bf16[1024,1024]{1,0:T(8,128)(2,1)} %convolution_convert_fusion.5), channel_id=1, source_target_pairs={{0,1},{1,0},{2,3},{3,2},{4,5},{5,4},{6,7},{7,6},{8,9},{9,8},{10,11... | collective-permute-start | bytes 6291464 | tf_op jit(solution)/shard_map/ppermute | solution.py:716
  137.2 36.1 %collective-permute-start.16 = (bf16[256,1536]{1,0:T(8,128)(2,1)}, bf16[256,1536]{1,0:T(8,128)(2,1)}, u32[]{:S(2)}, u32[]{:S(2)}) collective-permute-start(bf16[256,1536]{1,0:T(8,128)(2,1)} %collective-permute-done.14.diag_ref), channel_id=1, source_target_pairs={{0,4},{1,5},{2,6},{3,7},{4,0},{5,1},{6,2},{7,3},{8,12},{9,13},{10,... | collective-permute-start | bytes 2359304 | tf_op jit(solution)/shard_map/ppermute | solution.py:716
  137.7 51.4 %collective-permute-start.18 = (bf16[384,1024]{1,0:T(8,128)(2,1)}, bf16[384,1024]{1,0:T(8,128)(2,1)}, u32[]{:S(2)}, u32[]{:S(2)}) collective-permute-start(bf16[384,1024]{1,0:T(8,128)(2,1)} %collective-permute-done.17), channel_id=1, source_target_pairs={{0,4},{1,5},{2,6},{3,7},{4,0},{5,1},{6,2},{7,3},{8,12},{9,13},{10,... | collective-permute-start | bytes 2359304 | tf_op jit(solution)/shard_map/ppermute | solution.py:716
  141.3 50.4 %collective-permute-start.22 = (bf16[512,1024]{1,0:T(8,128)(2,1)}, bf16[512,1024]{1,0:T(8,128)(2,1)}, u32[]{:S(2)}, u32[]{:S(2)}) collective-permute-start(bf16[512,1024]{1,0:T(8,128)(2,1)} %pad_maximum_fusion.16.mine_ref), channel_id=1, source_target_pairs={{0,1},{1,0},{2,3},{3,2},{4,5},{5,4},{6,7},{7,6},{8,9},{9,8},{10,11... | collective-permute-start | bytes 3145736 | tf_op jit(solution)/shard_map/ppermute | solution.py:716
  263.3 58.7 %collective-permute-start.75 = (bf16[768,1024]{1,0:T(8,128)(2,1)}, bf16[768,1024]{1,0:T(8,128)(2,1)}, u32[]{:S(2)}, u32[]{:S(2)}) collective-permute-start(bf16[768,1024]{1,0:T(8,128)(2,1)} %convolution_convert_fusion.7), channel_id=1, source_target_pairs={{0,2},{1,3},{2,0},{3,1},{4,6},{5,7},{6,4},{7,5},{8,10},{9,11},{10,... | collective-permute-start | bytes 4718600 | tf_op jit(solution)/shard_map/ppermute | solution.py:716
  263.7 71.0 %collective-permute-start.65 = (bf16[512,1536]{1,0:T(8,128)(2,1)}, bf16[512,1536]{1,0:T(8,128)(2,1)}, u32[]{:S(2)}, u32[]{:S(2)}) collective-permute-start(bf16[512,1536]{1,0:T(8,128)(2,1)} %convolution_convert_fusion), channel_id=1, source_target_pairs={{0,2},{1,3},{2,0},{3,1},{4,6},{5,7},{6,4},{7,5},{8,10},{9,11},{10,... | collective-permute-start | bytes 4718600 | tf_op jit(solution)/shard_map/ppermute | solution.py:716
  265.4 102.0 %collective-permute-start.55 = (bf16[512,1536]{1,0:T(8,128)(2,1)}, bf16[512,1536]{1,0:T(8,128)(2,1)}, u32[]{:S(2)}, u32[]{:S(2)}) collective-permute-start(bf16[512,1536]{1,0:T(8,128)(2,1)} %convolution_convert_fusion.2), channel_id=1, source_target_pairs={{0,2},{1,3},{2,0},{3,1},{4,6},{5,7},{6,4},{7,5},{8,10},{9,11},{10,... | collective-permute-start | bytes 4718600 | tf_op jit(solution)/shard_map/ppermute | solution.py:716
  321.9 70.1 %collective-permute-start.24 = (bf16[512,1024]{1,0:T(8,128)(2,1)S(1)}, bf16[512,1024]{1,0:T(8,128)(2,1)S(1)}, u32[]{:S(2)}, u32[]{:S(2)}) collective-permute-start(bf16[512,1024]{1,0:T(8,128)(2,1)S(1)} %pad_maximum_fusion.18), channel_id=1, source_target_pairs={{0,1},{1,0},{2,3},{3,2},{4,5},{5,4},{6,7},{7,6},{8,9},{9,8},{10,11... | collective-permute-start | bytes 3145736 | tf_op jit(solution)/shard_map/ppermute | solution.py:716
  325.4 46.4 %collective-permute-start.76 = (bf16[4,96,1024]{2,1,0:T(8,128)(2,1)S(1)}, bf16[4,96,1024]{2,1,0:T(8,128)(2,1)S(1)}, u32[]{:S(2)}, u32[]{:S(2)}) collective-permute-start(bf16[4,96,1024]{2,1,0:T(8,128)(2,1)S(1)} %dynamic-slice_bitcast_fusion), channel_id=1, source_target_pairs={{0,4},{1,5},{2,6},{3,7},{4,0},{5,1},{6,2},{7,3},{8,12},{9,13},{10,... | collective-permute-start | bytes 2359304 | tf_op jit(solution)/shard_map/ppermute | solution.py:716
  337.9 36.0 %collective-permute-start.66 = (bf16[256,1536]{1,0:T(8,128)(2,1)S(1)}, bf16[256,1536]{1,0:T(8,128)(2,1)S(1)}, u32[]{:S(2)}, u32[]{:S(2)}) collective-permute-start(bf16[256,1536]{1,0:T(8,128)(2,1)S(1)} %get-tuple-element.114), channel_id=1, source_target_pairs={{0,1},{1,0},{2,3},{3,2},{4,5},{5,4},{6,7},{7,6},{8,9},{9,8},{10,11... | collective-permute-start | bytes 2359304 | tf_op jit(solution)/shard_map/ppermute | solution.py:716
  381.8 117.6 %collective-permute-start.20 = (bf16[256,1024]{1,0:T(8,128)(2,1)S(1)}, bf16[256,1024]{1,0:T(8,128)(2,1)S(1)}, u32[]{:S(2)}, u32[]{:S(2)}) collective-permute-start(bf16[256,1024]{1,0:T(8,128)(2,1)S(1)} %copy-done.58), channel_id=1, source_target_pairs={{0,2},{1,3},{2,0},{3,1},{4,6},{5,7},{6,4},{7,5},{8,10},{9,11},{10,... | collective-permute-start | bytes 1572872 | tf_op jit(solution)/shard_map/ppermute | solution.py:716
  389.7 62.9 %collective-permute-start.46 = (bf16[512,1024]{1,0:T(8,128)(2,1)S(1)}, bf16[512,1024]{1,0:T(8,128)(2,1)S(1)}, u32[]{:S(2)}, u32[]{:S(2)}) collective-permute-start(bf16[512,1024]{1,0:T(8,128)(2,1)S(1)} %convolution_convert_fusion.9), channel_id=1, source_target_pairs={{0,2},{1,3},{2,0},{3,1},{4,6},{5,7},{6,4},{7,5},{8,10},{9,11},{10,... | collective-permute-start | bytes 3145736 | tf_op jit(solution)/shard_map/ppermute | solution.py:716
  391.2 61.3 %collective-permute-start.26 = (bf16[512,1024]{1,0:T(8,128)(2,1)S(1)}, bf16[512,1024]{1,0:T(8,128)(2,1)S(1)}, u32[]{:S(2)}, u32[]{:S(2)}) collective-permute-start(bf16[512,1024]{1,0:T(8,128)(2,1)S(1)} %convolution_convert_fusion.13), channel_id=1, source_target_pairs={{0,2},{1,3},{2,0},{3,1},{4,6},{5,7},{6,4},{7,5},{8,10},{9,11},{10,... | collective-permute-start | bytes 3145736 | tf_op jit(solution)/shard_map/ppermute | solution.py:716
  392.0 116.5 %collective-permute-start.67 = (bf16[4,64,1536]{2,1,0:T(8,128)(2,1)S(1)}, bf16[4,64,1536]{2,1,0:T(8,128)(2,1)S(1)}, u32[]{:S(2)}, u32[]{:S(2)}) collective-permute-start(bf16[4,64,1536]{2,1,0:T(8,128)(2,1)S(1)} %fusion.69), channel_id=1, source_target_pairs={{0,4},{1,5},{2,6},{3,7},{4,0},{5,1},{6,2},{7,3},{8,12},{9,13},{10,... | collective-permute-start | bytes 2359304 | tf_op jit(solution)/shard_map/ppermute | solution.py:716
  396.8 59.9 %collective-permute-start.84 = (f32[2304]{0:T(1024)S(1)}, f32[2304]{0:T(1024)S(1)}, u32[]{:S(2)}, u32[]{:S(2)}) collective-permute-start(f32[2304]{0:T(1024)S(1)} %pad_maximum_fusion.30), channel_id=1, source_target_pairs={{0,1},{1,0},{2,3},{3,2},{4,5},{5,4},{6,7},{7,6},{8,9},{9,8},{10,11... | collective-permute-start | bytes 27656 | tf_op jit(solution)/shard_map/ppermute | solution.py:716
  486.4 29.6 %collective-permute-start.57 = (bf16[4,64,1536]{2,1,0:T(8,128)(2,1)S(1)}, bf16[4,64,1536]{2,1,0:T(8,128)(2,1)S(1)}, u32[]{:S(2)}, u32[]{:S(2)}) collective-permute-start(bf16[4,64,1536]{2,1,0:T(8,128)(2,1)S(1)} %fusion.73), channel_id=1, source_target_pairs={{0,4},{1,5},{2,6},{3,7},{4,0},{5,1},{6,2},{7,3},{8,12},{9,13},{10,... | collective-permute-start | bytes 2359304 | tf_op jit(solution)/shard_map/ppermute | solution.py:716
  499.4 67.1 %collective-permute-start.83 = (bf16[384,1024]{1,0:T(8,128)(2,1)S(1)}, bf16[384,1024]{1,0:T(8,128)(2,1)S(1)}, u32[]{:S(2)}, u32[]{:S(2)}) collective-permute-start(bf16[384,1024]{1,0:T(8,128)(2,1)S(1)} %bitcast.328), channel_id=1, source_target_pairs={{0,4},{1,5},{2,6},{3,7},{4,0},{5,1},{6,2},{7,3},{8,12},{9,13},{10,... | collective-permute-start | bytes 2359304 | tf_op jit(solution)/shard_map/ppermute | solution.py:716
  516.0 83.6 %collective-permute-start.38 = (bf16[4,64,1024]{2,1,0:T(8,128)(2,1)S(1)}, bf16[4,64,1024]{2,1,0:T(8,128)(2,1)S(1)}, u32[]{:S(2)}, u32[]{:S(2)}) collective-permute-start(bf16[4,64,1024]{2,1,0:T(8,128)(2,1)S(1)} %fusion.79), channel_id=1, source_target_pairs={{0,4},{1,5},{2,6},{3,7},{4,0},{5,1},{6,2},{7,3},{8,12},{9,13},{10,... | collective-permute-start | bytes 1572872 | tf_op jit(solution)/shard_map/ppermute | solution.py:716
  542.3 61.5 %collective-permute-start.28 = (bf16[4,64,1024]{2,1,0:T(8,128)(2,1)S(1)}, bf16[4,64,1024]{2,1,0:T(8,128)(2,1)S(1)}, u32[]{:S(2)}, u32[]{:S(2)}) collective-permute-start(bf16[4,64,1024]{2,1,0:T(8,128)(2,1)S(1)} %fusion.83), channel_id=1, source_target_pairs={{0,4},{1,5},{2,6},{3,7},{4,0},{5,1},{6,2},{7,3},{8,12},{9,13},{10,... | collective-permute-start | bytes 1572872 | tf_op jit(solution)/shard_map/ppermute | solution.py:716
  588.6 64.8 %collective-permute-start.54 = (bf16[256,1024]{1,0:T(8,128)(2,1)S(1)}, bf16[256,1024]{1,0:T(8,128)(2,1)S(1)}, u32[]{:S(2)}, u32[]{:S(2)}) collective-permute-start(bf16[256,1024]{1,0:T(8,128)(2,1)S(1)} %bitcast.334), channel_id=1, source_target_pairs={{0,4},{1,5},{2,6},{3,7},{4,0},{5,1},{6,2},{7,3},{8,12},{9,13},{10,... | collective-permute-start | bytes 1572872 | tf_op jit(solution)/shard_map/ppermute | solution.py:716
  598.1 59.4 %collective-permute-start.74 = (bf16[256,1536]{1,0:T(8,128)(2,1)S(1)}, bf16[256,1536]{1,0:T(8,128)(2,1)S(1)}, u32[]{:S(2)}, u32[]{:S(2)}) collective-permute-start(bf16[256,1536]{1,0:T(8,128)(2,1)S(1)} %bitcast.326), channel_id=1, source_target_pairs={{0,4},{1,5},{2,6},{3,7},{4,0},{5,1},{6,2},{7,3},{8,12},{9,13},{10,... | collective-permute-start | bytes 2359304 | tf_op jit(solution)/shard_map/ppermute | solution.py:716
  618.9 38.9 %collective-permute-start.64 = (bf16[256,1536]{1,0:T(8,128)(2,1)S(1)}, bf16[256,1536]{1,0:T(8,128)(2,1)S(1)}, u32[]{:S(2)}, u32[]{:S(2)}) collective-permute-start(bf16[256,1536]{1,0:T(8,128)(2,1)S(1)} %bitcast.327), channel_id=1, source_target_pairs={{0,4},{1,5},{2,6},{3,7},{4,0},{5,1},{6,2},{7,3},{8,12},{9,13},{10,... | collective-permute-start | bytes 2359304 | tf_op jit(solution)/shard_map/ppermute | solution.py:716
  (131 other events, 1452.1 us)

commit v3 on v2

--- a/solution.py
+++ b/solution.py
@@ -328,6 +328,7 @@
 
 ALL = ("dp", "group")
 LOG2E = 1.4426950408889634
+SMALL = pl.CostEstimate(flops=1000000, bytes_accessed=100000, transcendentals=0)
 
 
 def tie(value, *others):
@@ -380,11 +381,81 @@
             in_specs=in_specs,
             out_specs=[pl.BlockSpec((chunk, width), target_row)] * outputs,
         ),
-        cost_estimate=pl.CostEstimate(
-            flops=0, bytes_accessed=4 * outputs * count * chunk * width, transcendentals=0
-        ),
+        cost_estimate=SMALL,
         name="place_rows",
     )(targets, *operands)
+
+
+def cut_columns(array, rows_array, where_at, kinds, parts):
+    lead, total = array.shape
+    groups = 4
+    kept = total // groups
+    rows_lead, rows_width = rows_array.shape
+
+    def kernel(at_ref, *refs):
+        sources = refs[: len(kinds)]
+        rows_ref = refs[len(kinds)]
+        chip, diagonal, core, near, far, rows_out = refs[len(kinds) + 1 :]
+        step = pl.program_id(0)
+        for number, target in enumerate(
+            (chip, diagonal, core.at[0], core.at[1], near, far)
+        ):
+
+            @pl.when(step == number)
+            def _(target=target):
+                low = 0
+                for part in range(parts):
+                    for source, (first, size) in zip(sources, kinds):
+                        width = size // parts
+                        target[:, low : low + width] = source[
+                            :, part * width : (part + 1) * width
+                        ].astype(jnp.bfloat16)
+                        low += width
+
+        @pl.when(step == 0)
+        def _():
+            rows_out[...] = rows_ref[...].astype(jnp.bfloat16)
+
+    def block_at(step, at_ref):
+        half, rank, side = at_ref[0], at_ref[1], at_ref[2]
+        sent = jnp.where(side == 0, 1 - half, half)
+        pair = jnp.where(
+            step < 2, sent, jnp.where((step == 2) | (step == 4), half, 1 - half)
+        )
+        other = (step == 1) | (step == 2) | (step == 3)
+        return pair * 2 + jnp.where(other, 1 - rank, rank)
+
+    def source_spec(first, size):
+        return pl.BlockSpec(
+            (lead, size), lambda i, at_ref: (0, first // size + block_at(i, at_ref))
+        )
+
+    flat = pl.BlockSpec((lead, kept), lambda i, at_ref: (0, 0))
+    pair = pl.BlockSpec((2, lead, kept), lambda i, at_ref: (0, 0, 0))
+    half_rows = (rows_lead // 2, rows_width)
+    single = jax.ShapeDtypeStruct((lead, kept), jnp.bfloat16)
+    return pl.pallas_call(
+        kernel,
+        out_shape=[
+            single,
+            single,
+            jax.ShapeDtypeStruct((2, lead, kept), jnp.bfloat16),
+            single,
+            single,
+            jax.ShapeDtypeStruct(half_rows, jnp.bfloat16),
+        ],
+        grid_spec=pltpu.PrefetchScalarGridSpec(
+            num_scalar_prefetch=1,
+            grid=(6,),
+            in_specs=[source_spec(first, size) for first, size in kinds]
+            + [pl.BlockSpec(half_rows, lambda i, at_ref: (at_ref[2], 0))],
+            out_specs=[flat, flat, pair, flat, flat]
+            + [pl.BlockSpec(half_rows, lambda i, at_ref: (0, 0))],
+        ),
+        compiler_params=pltpu.CompilerParams(vmem_limit_bytes=48 * 1024 * 1024),
+        cost_estimate=SMALL,
+        name="cut_columns",
+    )(where_at, *([array] * len(kinds)), rows_array)
 
 
 def join_columns(own_near, own_far, peer, chip, diagonal, chip_side, diagonal_side, where_at, parts):
@@ -427,9 +498,7 @@
             out_specs=pl.BlockSpec((lead, 2 * cols), lambda i, at_ref: (i, 0)),
         ),
         compiler_params=pltpu.CompilerParams(vmem_limit_bytes=48 * 1024 * 1024),
-        cost_estimate=pl.CostEstimate(
-            flops=0, bytes_accessed=32 * lead * cols, transcendentals=0
-        ),
+        cost_estimate=SMALL,
         name="join_columns",
     )(where_at, own_near, own_far, peer, chip, diagonal, chip_side, diagonal_side)
 
@@ -506,7 +575,6 @@
                     )
             total_ref[low:high, :] = kept
 
-    work = heads * ratio * rows * rows * HD * 4 * 5 // 8
     return pl.pallas_call(
         kernel,
         grid=(heads,),
@@ -526,11 +594,7 @@
             jax.ShapeDtypeStruct((rows, heads * HD), f32),
         ],
         compiler_params=pltpu.CompilerParams(vmem_limit_bytes=48 * 1024 * 1024),
-        cost_estimate=pl.CostEstimate(
-            flops=work,
-            bytes_accessed=heads * rows * (wide * 4 + ratio * HD * 2 + HD * 4),
-            transcendentals=heads * ratio * rows * rows * 5 // 8,
-        ),
+        cost_estimate=SMALL,
         name="attend_forward",
     )(mixed, cosine, sine, gain_query, gain_key)
 
@@ -631,7 +695,6 @@
         out_ref[:, ratio * HD : (ratio + 1) * HD] = back.astype(bf16)
         out_ref[:, (ratio + 1) * HD :] = value_sum[...].astype(bf16)
 
-    work = heads * ratio * rows * rows * HD * 10 * 5 // 8
     return pl.pallas_call(
         kernel,
         grid=(heads,),
@@ -657,11 +720,7 @@
         ],
         scratch_shapes=[pltpu.VMEM((rows, HD), f32), pltpu.VMEM((rows, HD), f32)],
         compiler_params=pltpu.CompilerParams(vmem_limit_bytes=48 * 1024 * 1024),
-        cost_estimate=pl.CostEstimate(
-            flops=work,
-            bytes_accessed=heads * rows * (wide * 6 + ratio * HD * 4 + HD * 4),
-            transcendentals=heads * ratio * rows * rows * 5 // 8,
-        ),
+        cost_estimate=SMALL,
         name="attend_backward",
     )(mixed, cosine, sine, gain_query, gain_key, attended, totals, grad_att)
 
@@ -705,7 +764,6 @@
     rank = member % 2
     side = copy % 2
     depth = copies // 2
-    deep = copy // 2
 
     def permute(value, target):
         pairs = []
@@ -727,9 +785,6 @@
     def over_side(value):
         return permute(value, lambda d, g: (d ^ 1, g))
 
-    def over_depth(value, shift):
-        return permute(value, lambda d, g: ((d // 2 + shift) % depth * 2 + d % 2, g))
-
     def block_of(far, other_rank):
         at = half if not far else 1 - half
         return at * 2 + (rank if not other_rank else 1 - rank)
@@ -742,16 +797,19 @@
             [jnp.where(first_side, mine, theirs), jnp.where(first_side, theirs, mine)]
         )
 
-    gain_low = gain_weight.astype(bf16)
-    gain_pair = ordered(rank == 0, gain_low, over_core(gain_low))
-    gains = ordered(half == 0, gain_pair, over_chip(gain_pair)).astype(f32)
-    gain_one = gains[:D]
-    gain_two = gains[D : 2 * D]
-    gain_query = gains[2 * D : 2 * D + HD].reshape(1, HD)
-    gain_key = gains[2 * D + HD :].reshape(1, HD)
-
-    first_piece = pick(stretch_order, member * held)
-    start = pick(positions, half)[0] - first_piece * chunk
+    table = jnp.arange(pieces, dtype=jnp.int32)
+
+    def places_of(stored):
+        return jnp.sum(
+            jnp.where(stored[:, None] == table[None, :], stretch_order[None, :], 0), axis=1
+        )
+
+    slots = jnp.arange(pieces, dtype=jnp.int32)
+    slot_rank = jnp.where(slots < 2 * held, rank, 1 - rank)
+    slot_half = jnp.where(slots // held % 2 == 0, half, 1 - half)
+    all_targets = places_of((slot_half * 2 + slot_rank) * held + slots % held)
+    own_targets, peer_targets = all_targets[: 2 * held], all_targets[2 * held :]
+    start = pick(positions, half)[0] - all_targets[0] * chunk
     exponent = jnp.arange(HD // 2, dtype=f32) * (2.0 / HD)
     inverse = jnp.power(jnp.float32(ROPE_BASE), -exponent)
     places = (start + jnp.arange(seq_len, dtype=jnp.int32)).astype(f32)
@@ -760,69 +818,16 @@
     cosine = jnp.concatenate([cosine_half, cosine_half], axis=-1)
     sine = jnp.concatenate([-sine_half, sine_half], axis=-1)
 
-    def piece_targets(other_rank):
-        return [
-            stretch_order[block_of(far, other_rank) * held + number]
-            for far in (False, True)
-            for number in range(held)
-        ]
-
-    own_targets = jnp.stack(piece_targets(False))
-    peer_targets = jnp.stack(piece_targets(True))
-    all_targets = jnp.concatenate([own_targets, peer_targets])
-
-    def whole_sequence(array, far_part, gain):
-        mine = jnp.concatenate([pick(array, half), far_part], axis=0)
-        return place_rows(mine, over_core(mine), all_targets, chunk, gain)
-
     parts = 2
     wide = (ratio + 2) * HD
     some = ff // parts
-
-    def by_heads(array):
-        blocks = []
-        for head in range(KV):
-            blocks.append(array[:, head * ratio * HD : (head + 1) * ratio * HD])
-            blocks.append(array[:, (H + head) * HD : (H + head + 1) * HD])
-            blocks.append(array[:, (H + KV + head) * HD : (H + KV + head + 1) * HD])
-        size = 3 * KV // groups
-        return jnp.stack(
-            [
-                jnp.concatenate(blocks[number * size : (number + 1) * size], axis=1)
-                for number in range(groups)
-            ]
-        )
-
-    def by_units(array):
-        stacked = []
-        for number in range(groups):
-            blocks = []
-            for part in range(parts):
-                low = number * ff + part * some
-                blocks.append(array[:, low : low + some])
-                blocks.append(array[:, FF + low : FF + low + some])
-            stacked.append(jnp.concatenate(blocks, axis=1))
-        return jnp.stack(stacked)
-
     where_at = jnp.stack([half, rank, side]).astype(jnp.int32)
 
     class Columns:
-        def __init__(self, blocked):
-            sent_half = jnp.where(side == 0, 1 - half, half)
-            self.to_chip = pick(blocked, sent_half * 2 + rank)
-            self.to_diagonal = pick(blocked, sent_half * 2 + 1 - rank)
-            self.to_core = jnp.stack(
-                [pick(blocked, block_of(False, True)), pick(blocked, block_of(True, True))]
+        def __init__(self, array, rows_array, kinds):
+            self.to_chip, self.to_diagonal, self.to_core, self.near, self.far, self.rows = (
+                cut_columns(array, rows_array, where_at, kinds, parts)
             )
-            self.near = pick(blocked, block_of(False, False))
-            self.far = pick(blocked, block_of(True, False))
-
-        def send(self):
-            self.chip = over_chip(self.to_chip)
-            self.diagonal = over_diagonal(self.to_diagonal)
-            self.peer = over_core(self.to_core)
-            self.chip_side = over_side(self.chip)
-            self.diagonal_side = over_side(self.diagonal)
 
         def joined(self):
             return join_columns(
@@ -830,34 +835,65 @@
                 self.chip_side, self.diagonal_side, where_at, parts,
             )
 
-    class Rows:
-        def __init__(self, own):
-            self.own = own
-            self.payload = pick(own.reshape(2, own.shape[0] // 2, own.shape[1]), side)
-
-        def send(self):
-            self.chip = over_chip(self.payload)
-            self.side = over_side(self.chip)
-
-        def joined(self):
-            return jnp.concatenate([self.own, ordered(side == 0, self.chip, self.side)], axis=0)
-
-    hidden_far = over_chip(pick(hidden_in, 1 - half))
-    qkv = Columns(by_heads(qkv_weight.astype(bf16)))
-    qkv.send()
-    out = Rows(tie(out_weight, qkv.to_chip, qkv.to_diagonal, qkv.to_core).astype(bf16))
-    out.payload = tie(out.payload, hidden_far)
-    out.send()
-    gateup = Columns(by_units(tie(gateup_weight, qkv.to_chip, out.payload).astype(bf16)))
-    gateup.to_chip = tie(gateup.to_chip, qkv.chip)
-    gateup.to_diagonal = tie(gateup.to_diagonal, qkv.diagonal)
-    gateup.send()
-    down = Rows(tie(down_weight, gateup.to_chip, gateup.to_diagonal).astype(bf16))
-    down.payload = tie(down.payload, out.chip, gateup.chip)
-    down.send()
-    grad_far = over_chip(tie(pick(out_grad, 1 - half), gateup.diagonal))
-
-    hidden, normed_low = whole_sequence(hidden_in, hidden_far, gain_one)
+    def join_rows(own, chip, other_side):
+        return jnp.concatenate([own.astype(bf16), ordered(side == 0, chip, other_side)], axis=0)
+
+    gain_rows = gain_weight.shape[0]
+    gain_pad = jnp.pad(gain_weight.astype(bf16), (0, 16 * width - gain_rows)).reshape(16, width)
+    hidden_sent = jnp.concatenate([pick(hidden_in, 1 - half), gain_pad], axis=0)
+    hidden_far = over_chip(hidden_sent)
+    block_cols = H * HD // groups
+    key_cols = KV * HD // groups
+    qkv = Columns(
+        tie(qkv_weight, hidden_sent),
+        out_weight,
+        [(0, block_cols), (H * HD, key_cols), ((H + KV) * HD, key_cols)],
+    )
+    qkv_chip = over_chip(jnp.stack([qkv.to_chip, qkv.rows]))
+    qkv.diagonal = over_diagonal(qkv.to_diagonal)
+    qkv.peer = over_core(qkv.to_core)
+    gateup = Columns(
+        tie(gateup_weight, qkv.to_chip, qkv.to_diagonal), down_weight, [(0, ff), (FF, ff)]
+    )
+    gateup.chip = over_chip(tie(gateup.to_chip, hidden_far))
+    hidden_mine = jnp.concatenate(
+        [pick(hidden_in, half), hidden_far[:local_len], gain_pad, hidden_far[local_len:]], axis=0
+    )
+    hidden_theirs = over_core(hidden_mine)
+    gain_low = gain_pad.reshape(-1)[:gain_rows]
+    gain_parts = [
+        block.reshape(-1)[:gain_rows]
+        for block in (
+            hidden_theirs[2 * local_len : 2 * local_len + 16],
+            hidden_far[local_len:],
+            hidden_theirs[2 * local_len + 16 :],
+        )
+    ]
+    gains = ordered(
+        half == 0,
+        ordered(rank == 0, gain_low, gain_parts[0]),
+        ordered(rank == 0, gain_parts[1], gain_parts[2]),
+    ).astype(f32)
+    gain_one = gains[:D]
+    gain_two = gains[D : 2 * D]
+    gain_query = gains[2 * D : 2 * D + HD].reshape(1, HD)
+    gain_key = gains[2 * D + HD :].reshape(1, HD)
+
+    qkv_side = over_side(tie(qkv_chip, hidden_mine))
+    gateup.diagonal = over_diagonal(tie(gateup.to_diagonal, qkv_chip))
+    qkv.diagonal_side = over_side(qkv.diagonal)
+    qkv.chip, qkv.chip_side = qkv_chip[0], qkv_side[0]
+    w_out = join_rows(out_weight, qkv_chip[1], qkv_side[1])
+    down_chip = over_chip(tie(gateup.rows, qkv.diagonal))
+    gateup.chip_side = over_side(gateup.chip)
+    gateup.diagonal_side = over_side(gateup.diagonal)
+    grad_far = over_chip(tie(pick(out_grad, 1 - half), gateup.chip))
+    gateup.peer = over_core(tie(gateup.to_core, qkv.peer))
+    grad_mine = jnp.concatenate([pick(out_grad, half), grad_far], axis=0)
+    grad_theirs = over_core(grad_mine)
+    down_side = over_side(down_chip)
+
+    hidden, normed_low = place_rows(hidden_mine, hidden_theirs, all_targets, chunk, gain_one)
     tokens = hidden.astype(f32)
     w_qkv = qkv.joined()
     mixed = split_product(normed_low, w_qkv, 1, 0)
@@ -865,7 +901,6 @@
     attended, totals = attend_forward(
         mixed, cosine, sine, gain_query, gain_key, heads, ratio, block
     )
-    w_out = out.joined()
     branch = split_product(attended, w_out, 1, 0).astype(bf16)
     middle = tokens + (branch.astype(f32) + over_core(branch).astype(f32))
     second, pull_two = jax.vjp(rms_scale, middle, gain_two)
@@ -890,7 +925,7 @@
 
     inner, pull_gate = jax.vjp(gated_all, gate_up)
     inner_low = inner.astype(bf16)
-    (grad_result,) = whole_sequence(out_grad, grad_far, None)
+    (grad_result,) = place_rows(grad_mine, grad_theirs, all_targets, chunk, None)
 
     def half_columns(array, far):
         size = array.shape[1] // 2
@@ -930,27 +965,29 @@
         value = value.reshape(2, depth, -1, value.shape[-1])
         return add(pick(value, side), over_side(pick(value, 1 - side)))
 
-    def depth_sum(value):
-        received = [
-            over_depth(pick(value, (deep + shift) % depth), shift) for shift in range(1, depth)
-        ]
-        return add(pick(value, deep), *received)
-
-    def depth_gather(value):
-        whole = jnp.zeros((depth, *value.shape), bf16)
-        for shift in range(depth):
-            piece = value if shift == 0 else over_depth(value, shift)
-            whole = lax.dynamic_update_index_in_dim(whole, piece, (deep - shift) % depth, 0)
-        return whole
+    deep_groups = [[d * 2 + x for d in range(depth)] for x in range(2)]
+
+    def depth_all(value):
+        return lax.psum(value, "dp", axis_index_groups=deep_groups)
 
     def side_gather(value):
         flat = value.reshape(-1, value.shape[-1])
         return ordered(side == 0, flat, over_side(flat))
 
+    token = [None]
+
+    def event(*values):
+        if token[0] is None:
+            return values
+        return lax.optimization_barrier((*values, token[0]))[: len(values)]
+
+    def passed(value):
+        token[0] = value
+
+    w_down = join_rows(down_weight, down_chip, down_side)
     down_near, down_received = exchange(
         far_columns(inner_low, True), far_columns(inner_low, False), grad_result
     )
-    w_down = down.joined()
     grad_inner = split_product(grad_result, w_down, 1, 1)
     (grad_gate_up,) = pull_gate(grad_inner)
     grad_gate_low = grad_gate_up.astype(bf16)
@@ -971,29 +1008,6 @@
     )
     grad_att = split_product(grad_branch_low, w_out, 1, 1).astype(bf16)
     normed_near, normed_far = half_columns(normed_low, False), half_columns(normed_low, True)
-    grad_parts = []
-    qkv_sent = []
-    gain_parts = []
-    for part in range(parts):
-        grad_part, grad_query_part, grad_key_part = attend_backward(
-            mixed, cosine, sine, gain_query, gain_key, attended, totals, grad_att,
-            part, parts, ratio, block,
-        )
-        grad_parts.append(grad_part)
-        gain_parts.append((grad_query_part[0], grad_key_part[0]))
-        qkv_sent.append(exchange(normed_far, normed_near, grad_part))
-    normed_part = sum(
-        split_product(grad_parts[part], w_qkv[:, part * 2 * wide : (part + 1) * 2 * wide], 1, 1)
-        for part in range(parts)
-    ).astype(bf16)
-
-    down_sum = side_sum(add(down_near, tie(down_received, grad_att)))
-    down_sum = depth_sum(tie(down_sum, grad_parts[0]))
-    down_sum = side_gather(depth_gather(tie(down_sum, grad_parts[1])))
-    gateup_swapped = []
-    for part in range(parts):
-        near, received = gateup_sent[part]
-        gateup_swapped.append(swap_rows(near, tie(received, grad_parts[part])))
 
     def share_rows(part):
         return take_rows(part, own_targets, chunk).astype(f32) + over_core(
@@ -1007,19 +1021,95 @@
         last = jnp.where(half == 0, from_far, stored[0])
         return jnp.stack([first, last])
 
-    layer_out = to_stored(take_rows(middle, own_targets, chunk) + share_rows(result_part))
+    def backward_part(part, grad_att):
+        grad_part, grad_query_part, grad_key_part = attend_backward(
+            mixed, cosine, sine, gain_query, gain_key, attended, totals, grad_att,
+            part, parts, ratio, block,
+        )
+        return grad_part, grad_query_part[0], grad_key_part[0]
+
+    def y_step(near, received):
+        near, received = event(near, received)
+        value = add(near, received)
+        passed(value)
+        return value
+
+    def swap_step(near, received):
+        near, received = event(near, received)
+        value = swap_rows(near, received)
+        passed(value)
+        return value
+
+    def x_parts(value):
+        value = value.reshape(2, depth, -1, value.shape[-1])
+        return pick(value, side), over_side(pick(value, 1 - side))
+
+    def x_step(kept_received):
+        value = add(*event(*kept_received))
+        passed(value)
+        return depth_all(value)
+
+    def back_step(value):
+        (value,) = event(value)
+        flat = value.reshape(-1, value.shape[-1])
+        received = over_side(flat)
+        passed(flat)
+        return flat, received
+
+    def last_step(flat_received):
+        flat, received = flat_received
+        return ordered(side == 0, flat, received)
+
+    down_x = x_parts(y_step(down_near, tie(down_received, grad_att)))
+    grad_att = tie(grad_att, down_x[0])
+    back_0 = backward_part(0, grad_att)
+    qkv_0 = exchange(normed_far, normed_near, back_0[0])
+    down_z = x_step((down_x[0], tie(down_x[1], qkv_0[0])))
+    grad_att = tie(grad_att, token[0])
+    back_1 = backward_part(1, grad_att)
+    far_1 = split_product(normed_far, back_1[0], 0, 0).astype(bf16)
+    near_1 = split_product(normed_near, back_1[0], 0, 0).astype(bf16)
+    gateup_0 = swap_step(gateup_sent[0][0], tie(gateup_sent[0][1], near_1))
+    gateup_0x = x_parts(gateup_0)
+    normed_part = split_product(
+        tie(back_0[0], token[0]), w_qkv[:, : 2 * wide], 1, 1
+    ) + split_product(tie(back_1[0], token[0]), w_qkv[:, 2 * wide :], 1, 1)
+    normed_part = normed_part.astype(bf16)
+    down_b = back_step(tie(down_z, normed_part))
+    gateup_0z = x_step(gateup_0x)
+    gateup_1 = swap_step(*gateup_sent[1])
+    received_1 = over_chip(tie(far_1, token[0]))
+    gateup_1x = x_parts(gateup_1)
     grad_normed = share_rows(normed_part)
     own_tokens = take_rows(hidden, own_targets, chunk).astype(f32)
     unused, pull_one = jax.vjp(rms_scale, own_tokens, gain_one)
     grad_token_part, grad_gain_one = pull_one(grad_normed)
-    input_grad = to_stored(take_rows(grad_middle, own_targets, chunk) + grad_token_part)
-
-    def rest_of_sum(value):
-        return side_gather(depth_gather(depth_sum(side_sum(value))))
-
-    gateup_sums = [rest_of_sum(value) for value in gateup_swapped]
-    out_sum = rest_of_sum(add(out_near, out_received))
-    qkv_sums = [rest_of_sum(swap_rows(*sent)) for sent in qkv_sent]
+    input_rows = take_rows(grad_middle, own_targets, chunk) + grad_token_part
+    down_sum = last_step(down_b)
+    gateup_0b = back_step(gateup_0z)
+    out_x = x_parts(y_step(out_near, out_received))
+    gateup_1z = x_step(gateup_1x)
+    gateup_0sum = last_step(gateup_0b)
+    qkv_0x = x_parts(swap_step(*qkv_0))
+    gateup_1b = back_step(gateup_1z)
+    out_z = x_step(out_x)
+    out_b = back_step(out_z)
+    qkv_0z = x_step(qkv_0x)
+    qkv_1x = x_parts(swap_step(near_1, received_1))
+    layer_out = to_stored(
+        take_rows(middle, own_targets, chunk) + share_rows(tie(result_part, token[0]))
+    )
+    input_grad = to_stored(tie(input_rows, token[0]))
+    gateup_1sum = last_step(gateup_1b)
+    qkv_0b = back_step(qkv_0z)
+    qkv_1z = x_step(qkv_1x)
+    out_sum = last_step(out_b)
+    qkv_1b = back_step(qkv_1z)
+    qkv_0sum = last_step(qkv_0b)
+    qkv_1sum = last_step(qkv_1b)
+    gateup_sums = [gateup_0sum, gateup_1sum]
+    qkv_sums = [qkv_0sum, qkv_1sum]
+    gain_parts = [back_0[1:], back_1[1:]]
     total_down = down_sum.astype(f32)
     total_out = out_sum.astype(f32)
 
@@ -1061,7 +1151,7 @@
     total_gains = total_gains + over_core(total_gains)
     total_gains = total_gains + over_chip(total_gains)
     total_gains = total_gains + over_side(total_gains)
-    total_gains = total_gains + sum(over_depth(total_gains, shift) for shift in range(1, depth))
+    total_gains = lax.psum(tie(total_gains, token[0]), "dp", axis_index_groups=deep_groups)
     gain_rows = gain_weight.shape[0]
     total_gain = lax.dynamic_slice_in_dim(total_gains, member * gain_rows, gain_rows, 0)
 

time: 690 us -> 694 us (level); the launches traced: 686 us -> 683 us
  starting transfers between devices: 115 us -> 43.3 us
  other arithmetic: 96.3 us -> 116 us
  blocking collectives: 0 us -> 18 us
  Pallas kernels: 82.7 us -> 96 us
  between operations: 9.49 us -> 21.6 us
    psum x0 -> x6, waiting for transfers between devices: none -> 124 us  [depth_all(): return lax.psum(value, 'dp', axis_index_groups=deep_groups)]
    ppermute x90 -> x47, waiting for transfers between devices: 252 us -> 129 us  [permute(): return lax.ppermute(value, ALL, pairs)]
    ppermute x90 -> x47, starting transfers between devices: 115 us -> 42.1 us  [permute(): return lax.ppermute(value, ALL, pairs)]
    psum x0 -> x1, blocking collectives: none -> 18 us  [paired_shards(): lax.psum(tie(total_gains, token[0]), 'dp', axis_index_groups=deep_groups)]
    pallas_call x0 -> x2, Pallas kernels: none -> 14.2 us  [cut_columns(): pl.pallas_call(kernel, out_shape=[single, single, jax.ShapeDtypeStruct((2...]
    convert_element_type x13 -> x12, other arithmetic: 6.23 us -> 17.8 us  [add(): return total.astype(bf16)]
    unnamed x189 -> x231, local copies, waits for them, and re-layouts: 18.3 us -> 28.1 us
    squeeze x4, other arithmetic: 0.96 us -> 8.11 us  [pick(): return lax.dynamic_index_in_dim(array, index, 0, keepdims=False)]
  transfers between devices with their start and end apart: 90 -> 53, of which waited for: 38 -> 18; matrix products, arithmetic and copies ran while one was open for 22% -> 26% of each run, Pallas kernels for 12% -> 14%
where the time goes in v3:
time: 694 us; the launch traced here: 683 us
  waiting for transfers between devices  253 us (36%)
  other arithmetic  116 us (17%)
  Pallas kernels  96 us (14%)
  matrix products  84.2 us (12%)
  local copies, waits for them, and re-layouts  51 us (7%)
  starting transfers between devices  43.3 us (6%)
  between operations  21.6 us (3%)
  blocking collectives  18 us (3%)
    ppermute x47, waiting for transfers between devices, permute(): return lax.ppermute(value, ALL, pairs)  129 us
    psum x6, waiting for transfers between devices, depth_all(): return lax.psum(value, 'dp', axis_index_groups=deep_groups)  124 us
    dot_general x21, matrix products, split_product(): lax.dot_general(left, right, (((left_dim,), (right_dim,)), ((), ())), pre...  84.2 us
    ppermute x47, starting transfers between devices, permute(): return lax.ppermute(value, ALL, pairs)  42.1 us
    pallas_call x2, Pallas kernels, attend_backward(): pl.pallas_call(kernel, grid=(heads,), in_specs=[pl.BlockSpec((rows, wide)...  35.8 us
    unnamed x231, local copies, waits for them, and re-layouts  28.1 us
    sub x5, other arithmetic, adam_step(): return (weight - rate * (ratio + decay * weight), moment_new, square_new)  27.5 us
    pallas_call x1, Pallas kernels, attend_forward(): pl.pallas_call(kernel, grid=(heads,), in_specs=[pl.BlockSpec((rows, wide)...  22.2 us
  transfers between devices with their start and end apart: 53, of which 18 were waited for; matrix products, arithmetic and copies ran while one was open for 26% of the time, Pallas kernels for 14%

profile of v3, /device:TPU:0, one launch (start us, length us, event | category | flops | bytes accessed | tf_op | source)
XLA Modules:
  0.0 683.4 jit_solution(1991261072223097708)
XLA Ops:
  14.1 5.9 cut_columns.2
  31.9 8.2 %cut_columns.3 = (bf16[256,1536]{1,0:T(8,128)(2,1)}, bf16[256,1536]{1,0:T(8,128)(2,1)}, bf16[2,256,1536]{2,1,0:T(8,128)(2,1)}, bf16[256,1536]{1,0:T(8,128)(2,1)S...) custom-call(s32[3]{0:T(128)S(1)} %pad_add_fusion.at_ref, f32[256,6144]{1,0:T(8,128)} %refs_1_.1, ...), custom_call_target="tpu_custom_call" | custom-call | flops 1000000 | bytes 100000 | tf_op jit(solution)/shard_map/cut_columns/pallas_call | solution.py:437
  42.7 17.1 %collective-permute-done.4.diag_ref = bf16[256,1024]{1,0:T(8,128)(2,1)} collective-permute-done((bf16[256,1024]{1,0:T(8,128)(2,1)S(1)}, bf16[256,1024]{1,0:T(8,128)(2,1)}, u32[]{:S(2)}, u32[]{:S(2)}) %collective-permute-start.4) | collective-permute-done | bytes 524320 | tf_op jit(solution)/shard_map/ppermute | solution.py:774
  71.6 25.5 %collective-permute-done.9.chip_ref = bf16[256,1536]{1,0:T(8,128)(2,1)} collective-permute-done((bf16[256,1536]{1,0:T(8,128)(2,1)}, bf16[256,1536]{1,0:T(8,128)(2,1)}, u32[]{:S(2)}, u32[]{:S(2)}) %collective-permute-start.9) | collective-permute-done | bytes 786464 | tf_op jit(solution)/shard_map/ppermute | solution.py:774
  102.0 7.0 %place_rows.2 = (bf16[1024,1024]{1,0:T(8,128)(2,1)}, bf16[1024,1024]{1,0:T(8,128)(2,1)}) custom-call(s32[8]{0:T(128)} %copy-done.78, bf16[544,1024]{1,0:T(8,128)(2,1)} %pad_maximum_fusion.11.mine_ref, bf16[544,1024]{1,0:T(8,128)(2,1)} %collective-permute-done.1.theirs_ref, f32[1,1024]{1,0:T(1,128)} %bitcast.194), custom_call_target="tpu_custom_call" | custom-call | flops 1000000 | bytes 100000 | tf_op jit(solution)/shard_map/place_rows/pallas_call | solution.py:375
  116.2 9.0 %fusion.112.mixed_ref = f32[1024,2048]{1,0:T(8,128)} fusion(bf16[1024,1024]{1,0:T(8,128)(2,1)S(1)} %copy-done.86, bf16[1024,2048]{1,0:T(8,128)(2,1)} %join_columns.2), kind=kOutput, calls=%fused_computation.387 | convolution fusion | flops 4294967296 | bytes 14680064 | tf_op jit(solution)/shard_map/dot_general | solution.py:339
  125.2 22.2 %attend_forward.1 = (bf16[1024,1024]{1,0:T(8,128)(2,1)S(1)}, f32[1024,512]{1,0:T(8,128)S(1)}) custom-call(f32[1024,2048]{1,0:T(8,128)} %fusion.112.mixed_ref, f32[1024,128]{1,0:T(8,128)S(1)} %pad_maximum_fusion.29.cos_ref, f32[1024,128]{1,0:T(8,128)S(1)} %pad_maximum_fusion.30.sin_ref, f32[1,128]{1,0:T(1,128)S(1)} %get-tuple-element.303.gq_ref, ...), custom_call_target="tpu_custom_call" | custom-call | flops 1000000 | bytes 100000 | tf_op jit(solution)/shard_map/attend_forward/pallas_call | solution.py:578
  165.5 13.7 %collective-permute-done.11.chip_x_ref = bf16[256,1536]{1,0:T(8,128)(2,1)S(1)} collective-permute-done((bf16[256,1536]{1,0:T(8,128)(2,1)}, bf16[256,1536]{1,0:T(8,128)(2,1)S(1)}, u32[]{:S(2)}, u32[]{:S(2)}) %collective-permute-start.11) | collective-permute-done | bytes 786464 | tf_op jit(solution)/shard_map/ppermute | solution.py:774
  179.2 15.9 %collective-permute-done.12.diag_x_ref = bf16[256,1536]{1,0:T(8,128)(2,1)S(1)} collective-permute-done((bf16[256,1536]{1,0:T(8,128)(2,1)}, bf16[256,1536]{1,0:T(8,128)(2,1)S(1)}, u32[]{:S(2)}, u32[]{:S(2)}) %collective-permute-start.12) | collective-permute-done | bytes 786464 | tf_op jit(solution)/shard_map/ppermute | solution.py:774
  195.1 5.5 join_columns.3
  200.7 6.5 place_rows.3
  207.2 8.8 %fusion.56 = f32[1024,1536]{1,0:T(8,128)} fusion(bf16[1024,1024]{1,0:T(8,128)(2,1)} %place_rows.3, bf16[384,1024]{1,0:T(8,128)(2,1)} %get-tuple-element.251, bf16[384,1024]{1,0:T(8,128)(2,1)} %get-tuple-element.250, bf16[768,1024]{1,0:T(8,128)(2,1)} %convert_element_type.318), kind=kOutput, calls=%fused_computation.137 | convolution fusion | flops 3230662656 | bytes 11534336 | tf_op jit(solution)/shard_map/dot_general | solution.py:339
  222.8 6.7 fusion.113
  229.5 6.7 slice_multiply_fusion.3
  240.5 4.9 add_convert_fusion
  245.5 9.1 %convolution_convert_fusion.6 = bf16[1024,1024]{1,0:T(8,128)(2,1)S(1)} fusion(bf16[1024,3072]{1,0:T(8,128)(2,1)S(1)} %add_convert_fusion, bf16[1024,3072]{1,0:T(8,128)(2,1)} %join_columns.3), kind=kOutput, calls=%fused_computation.76 | convolution fusion | flops 6443499520 | bytes 14680064 | tf_op jit(solution)/shard_map/dot_general | solution.py:339
  277.8 6.1 fusion.33
  294.3 9.6 %collective-permute-done.18 = bf16[768,1024]{1,0:T(8,128)(2,1)S(1)} collective-permute-done((bf16[768,1024]{1,0:T(8,128)(2,1)}, bf16[768,1024]{1,0:T(8,128)(2,1)S(1)}, u32[]{:S(2)}, u32[]{:S(2)}) %collective-permute-start.18) | collective-permute-done | bytes 1572896 | tf_op jit(solution)/shard_map/ppermute | solution.py:774
  305.1 17.8 %attend_backward.2 = (bf16[1024,1024]{1,0:T(8,128)(2,1)S(1)}, f32[1,128]{1,0:T(1,128)S(1)}, f32[1,128]{1,0:T(1,128)S(1)}) custom-call(f32[1024,2048]{1,0:T(8,128)} %fusion.112.mixed_ref, f32[1024,128]{1,0:T(8,128)S(1)} %pad_maximum_fusion.29.cos_ref, f32[1024,128]{1,0:T(8,128)S(1)} %pad_maximum_fusion.30.sin_ref, f32[1,128]{1,0:T(1,128)S(1)} %get-tuple-element.303.gq_ref, ...), custom_call_target="tpu_custom_call" | custom-call | flops 1000000 | bytes 100000 | tf_op jit(solution)/shard_map/attend_backward/pallas_call | solution.py:698
  333.0 17.9 %attend_backward.3 = (bf16[1024,1024]{1,0:T(8,128)(2,1)S(1)}, f32[1,128]{1,0:T(1,128)S(1)}, f32[1,128]{1,0:T(1,128)S(1)}) custom-call(f32[1024,2048]{1,0:T(8,128)} %fusion.112.mixed_ref, f32[1024,128]{1,0:T(8,128)S(1)} %pad_maximum_fusion.29.cos_ref, f32[1024,128]{1,0:T(8,128)S(1)} %pad_maximum_fusion.30.sin_ref, f32[1,128]{1,0:T(1,128)S(1)} %get-tuple-element.303.gq_ref, ...), custom_call_target="tpu_custom_call" | custom-call | flops 1000000 | bytes 100000 | tf_op jit(solution)/shard_map/attend_backward/pallas_call | solution.py:698
  375.7 29.7 %all-reduce.16.cloned.1.call-done = bf16[4,96,1024]{2,1,0:T(8,128)(2,1)} async-done(((bf16[4,96,1024]{2,1,0:T(8,128)(2,1)}), bf16[4,96,1024]{2,1,0:T(8,128)(2,1)}) %all-reduce.16.cloned.1.call-update) | async-done | bytes 786448 | tf_op jit(solution)/shard_map/psum | solution.py:971
  412.9 12.0 %collective-permute-done.43 = bf16[384,1024]{1,0:T(8,128)(2,1)} collective-permute-done((bf16[384,1024]{1,0:T(8,128)(2,1)}, bf16[384,1024]{1,0:T(8,128)(2,1)}, u32[]{:S(2)}, u32[]{:S(2)}) %collective-permute-start.43) | collective-permute-done | bytes 786464 | tf_op jit(solution)/shard_map/ppermute | solution.py:774
  445.4 5.9 all-reduce.18.cloned.1.call-done
  464.9 12.5 %collective-permute-done.41 = bf16[256,1536]{1,0:T(8,128)(2,1)} collective-permute-done((bf16[256,1536]{1,0:T(8,128)(2,1)}, bf16[256,1536]{1,0:T(8,128)(2,1)}, u32[]{:S(2)}, u32[]{:S(2)}) %collective-permute-start.41) | collective-permute-done | bytes 786464 | tf_op jit(solution)/shard_map/ppermute | solution.py:774
  480.6 24.3 %all-reduce.20.cloned.1.call-done = bf16[4,64,1536]{2,1,0:T(8,128)(2,1)} async-done(((bf16[4,64,1536]{2,1,0:T(8,128)(2,1)}), bf16[4,64,1536]{2,1,0:T(8,128)(2,1)}) %all-reduce.20.cloned.1.call-update) | async-done | bytes 786448 | tf_op jit(solution)/shard_map/psum | solution.py:971
  508.8 36.5 %all-reduce.22.cloned.1.call-done = bf16[4,64,1024]{2,1,0:T(8,128)(2,1)} async-done(((bf16[4,64,1024]{2,1,0:T(8,128)(2,1)}), bf16[4,64,1024]{2,1,0:T(8,128)(2,1)}) %all-reduce.22.cloned.1.call-update) | async-done | bytes 524304 | tf_op jit(solution)/shard_map/psum | solution.py:971
  565.7 10.9 %multiply_subtract_fusion = (f32[256,6144]{1,0:T(8,128)}, f32[256,6144]{1,0:T(8,128)}, f32[256,6144]{1,0:T(8,128)}) fusion(f32[256,6144]{1,0:T(8,128)S(1)} %bitcast.166, bf16[256,6144]{1,0:T(8,128)(2,1)} %slice_dynamic-update-slice_fusion, f32[256,6144]{1,0:T(8,128)S(1)} %bitcast.168, f32[256,6144]{1,0:T(8,128)} %param.31), kind=kLoop, calls=%fused_computation.5 | loop fusion | flops 25165824 | bytes 40894464 | tf_op jit(solution)/shard_map/sub | solution.py:93
  589.2 5.6 multiply_subtract_fusion.3
  600.8 8.5 %collective-permute-done.37 = bf16[256,1024]{1,0:T(8,128)(2,1)} collective-permute-done((bf16[256,1024]{1,0:T(8,128)(2,1)}, bf16[256,1024]{1,0:T(8,128)(2,1)}, u32[]{:S(2)}, u32[]{:S(2)}) %collective-permute-start.37) | collective-permute-done | bytes 524320 | tf_op jit(solution)/shard_map/ppermute | solution.py:774
  611.6 25.7 %all-reduce.26.cloned.1.call-done = bf16[4,64,1024]{2,1,0:T(8,128)(2,1)} async-done(((bf16[4,64,1024]{2,1,0:T(8,128)(2,1)}), bf16[4,64,1024]{2,1,0:T(8,128)(2,1)}) %all-reduce.26.cloned.1.call-update) | async-done | bytes 524304 | tf_op jit(solution)/shard_map/psum | solution.py:971
  643.4 18.0 %psum.55 = f32[2304]{0:T(1024)S(1)} all-reduce(f32[2304]{0:T(1024)S(1)} %add.506), channel_id=1, replica_groups={{0,8,16,24},{4,12,20,28},{1,9,17,25},{5,13,21,29},{2,10,18,26},{6,14,22..., use_global_device_ids=true, to_apply=%region_13.14 | all-reduce | flops 2304 | bytes 18432 | tf_op jit(solution)/shard_map/psum | solution.py:1154
  670.6 5.8 multiply_subtract_fusion.1
  (459 shorter events, 241.8 us)
Async XLA Ops:
  7.2 398.1 %all-reduce.16.cloned.1.call-start = ((), (), s32[]{:S(2)}) async-start(), calls=%async_computation | async-start | bytes 1572864 | tf_op jit(solution)/shard_map/psum | solution.py:971
  21.6 49.3 %collective-permute-start.2 = (bf16[2,256,1024]{2,1,0:T(8,128)(2,1)}, bf16[2,256,1024]{2,1,0:T(8,128)(2,1)}, u32[]{:S(2)}, u32[]{:S(2)}) collective-permute-start(bf16[2,256,1024]{2,1,0:T(8,128)(2,1)} %get-tuple-element.91), channel_id=1, source_target_pairs={{0,1},{1,0},{2,3},{3,2},{4,5},{5,4},{6,7},{7,6},{8,9},{9,8},{10,11... | collective-permute-start | bytes 3145736 | tf_op jit(solution)/shard_map/ppermute | solution.py:774
  22.7 45.4 %collective-permute-start.3 = (bf16[2,256,1024]{2,1,0:T(8,128)(2,1)}, bf16[2,256,1024]{2,1,0:T(8,128)(2,1)}, u32[]{:S(2)}, u32[]{:S(2)}) collective-permute-start(bf16[2,256,1024]{2,1,0:T(8,128)(2,1)} %pad_maximum_fusion.12), channel_id=1, source_target_pairs={{0,2},{1,3},{2,0},{3,1},{4,6},{5,7},{6,4},{7,5},{8,10},{9,11},{10,... | collective-permute-start | bytes 3145736 | tf_op jit(solution)/shard_map/ppermute | solution.py:774
  22.7 37.2 %collective-permute-start.4 = (bf16[256,1024]{1,0:T(8,128)(2,1)S(1)}, bf16[256,1024]{1,0:T(8,128)(2,1)}, u32[]{:S(2)}, u32[]{:S(2)}) collective-permute-start(bf16[256,1024]{1,0:T(8,128)(2,1)S(1)} %get-tuple-element.94), channel_id=1, source_target_pairs={{0,3},{1,2},{2,1},{3,0},{4,7},{5,6},{6,5},{7,4},{8,11},{9,10},{10,... | collective-permute-start | bytes 1572872 | tf_op jit(solution)/shard_map/ppermute | solution.py:774
  31.9 67.1 %collective-permute-start.1 = (bf16[544,1024]{1,0:T(8,128)(2,1)}, bf16[544,1024]{1,0:T(8,128)(2,1)}, u32[]{:S(2)}, u32[]{:S(2)}) collective-permute-start(bf16[544,1024]{1,0:T(8,128)(2,1)} %pad_maximum_fusion.11.mine_ref), channel_id=1, source_target_pairs={{0,1},{1,0},{2,3},{3,2},{4,5},{5,4},{6,7},{7,6},{8,9},{9,8},{10,11... | collective-permute-start | bytes 3342344 | tf_op jit(solution)/shard_map/ppermute | solution.py:774
  59.9 37.3 %collective-permute-start.13 = (bf16[384,1024]{1,0:T(8,128)(2,1)}, bf16[384,1024]{1,0:T(8,128)(2,1)}, u32[]{:S(2)}, u32[]{:S(2)}) collective-permute-start(bf16[384,1024]{1,0:T(8,128)(2,1)} %get-tuple-element.107), channel_id=1, source_target_pairs={{0,2},{1,3},{2,0},{3,1},{4,6},{5,7},{6,4},{7,5},{8,10},{9,11},{10,... | collective-permute-start | bytes 2359304 | tf_op jit(solution)/shard_map/ppermute | solution.py:774
  68.1 40.9 %collective-permute-start.5 = (bf16[2,256,1024]{2,1,0:T(8,128)(2,1)}, bf16[2,256,1024]{2,1,0:T(8,128)(2,1)}, u32[]{:S(2)}, u32[]{:S(2)}) collective-permute-start(bf16[2,256,1024]{2,1,0:T(8,128)(2,1)} %collective-permute-done.3), channel_id=1, source_target_pairs={{0,4},{1,5},{2,6},{3,7},{4,0},{5,1},{6,2},{7,3},{8,12},{9,13},{10,... | collective-permute-start | bytes 3145736 | tf_op jit(solution)/shard_map/ppermute | solution.py:774
  71.0 40.3 %collective-permute-start.6 = (bf16[256,1024]{1,0:T(8,128)(2,1)}, bf16[256,1024]{1,0:T(8,128)(2,1)S(1)}, u32[]{:S(2)}, u32[]{:S(2)}) collective-permute-start(bf16[256,1024]{1,0:T(8,128)(2,1)} %collective-permute-done.4.diag_ref), channel_id=1, source_target_pairs={{0,4},{1,5},{2,6},{3,7},{4,0},{5,1},{6,2},{7,3},{8,12},{9,13},{10,... | collective-permute-start | bytes 1572872 | tf_op jit(solution)/shard_map/ppermute | solution.py:774
  97.1 82.1 %collective-permute-start.8 = (bf16[2,256,1536]{2,1,0:T(8,128)(2,1)}, bf16[2,256,1536]{2,1,0:T(8,128)(2,1)}, u32[]{:S(2)}, u32[]{:S(2)}) collective-permute-start(bf16[2,256,1536]{2,1,0:T(8,128)(2,1)} %get-tuple-element.101), channel_id=1, source_target_pairs={{0,1},{1,0},{2,3},{3,2},{4,5},{5,4},{6,7},{7,6},{8,9},{9,8},{10,11... | collective-permute-start | bytes 4718600 | tf_op jit(solution)/shard_map/ppermute | solution.py:774
  97.1 61.4 %collective-permute-start.10 = (bf16[256,1536]{1,0:T(8,128)(2,1)}, bf16[256,1536]{1,0:T(8,128)(2,1)}, u32[]{:S(2)}, u32[]{:S(2)}) collective-permute-start(bf16[256,1536]{1,0:T(8,128)(2,1)} %get-tuple-element.105), channel_id=1, source_target_pairs={{0,3},{1,2},{2,1},{3,0},{4,7},{5,6},{6,5},{7,4},{8,11},{9,10},{10,... | collective-permute-start | bytes 2359304 | tf_op jit(solution)/shard_map/ppermute | solution.py:774
  99.0 59.9 %collective-permute-start.14 = (bf16[384,1024]{1,0:T(8,128)(2,1)}, bf16[384,1024]{1,0:T(8,128)(2,1)}, u32[]{:S(2)}, u32[]{:S(2)}) collective-permute-start(bf16[384,1024]{1,0:T(8,128)(2,1)} %collective-permute-done.13), channel_id=1, source_target_pairs={{0,4},{1,5},{2,6},{3,7},{4,0},{5,1},{6,2},{7,3},{8,12},{9,13},{10,... | collective-permute-start | bytes 2359304 | tf_op jit(solution)/shard_map/ppermute | solution.py:774
  109.0 42.1 %collective-permute-start.15 = (bf16[256,1024]{1,0:T(8,128)(2,1)}, bf16[256,1024]{1,0:T(8,128)(2,1)S(1)}, u32[]{:S(2)}, u32[]{:S(2)}) collective-permute-start(bf16[256,1024]{1,0:T(8,128)(2,1)} %get-tuple-element.109), channel_id=1, source_target_pairs={{0,2},{1,3},{2,0},{3,1},{4,6},{5,7},{6,4},{7,5},{8,10},{9,11},{10,... | collective-permute-start | bytes 1572872 | tf_op jit(solution)/shard_map/ppermute | solution.py:774
  151.2 64.8 %collective-permute-start.7 = (bf16[1024,1024]{1,0:T(8,128)(2,1)}, bf16[1024,1024]{1,0:T(8,128)(2,1)}, u32[]{:S(2)}, u32[]{:S(2)}) collective-permute-start(bf16[1024,1024]{1,0:T(8,128)(2,1)} %convolution_convert_fusion.5), channel_id=1, source_target_pairs={{0,1},{1,0},{2,3},{3,2},{4,5},{5,4},{6,7},{7,6},{8,9},{9,8},{10,11... | collective-permute-start | bytes 6291464 | tf_op jit(solution)/shard_map/ppermute | solution.py:774
  152.2 48.4 %collective-permute-start.16 = (bf16[512,1024]{1,0:T(8,128)(2,1)}, bf16[512,1024]{1,0:T(8,128)(2,1)}, u32[]{:S(2)}, u32[]{:S(2)}) collective-permute-start(bf16[512,1024]{1,0:T(8,128)(2,1)} %pad_maximum_fusion.13.mine_ref), channel_id=1, source_target_pairs={{0,1},{1,0},{2,3},{3,2},{4,5},{5,4},{6,7},{7,6},{8,9},{9,8},{10,11... | collective-permute-start | bytes 3145736 | tf_op jit(solution)/shard_map/ppermute | solution.py:774
  266.4 37.6 %collective-permute-start.18 = (bf16[768,1024]{1,0:T(8,128)(2,1)}, bf16[768,1024]{1,0:T(8,128)(2,1)S(1)}, u32[]{:S(2)}, u32[]{:S(2)}) collective-permute-start(bf16[768,1024]{1,0:T(8,128)(2,1)} %convolution_convert_fusion.7), channel_id=1, source_target_pairs={{0,2},{1,3},{2,0},{3,1},{4,6},{5,7},{6,4},{7,5},{8,10},{9,11},{10,... | collective-permute-start | bytes 4718600 | tf_op jit(solution)/shard_map/ppermute | solution.py:774
  267.9 85.4 %collective-permute-start.21 = (bf16[512,1536]{1,0:T(8,128)(2,1)}, bf16[512,1536]{1,0:T(8,128)(2,1)}, u32[]{:S(2)}, u32[]{:S(2)}) collective-permute-start(bf16[512,1536]{1,0:T(8,128)(2,1)} %convolution_convert_fusion), channel_id=1, source_target_pairs={{0,2},{1,3},{2,0},{3,1},{4,6},{5,7},{6,4},{7,5},{8,10},{9,11},{10,... | collective-permute-start | bytes 4718600 | tf_op jit(solution)/shard_map/ppermute | solution.py:774
  268.4 140.7 %collective-permute-start.20 = (bf16[512,1536]{1,0:T(8,128)(2,1)}, bf16[512,1536]{1,0:T(8,128)(2,1)}, u32[]{:S(2)}, u32[]{:S(2)}) collective-permute-start(bf16[512,1536]{1,0:T(8,128)(2,1)} %convolution_convert_fusion.2), channel_id=1, source_target_pairs={{0,2},{1,3},{2,0},{3,1},{4,6},{5,7},{6,4},{7,5},{8,10},{9,11},{10,... | collective-permute-start | bytes 4718600 | tf_op jit(solution)/shard_map/ppermute | solution.py:774
  325.2 137.6 %collective-permute-start.26 = (bf16[512,1024]{1,0:T(8,128)(2,1)}, bf16[512,1024]{1,0:T(8,128)(2,1)}, u32[]{:S(2)}, u32[]{:S(2)}) collective-permute-start(bf16[512,1024]{1,0:T(8,128)(2,1)} %convolution_convert_fusion.11), channel_id=1, source_target_pairs={{0,2},{1,3},{2,0},{3,1},{4,6},{5,7},{6,4},{7,5},{8,10},{9,11},{10,... | collective-permute-start | bytes 3145736 | tf_op jit(solution)/shard_map/ppermute | solution.py:774
  327.0 125.8 %collective-permute-start.28 = (bf16[512,1024]{1,0:T(8,128)(2,1)}, bf16[512,1024]{1,0:T(8,128)(2,1)}, u32[]{:S(2)}, u32[]{:S(2)}) collective-permute-start(bf16[512,1024]{1,0:T(8,128)(2,1)} %convolution_convert_fusion.9), channel_id=1, source_target_pairs={{0,2},{1,3},{2,0},{3,1},{4,6},{5,7},{6,4},{7,5},{8,10},{9,11},{10,... | collective-permute-start | bytes 3145736 | tf_op jit(solution)/shard_map/ppermute | solution.py:774
  360.0 91.3 %all-reduce.18.cloned.1.call-start = ((), (), s32[]{:S(2)}) async-start(), calls=%async_computation.1 | async-start | bytes 1572864 | tf_op jit(solution)/shard_map/psum | solution.py:971
  375.7 50.5 %collective-permute-start.35 = (bf16[512,1024]{1,0:T(8,128)(2,1)}, bf16[512,1024]{1,0:T(8,128)(2,1)S(1)}, u32[]{:S(2)}, u32[]{:S(2)}) collective-permute-start(bf16[512,1024]{1,0:T(8,128)(2,1)} %pad_maximum_fusion.20), channel_id=1, source_target_pairs={{0,1},{1,0},{2,3},{3,2},{4,5},{5,4},{6,7},{7,6},{8,9},{9,8},{10,11... | collective-permute-start | bytes 3145736 | tf_op jit(solution)/shard_map/ppermute | solution.py:774
  409.1 95.8 %all-reduce.20.cloned.1.call-start = ((), (), s32[]{:S(2)}) async-start(), calls=%async_computation.2 | async-start | bytes 1572864 | tf_op jit(solution)/shard_map/psum | solution.py:971
  443.9 105.0 %collective-permute-start.25 = (bf16[512,1024]{1,0:T(8,128)(2,1)}, bf16[512,1024]{1,0:T(8,128)(2,1)}, u32[]{:S(2)}, u32[]{:S(2)}) collective-permute-start(bf16[512,1024]{1,0:T(8,128)(2,1)} %convolution_convert_fusion.12), channel_id=1, source_target_pairs={{0,2},{1,3},{2,0},{3,1},{4,6},{5,7},{6,4},{7,5},{8,10},{9,11},{10,... | collective-permute-start | bytes 3145736 | tf_op jit(solution)/shard_map/ppermute | solution.py:774
  455.8 49.1 %collective-permute-start.31 = (bf16[4,64,1024]{2,1,0:T(8,128)(2,1)}, bf16[4,64,1024]{2,1,0:T(8,128)(2,1)}, u32[]{:S(2)}, u32[]{:S(2)}) collective-permute-start(bf16[4,64,1024]{2,1,0:T(8,128)(2,1)} %get-tuple-element.268), channel_id=1, source_target_pairs={{0,4},{1,5},{2,6},{3,7},{4,0},{5,1},{6,2},{7,3},{8,12},{9,13},{10,... | collective-permute-start | bytes 1572872 | tf_op jit(solution)/shard_map/ppermute | solution.py:774
  462.9 82.5 %all-reduce.22.cloned.1.call-start = ((), (), s32[]{:S(2)}) async-start(), calls=%async_computation.3 | async-start | bytes 1048576 | tf_op jit(solution)/shard_map/psum | solution.py:971
  480.1 66.8 %collective-permute-start.30 = (bf16[4,64,1024]{2,1,0:T(8,128)(2,1)}, bf16[4,64,1024]{2,1,0:T(8,128)(2,1)}, u32[]{:S(2)}, u32[]{:S(2)}) collective-permute-start(bf16[4,64,1024]{2,1,0:T(8,128)(2,1)} %get-tuple-element.270), channel_id=1, source_target_pairs={{0,4},{1,5},{2,6},{3,7},{4,0},{5,1},{6,2},{7,3},{8,12},{9,13},{10,... | collective-permute-start | bytes 1572872 | tf_op jit(solution)/shard_map/ppermute | solution.py:774
  507.0 79.4 %all-reduce.24.cloned.1.call-start = ((), (), s32[]{:S(2)}) async-start(), calls=%async_computation.4 | async-start | bytes 1048576 | tf_op jit(solution)/shard_map/psum | solution.py:971
  507.3 45.1 %collective-permute-start.42 = (bf16[256,1536]{1,0:T(8,128)(2,1)}, bf16[256,1536]{1,0:T(8,128)(2,1)}, u32[]{:S(2)}, u32[]{:S(2)}) collective-permute-start(bf16[256,1536]{1,0:T(8,128)(2,1)} %bitcast.52), channel_id=1, source_target_pairs={{0,4},{1,5},{2,6},{3,7},{4,0},{5,1},{6,2},{7,3},{8,12},{9,13},{10,... | collective-permute-start | bytes 2359304 | tf_op jit(solution)/shard_map/ppermute | solution.py:774
  545.3 42.6 %collective-permute-start.40 = (bf16[256,1024]{1,0:T(8,128)(2,1)}, bf16[256,1024]{1,0:T(8,128)(2,1)}, u32[]{:S(2)}, u32[]{:S(2)}) collective-permute-start(bf16[256,1024]{1,0:T(8,128)(2,1)} %bitcast.190), channel_id=1, source_target_pairs={{0,4},{1,5},{2,6},{3,7},{4,0},{5,1},{6,2},{7,3},{8,12},{9,13},{10,... | collective-permute-start | bytes 1572872 | tf_op jit(solution)/shard_map/ppermute | solution.py:774
  548.9 88.4 %all-reduce.26.cloned.1.call-start = ((), (), s32[]{:S(2)}) async-start(), calls=%async_computation.5 | async-start | bytes 1048576 | tf_op jit(solution)/shard_map/psum | solution.py:971
  577.5 87.9 %collective-permute-start.36 = (bf16[256,1024]{1,0:T(8,128)(2,1)}, bf16[256,1024]{1,0:T(8,128)(2,1)}, u32[]{:S(2)}, u32[]{:S(2)}) collective-permute-start(bf16[256,1024]{1,0:T(8,128)(2,1)} %slice.533), channel_id=1, source_target_pairs={{0,2},{1,3},{2,0},{3,1},{4,6},{5,7},{6,4},{7,5},{8,10},{9,11},{10,... | collective-permute-start | bytes 1572872 | tf_op jit(solution)/shard_map/ppermute | solution.py:774
  580.9 57.9 %collective-permute-start.33 = (bf16[512,1024]{1,0:T(8,128)(2,1)}, bf16[512,1024]{1,0:T(8,128)(2,1)}, u32[]{:S(2)}, u32[]{:S(2)}) collective-permute-start(bf16[512,1024]{1,0:T(8,128)(2,1)} %pad_maximum_fusion.17), channel_id=1, source_target_pairs={{0,1},{1,0},{2,3},{3,2},{4,5},{5,4},{6,7},{7,6},{8,9},{9,8},{10,11... | collective-permute-start | bytes 3145736 | tf_op jit(solution)/shard_map/ppermute | solution.py:774
  (115 other events, 1575.1 us)
Sparse Core Ops, SparseCore 0:
  360.2 45.1 all-reduce.15
  409.2 42.0 all-reduce.17
  463.0 41.8 all-reduce.19
  507.7 37.6 all-reduce.21
  549.0 37.3 all-reduce.23
  600.9 36.3 all-reduce.25

commit v4 on v3

--- a/solution.py
+++ b/solution.py
@@ -879,27 +879,28 @@
     gain_query = gains[2 * D : 2 * D + HD].reshape(1, HD)
     gain_key = gains[2 * D + HD :].reshape(1, HD)
 
-    qkv_side = over_side(tie(qkv_chip, hidden_mine))
+    gateup.peer = over_core(tie(gateup.to_core, qkv.peer))
+    qkv_side = over_side(qkv_chip)
     gateup.diagonal = over_diagonal(tie(gateup.to_diagonal, qkv_chip))
     qkv.diagonal_side = over_side(qkv.diagonal)
     qkv.chip, qkv.chip_side = qkv_chip[0], qkv_side[0]
     w_out = join_rows(out_weight, qkv_chip[1], qkv_side[1])
-    down_chip = over_chip(tie(gateup.rows, qkv.diagonal))
     gateup.chip_side = over_side(gateup.chip)
+    down_chip = over_chip(tie(gateup.rows, gateup.chip, qkv_side))
     gateup.diagonal_side = over_side(gateup.diagonal)
-    grad_far = over_chip(tie(pick(out_grad, 1 - half), gateup.chip))
-    gateup.peer = over_core(tie(gateup.to_core, qkv.peer))
+    grad_far = over_chip(tie(pick(out_grad, 1 - half), gateup.diagonal, qkv.diagonal_side))
     grad_mine = jnp.concatenate([pick(out_grad, half), grad_far], axis=0)
     grad_theirs = over_core(grad_mine)
-    down_side = over_side(down_chip)
+    down_side = over_side(tie(down_chip, gateup.chip_side))
 
     hidden, normed_low = place_rows(hidden_mine, hidden_theirs, all_targets, chunk, gain_one)
     tokens = hidden.astype(f32)
+    qkv.near = tie(qkv.near, gateup.chip)
     w_qkv = qkv.joined()
     mixed = split_product(normed_low, w_qkv, 1, 0)
     block = min(256, seq_len)
     attended, totals = attend_forward(
-        mixed, cosine, sine, gain_query, gain_key, heads, ratio, block
+        tie(mixed, gateup.diagonal), cosine, sine, gain_query, gain_key, heads, ratio, block
     )
     branch = split_product(attended, w_out, 1, 0).astype(bf16)
     middle = tokens + (branch.astype(f32) + over_core(branch).astype(f32))
@@ -965,15 +966,6 @@
         value = value.reshape(2, depth, -1, value.shape[-1])
         return add(pick(value, side), over_side(pick(value, 1 - side)))
 
-    deep_groups = [[d * 2 + x for d in range(depth)] for x in range(2)]
-
-    def depth_all(value):
-        return lax.psum(value, "dp", axis_index_groups=deep_groups)
-
-    def side_gather(value):
-        flat = value.reshape(-1, value.shape[-1])
-        return ordered(side == 0, flat, over_side(flat))
-
     token = [None]
 
     def event(*values):
@@ -988,7 +980,7 @@
     down_near, down_received = exchange(
         far_columns(inner_low, True), far_columns(inner_low, False), grad_result
     )
-    grad_inner = split_product(grad_result, w_down, 1, 1)
+    grad_inner = split_product(tie(grad_result, down_near), w_down, 1, 1)
     (grad_gate_up,) = pull_gate(grad_inner)
     grad_gate_low = grad_gate_up.astype(bf16)
     second_near, second_far = half_columns(second_low, False), half_columns(second_low, True)
@@ -1003,9 +995,8 @@
     grad_mid_part, grad_gain_two = pull_two(grad_second)
     grad_middle = grad_result.astype(f32) + grad_mid_part
     grad_branch_low = grad_middle.astype(bf16)
-    out_near, out_received = exchange(
-        far_columns(attended, True), far_columns(attended, False), grad_branch_low
-    )
+    out_far = split_product(far_columns(attended, True), grad_branch_low, 0, 0).astype(bf16)
+    out_near = split_product(far_columns(attended, False), grad_branch_low, 0, 0).astype(bf16)
     grad_att = split_product(grad_branch_low, w_out, 1, 1).astype(bf16)
     normed_near, normed_far = half_columns(normed_low, False), half_columns(normed_low, True)
 
@@ -1028,88 +1019,129 @@
         )
         return grad_part, grad_query_part[0], grad_key_part[0]
 
-    def y_step(near, received):
-        near, received = event(near, received)
-        value = add(near, received)
+    levels = [(side, over_side)]
+    near_step = 1
+    while near_step < depth:
+        levels.append(
+            (
+                copy // 2 // near_step % 2,
+                lambda value, step=near_step: permute(
+                    value, lambda d, g: ((d // 2 ^ step) * 2 + d % 2, g)
+                ),
+            )
+        )
+        near_step *= 2
+
+    class Summed:
+        def __init__(self, near, received):
+            near, received = event(near, received)
+            self.value = swap_rows(near, received)
+            passed(self.value)
+            self.level = 0
+            self.down = True
+            self.send_half()
+
+        def send_half(self):
+            bit, move = levels[self.level]
+            halves = self.value.reshape(2, -1, self.value.shape[-1])
+            self.kept = pick(halves, bit)
+            self.received = move(pick(halves, 1 - bit))
+
+        def send_back(self):
+            self.received = levels[self.level][1](self.value)
+
+        def step(self):
+            if self.down:
+                self.value = add(*event(self.kept, self.received))
+                self.level += 1
+                passed(self.value)
+                if self.level < len(levels):
+                    self.send_half()
+                    return
+                self.down = False
+            else:
+                value, received = event(self.value, self.received)
+                self.value = ordered(levels[self.level][0] == 0, value, received)
+                passed(self.value)
+            self.level -= 1
+            if self.level >= 0:
+                self.send_back()
+
+    def all_sum(near, received):
+        value = add(*event(near, received))
         passed(value)
-        return value
-
-    def swap_step(near, received):
-        near, received = event(near, received)
-        value = swap_rows(near, received)
-        passed(value)
-        return value
-
-    def x_parts(value):
-        value = value.reshape(2, depth, -1, value.shape[-1])
-        return pick(value, side), over_side(pick(value, 1 - side))
-
-    def x_step(kept_received):
-        value = add(*event(*kept_received))
-        passed(value)
-        return depth_all(value)
-
-    def back_step(value):
-        (value,) = event(value)
-        flat = value.reshape(-1, value.shape[-1])
-        received = over_side(flat)
-        passed(flat)
-        return flat, received
-
-    def last_step(flat_received):
-        flat, received = flat_received
-        return ordered(side == 0, flat, received)
-
-    down_x = x_parts(y_step(down_near, tie(down_received, grad_att)))
-    grad_att = tie(grad_att, down_x[0])
+        return lax.psum(value, "dp")
+
+    down_sum = all_sum(down_near, tie(down_received, grad_att))
+    grad_att = tie(grad_att, token[0])
     back_0 = backward_part(0, grad_att)
     qkv_0 = exchange(normed_far, normed_near, back_0[0])
-    down_z = x_step((down_x[0], tie(down_x[1], qkv_0[0])))
-    grad_att = tie(grad_att, token[0])
-    back_1 = backward_part(1, grad_att)
-    far_1 = split_product(normed_far, back_1[0], 0, 0).astype(bf16)
-    near_1 = split_product(normed_near, back_1[0], 0, 0).astype(bf16)
-    gateup_0 = swap_step(gateup_sent[0][0], tie(gateup_sent[0][1], near_1))
-    gateup_0x = x_parts(gateup_0)
+    back_1 = backward_part(1, tie(grad_att, qkv_0[0]))
+    qkv_1 = exchange(normed_far, normed_near, back_1[0])
+    out_far = tie(out_far, qkv_1[0])
+    out_received = over_chip(tie(out_far, gateup_sent[0][1]))
+    gateup_0 = Summed(gateup_sent[0][0], tie(gateup_sent[0][1], qkv_1[0]))
     normed_part = split_product(
         tie(back_0[0], token[0]), w_qkv[:, : 2 * wide], 1, 1
     ) + split_product(tie(back_1[0], token[0]), w_qkv[:, 2 * wide :], 1, 1)
     normed_part = normed_part.astype(bf16)
-    down_b = back_step(tie(down_z, normed_part))
-    gateup_0z = x_step(gateup_0x)
-    gateup_1 = swap_step(*gateup_sent[1])
-    received_1 = over_chip(tie(far_1, token[0]))
-    gateup_1x = x_parts(gateup_1)
+    gateup_0.received = tie(gateup_0.received, normed_part)
+    gateup_0.step()
+    gateup_1 = Summed(*gateup_sent[1])
     grad_normed = share_rows(normed_part)
     own_tokens = take_rows(hidden, own_targets, chunk).astype(f32)
     unused, pull_one = jax.vjp(rms_scale, own_tokens, gain_one)
     grad_token_part, grad_gain_one = pull_one(grad_normed)
-    input_rows = take_rows(grad_middle, own_targets, chunk) + grad_token_part
-    down_sum = last_step(down_b)
-    gateup_0b = back_step(gateup_0z)
-    out_x = x_parts(y_step(out_near, out_received))
-    gateup_1z = x_step(gateup_1x)
-    gateup_0sum = last_step(gateup_0b)
-    qkv_0x = x_parts(swap_step(*qkv_0))
-    gateup_1b = back_step(gateup_1z)
-    out_z = x_step(out_x)
-    out_b = back_step(out_z)
-    qkv_0z = x_step(qkv_0x)
-    qkv_1x = x_parts(swap_step(near_1, received_1))
+    input_rows = (take_rows(grad_middle, own_targets, chunk) + grad_token_part).astype(bf16)
+    gateup_0.step()
+    gateup_1.step()
+    gateup_0.step()
+    summed_0 = Summed(*qkv_0)
+    gateup_0.step()
+    gateup_1.step()
+    (down_sum,) = event(down_sum)
+    passed(down_sum)
+    summed_0.step()
+    gateup_0.step()
+    gateup_1.step()
+    summed_1 = Summed(*qkv_1)
+    summed_0.step()
+    gateup_1.step()
+    gateup_0.step()
+    summed_1.step()
+    out_sum = all_sum(out_near, out_received)
+    summed_0.step()
+    gateup_1.step()
+    summed_1.step()
+    summed_0.step()
+    gateup_1.step()
+    summed_1.step()
+    summed_0.step()
+    counted = jnp.where(rank == 0, 1.0, 0.0).astype(f32)
+    total_gains = jnp.concatenate(
+        [
+            grad_gain_one,
+            grad_gain_two * counted,
+            back_0[1] + back_1[1],
+            back_0[2] + back_1[2],
+        ]
+    )
     layer_out = to_stored(
         take_rows(middle, own_targets, chunk) + share_rows(tie(result_part, token[0]))
     )
     input_grad = to_stored(tie(input_rows, token[0]))
-    gateup_1sum = last_step(gateup_1b)
-    qkv_0b = back_step(qkv_0z)
-    qkv_1z = x_step(qkv_1x)
-    out_sum = last_step(out_b)
-    qkv_1b = back_step(qkv_1z)
-    qkv_0sum = last_step(qkv_0b)
-    qkv_1sum = last_step(qkv_1b)
-    gateup_sums = [gateup_0sum, gateup_1sum]
-    qkv_sums = [qkv_0sum, qkv_1sum]
-    gain_parts = [back_0[1:], back_1[1:]]
+    for move in (over_core, over_chip):
+        total_gains = total_gains + move(tie(total_gains, token[0]))
+    summed_1.step()
+    for bit, move in levels:
+        total_gains = total_gains + move(tie(total_gains, token[0]))
+    summed_0.step()
+    summed_1.step()
+    for summed in (gateup_0, gateup_1, summed_0, summed_1):
+        while summed.level >= 0:
+            summed.step()
+    gateup_sums = [gateup_0.value, gateup_1.value]
+    qkv_sums = [summed_0.value, summed_1.value]
     total_down = down_sum.astype(f32)
     total_out = out_sum.astype(f32)
 
@@ -1139,20 +1171,6 @@
         + [blocked[:, (ratio + 1) * HD :] for blocked in head_blocks],
         axis=1,
     ).astype(f32)
-    counted = jnp.where(rank == 0, 1.0, 0.0).astype(f32)
-    total_gains = jnp.concatenate(
-        [
-            grad_gain_one,
-            grad_gain_two * counted,
-            sum(pair[0] for pair in gain_parts),
-            sum(pair[1] for pair in gain_parts),
-        ]
-    )
-    total_gains = total_gains + over_core(total_gains)
-    total_gains = total_gains + over_chip(total_gains)
-    total_gains = total_gains + over_side(total_gains)
-    total_gains = lax.psum(tie(total_gains, token[0]), "dp", axis_index_groups=deep_groups)
-    gain_rows = gain_weight.shape[0]
     total_gain = lax.dynamic_slice_in_dim(total_gains, member * gain_rows, gain_rows, 0)
 
     out_fan = H * HD * 8 // seq_len

time: 694 us -> 631 us (0.909)
  waiting for transfers between devices: 253 us -> 206 us
  starting transfers between devices: 43.3 us -> 63 us
  blocking collectives: 18 us -> 0 us
  other arithmetic: 116 us -> 108 us
    psum x6 -> x2, waiting for transfers between devices: 124 us -> 4.55 us  [all_sum(): return lax.psum(value, 'dp')]
    ppermute x47 -> x61, waiting for transfers between devices: 129 us -> 202 us  [permute(): return lax.ppermute(value, ALL, pairs)]
    ppermute x47 -> x61, starting transfers between devices: 42.1 us -> 62.7 us  [permute(): return lax.ppermute(value, ALL, pairs)]
    psum x1 -> x0, blocking collectives: 18 us -> none  [paired_shards(): lax.psum(tie(total_gains, token[0]), 'dp', axis_index_groups=deep_groups)]
    convert_element_type x12 -> x18, other arithmetic: 17.8 us -> 10.6 us  [add(): return total.astype(bf16)]
    unnamed x231 -> x239, local copies, waits for them, and re-layouts: 28.1 us -> 28.2 us
  transfers between devices with their start and end apart: 53 -> 63, of which waited for: 18 -> 32; matrix products, arithmetic and copies ran while one was open for 26% -> 25% of each run, Pallas kernels for 14% -> 12%
where the time goes in v4:
time: 631 us; the launch traced here: 622 us
  waiting for transfers between devices  206 us (33%)
  other arithmetic  108 us (17%)
  Pallas kernels  96 us (15%)
  matrix products  80.4 us (13%)
  starting transfers between devices  63 us (10%)
  local copies, waits for them, and re-layouts  46 us (7%)
  between operations  21.9 us (3%)
    ppermute x61, waiting for transfers between devices, permute(): return lax.ppermute(value, ALL, pairs)  202 us
    dot_general x21, matrix products, split_product(): lax.dot_general(left, right, (((left_dim,), (right_dim,)), ((), ())), pre...  80.4 us
    ppermute x61, starting transfers between devices, permute(): return lax.ppermute(value, ALL, pairs)  62.7 us
    pallas_call x2, Pallas kernels, attend_backward(): pl.pallas_call(kernel, grid=(heads,), in_specs=[pl.BlockSpec((rows, wide)...  35.7 us
    sub x5, other arithmetic, adam_step(): return (weight - rate * (ratio + decay * weight), moment_new, square_new)  31.3 us
    unnamed x239, local copies, waits for them, and re-layouts  28.2 us
    pallas_call x1, Pallas kernels, attend_forward(): pl.pallas_call(kernel, grid=(heads,), in_specs=[pl.BlockSpec((rows, wide)...  22.2 us
    pallas_call x2, Pallas kernels, cut_columns(): pl.pallas_call(kernel, out_shape=[single, single, jax.ShapeDtypeStruct((2...  14.1 us
  transfers between devices with their start and end apart: 63, of which 32 were waited for; matrix products, arithmetic and copies ran while one was open for 25% of the time, Pallas kernels for 12%

profile of v4, /device:TPU:0, one launch (start us, length us, event | category | flops | bytes accessed | tf_op | source)
XLA Modules:
  0.0 621.6 jit_solution(853668473697515450)
XLA Ops:
  13.3 6.1 cut_columns.2
  20.6 6.4 %collective-permute-done = bf16[272,1024]{1,0:T(8,128)(2,1)} collective-permute-done((bf16[272,1024]{1,0:T(8,128)(2,1)}, bf16[272,1024]{1,0:T(8,128)(2,1)}, u32[]{:S(2)}, u32[]{:S(2)}) %collective-permute-start) | collective-permute-done | bytes 557088 | tf_op jit(solution)/shard_map/ppermute | solution.py:774
  32.2 8.0 %cut_columns.3 = (bf16[256,1536]{1,0:T(8,128)(2,1)}, bf16[256,1536]{1,0:T(8,128)(2,1)}, bf16[2,256,1536]{2,1,0:T(8,128)(2,1)}, bf16[256,1536]{1,0:T(8,128)(2,1)S...) custom-call(s32[3]{0:T(128)S(1)} %pad_add_fusion.at_ref, f32[256,6144]{1,0:T(8,128)} %refs_1_.1, ...), custom_call_target="tpu_custom_call" | custom-call | flops 1000000 | bytes 100000 | tf_op jit(solution)/shard_map/cut_columns/pallas_call | solution.py:437
  52.9 7.4 %collective-permute-done.5.diag_ref = bf16[256,1024]{1,0:T(8,128)(2,1)} collective-permute-done((bf16[256,1024]{1,0:T(8,128)(2,1)}, bf16[256,1024]{1,0:T(8,128)(2,1)}, u32[]{:S(2)}, u32[]{:S(2)}) %collective-permute-start.5) | collective-permute-done | bytes 524320 | tf_op jit(solution)/shard_map/ppermute | solution.py:774
  61.8 14.9 %collective-permute-done.2.chip_ref = bf16[256,1536]{1,0:T(8,128)(2,1)} collective-permute-done((bf16[256,1536]{1,0:T(8,128)(2,1)}, bf16[256,1536]{1,0:T(8,128)(2,1)}, u32[]{:S(2)}, u32[]{:S(2)}) %collective-permute-start.2) | collective-permute-done | bytes 786464 | tf_op jit(solution)/shard_map/ppermute | solution.py:774
  78.6 7.0 %place_rows.2 = (bf16[1024,1024]{1,0:T(8,128)(2,1)}, bf16[1024,1024]{1,0:T(8,128)(2,1)}) custom-call(s32[8]{0:T(128)} %copy-done.78, bf16[544,1024]{1,0:T(8,128)(2,1)} %pad_maximum_fusion.12.mine_ref, bf16[544,1024]{1,0:T(8,128)(2,1)} %collective-permute-done.1.theirs_ref, f32[1,1024]{1,0:T(1,128)} %bitcast.199), custom_call_target="tpu_custom_call" | custom-call | flops 1000000 | bytes 100000 | tf_op jit(solution)/shard_map/place_rows/pallas_call | solution.py:375
  92.3 9.0 %fusion.113.mixed_ref = f32[1024,2048]{1,0:T(8,128)} fusion(bf16[1024,1024]{1,0:T(8,128)(2,1)S(1)} %copy-done.89, bf16[1024,2048]{1,0:T(8,128)(2,1)} %join_columns.2), kind=kOutput, calls=%fused_computation.426 | convolution fusion | flops 4294967296 | bytes 14680064 | tf_op jit(solution)/shard_map/dot_general | solution.py:339
  101.2 22.2 %attend_forward.1 = (bf16[1024,1024]{1,0:T(8,128)(2,1)S(1)}, f32[1024,512]{1,0:T(8,128)S(1)}) custom-call(f32[1024,2048]{1,0:T(8,128)} %fusion.113.mixed_ref, f32[1024,128]{1,0:T(8,128)S(1)} %pad_maximum_fusion.30.cos_ref, f32[1024,128]{1,0:T(8,128)S(1)} %pad_maximum_fusion.31.sin_ref, f32[1,128]{1,0:T(1,128)S(1)} %get-tuple-element.405.gq_ref, ...), custom_call_target="tpu_custom_call" | custom-call | flops 1000000 | bytes 100000 | tf_op jit(solution)/shard_map/attend_forward/pallas_call | solution.py:578
  132.4 11.3 %collective-permute-done.15 = bf16[256,1024]{1,0:T(8,128)(2,1)S(1)} collective-permute-done((bf16[256,1024]{1,0:T(8,128)(2,1)S(1)}, bf16[256,1024]{1,0:T(8,128)(2,1)S(1)}, u32[]{:S(2)}, u32[]{:S(2)}) %collective-permute-start.15) | collective-permute-done | bytes 524320 | tf_op jit(solution)/shard_map/ppermute | solution.py:774
  151.9 7.8 %collective-permute-done.13 = bf16[384,1024]{1,0:T(8,128)(2,1)} collective-permute-done((bf16[384,1024]{1,0:T(8,128)(2,1)S(1)}, bf16[384,1024]{1,0:T(8,128)(2,1)}, u32[]{:S(2)}, u32[]{:S(2)}) %collective-permute-start.13) | collective-permute-done | bytes 786464 | tf_op jit(solution)/shard_map/ppermute | solution.py:774
  176.7 6.5 %place_rows.3 = bf16[1024,1024]{1,0:T(8,128)(2,1)} custom-call(s32[8]{0:T(128)} %copy-done.78, bf16[512,1024]{1,0:T(8,128)(2,1)} %pad_maximum_fusion.14.mine_ref, bf16[512,1024]{1,0:T(8,128)(2,1)} %collective-permute-done.16.theirs_ref), custom_call_target="tpu_custom_call" | custom-call | flops 1000000 | bytes 100000 | tf_op jit(solution)/shard_map/place_rows/pallas_call | solution.py:375
  194.0 6.7 %fusion.114 = f32[1024,3072]{1,0:T(8,128)S(1)} fusion(bf16[1024,1024]{1,0:T(8,128)(2,1)S(1)} %multiply_convert_fusion, bf16[1024,3072]{1,0:T(8,128)(2,1)S(1)} %bitcast.175), kind=kOutput, calls=%fused_computation.427 | convolution fusion | flops 6442450944 | bytes 20971520 | tf_op jit(solution)/shard_map/dot_general | solution.py:339
  205.4 6.7 %fusion.57 = f32[1024,1536]{1,0:T(8,128)} fusion(bf16[1024,1024]{1,0:T(8,128)(2,1)S(1)} %copy-done.27, bf16[384,1024]{1,0:T(8,128)(2,1)S(1)} %get-tuple-element.325, bf16[384,1024]{1,0:T(8,128)(2,1)S(1)} %get-tuple-element.324, bf16[768,1024]{1,0:T(8,128)(2,1)S(1)} %copy-done.53), kind=kOutput, calls=%fused_computation.146 | convolution fusion | flops 3230662656 | bytes 11534336 | tf_op jit(solution)/shard_map/dot_general | solution.py:339
  212.1 7.1 %slice_multiply_fusion.3 = (f32[1024,384]{1,0:T(8,128)}, f32[1024,384]{1,0:T(8,128)}, f32[1024,384]{1,0:T(8,128)}, f32[1024,384]{1,0:T(8,128)}, f32[1024,384]{1,...) fusion(f32[1024,1536]{1,0:T(8,128)} %fusion.57, f32[1024,3072]{1,0:T(8,128)S(1)} %fusion.114), kind=kLoop, calls=%fused_computation.135 | loop fusion | flops 18087936 | bytes 29884416 | tf_op jit(solution)/shard_map/transpose(jvp())/mul | solution.py:917
  228.6 9.0 %convolution_convert_fusion.6 = bf16[1024,1024]{1,0:T(8,128)(2,1)S(1)} fusion(bf16[1024,3072]{1,0:T(8,128)(2,1)S(1)} %add_convert_fusion, bf16[1024,3072]{1,0:T(8,128)(2,1)} %join_columns.3), kind=kOutput, calls=%fused_computation.87 | convolution fusion | flops 6443499520 | bytes 14680064 | tf_op jit(solution)/shard_map/dot_general | solution.py:339
  257.8 6.1 fusion.34
  271.3 12.7 %collective-permute-done.18 = bf16[768,1024]{1,0:T(8,128)(2,1)S(1)} collective-permute-done((bf16[768,1024]{1,0:T(8,128)(2,1)}, bf16[768,1024]{1,0:T(8,128)(2,1)S(1)}, u32[]{:S(2)}, u32[]{:S(2)}) %collective-permute-start.18) | collective-permute-done | bytes 1572896 | tf_op jit(solution)/shard_map/ppermute | solution.py:774
  285.9 17.8 %attend_backward.2 = (bf16[1024,1024]{1,0:T(8,128)(2,1)S(1)}, f32[1,128]{1,0:T(1,128)S(1)}, f32[1,128]{1,0:T(1,128)S(1)}) custom-call(f32[1024,2048]{1,0:T(8,128)} %fusion.113.mixed_ref, f32[1024,128]{1,0:T(8,128)S(1)} %pad_maximum_fusion.30.cos_ref, f32[1024,128]{1,0:T(8,128)S(1)} %pad_maximum_fusion.31.sin_ref, f32[1,128]{1,0:T(1,128)S(1)} %get-tuple-element.405.gq_ref, ...), custom_call_target="tpu_custom_call" | custom-call | flops 1000000 | bytes 100000 | tf_op jit(solution)/shard_map/attend_backward/pallas_call | solution.py:698
  306.0 17.8 %attend_backward.3 = (bf16[1024,1024]{1,0:T(8,128)(2,1)S(1)}, f32[1,128]{1,0:T(1,128)S(1)}, f32[1,128]{1,0:T(1,128)S(1)}) custom-call(f32[1024,2048]{1,0:T(8,128)} %fusion.113.mixed_ref, f32[1024,128]{1,0:T(8,128)S(1)} %pad_maximum_fusion.30.cos_ref, f32[1024,128]{1,0:T(8,128)S(1)} %pad_maximum_fusion.31.sin_ref, f32[1,128]{1,0:T(1,128)S(1)} %get-tuple-element.405.gq_ref, ...), custom_call_target="tpu_custom_call" | custom-call | flops 1000000 | bytes 100000 | tf_op jit(solution)/shard_map/attend_backward/pallas_call | solution.py:698
  350.2 14.9 %collective-permute-done.22 = bf16[256,1536]{1,0:T(8,128)(2,1)S(1)} collective-permute-done((bf16[256,1536]{1,0:T(8,128)(2,1)S(1)}, bf16[256,1536]{1,0:T(8,128)(2,1)S(1)}, u32[]{:S(2)}, u32[]{:S(2)}) %collective-permute-start.22) | collective-permute-done | bytes 786464 | tf_op jit(solution)/shard_map/ppermute | solution.py:774
  383.4 17.6 %collective-permute-done.27 = bf16[256,1536]{1,0:T(8,128)(2,1)S(1)} collective-permute-done((bf16[256,1536]{1,0:T(8,128)(2,1)S(1)}, bf16[256,1536]{1,0:T(8,128)(2,1)S(1)}, u32[]{:S(2)}, u32[]{:S(2)}) %collective-permute-start.27) | collective-permute-done | bytes 786464 | tf_op jit(solution)/shard_map/ppermute | solution.py:774
  406.1 13.7 %collective-permute-done.31 = bf16[64,1536]{1,0:T(8,128)(2,1)S(1)} collective-permute-done((bf16[64,1536]{1,0:T(8,128)(2,1)S(1)}, bf16[64,1536]{1,0:T(8,128)(2,1)S(1)}, u32[]{:S(2)}, u32[]{:S(2)}) %collective-permute-start.31) | collective-permute-done | bytes 196640 | tf_op jit(solution)/shard_map/ppermute | solution.py:774
  420.3 16.2 %collective-permute-done.30 = bf16[128,1536]{1,0:T(8,128)(2,1)S(1)} collective-permute-done((bf16[128,1536]{1,0:T(8,128)(2,1)S(1)}, bf16[128,1536]{1,0:T(8,128)(2,1)S(1)}, u32[]{:S(2)}, u32[]{:S(2)}) %collective-permute-start.30) | collective-permute-done | bytes 393248 | tf_op jit(solution)/shard_map/ppermute | solution.py:774
  447.5 7.2 %multiply_subtract_fusion.2 = (f32[768,1024]{1,0:T(8,128)}, f32[768,1024]{1,0:T(8,128)}, f32[768,1024]{1,0:T(8,128)}) fusion(f32[768,1024]{1,0:T(8,128)S(1)} %copy-done.23, bf16[768,1024]{1,0:T(8,128)(2,1)} %all-reduce.12.cloned.1.call-done, f32[768,1024]{1,0:T(8,128)} %param.33, f32[768,1024]{1,0:T(8,128)} %param.34), kind=kLoop, calls=%fused_computation.38 | loop fusion | flops 12582912 | bytes 20447232 | tf_op jit(solution)/shard_map/sub | solution.py:93
  468.1 8.1 %collective-permute-done.41 = bf16[64,1536]{1,0:T(8,128)(2,1)S(1)} collective-permute-done((bf16[64,1536]{1,0:T(8,128)(2,1)S(1)}, bf16[64,1536]{1,0:T(8,128)(2,1)S(1)}, u32[]{:S(2)}, u32[]{:S(2)}) %collective-permute-start.41) | collective-permute-done | bytes 196640 | tf_op jit(solution)/shard_map/ppermute | solution.py:774
  481.2 8.2 %collective-permute-done.39 = bf16[256,1024]{1,0:T(8,128)(2,1)S(1)} collective-permute-done((bf16[256,1024]{1,0:T(8,128)(2,1)S(1)}, bf16[256,1024]{1,0:T(8,128)(2,1)S(1)}, u32[]{:S(2)}, u32[]{:S(2)}) %collective-permute-start.39) | collective-permute-done | bytes 524320 | tf_op jit(solution)/shard_map/ppermute | solution.py:774
  508.8 6.7 %collective-permute-done.47 = bf16[256,1536]{1,0:T(8,128)(2,1)S(1)} collective-permute-done((bf16[256,1536]{1,0:T(8,128)(2,1)S(1)}, bf16[256,1536]{1,0:T(8,128)(2,1)S(1)}, u32[]{:S(2)}, u32[]{:S(2)}) %collective-permute-start.47) | collective-permute-done | bytes 786464 | tf_op jit(solution)/shard_map/ppermute | solution.py:774
  515.7 6.9 %collective-permute-done.46 = bf16[64,1024]{1,0:T(8,128)(2,1)S(1)} collective-permute-done((bf16[64,1024]{1,0:T(8,128)(2,1)S(1)}, bf16[64,1024]{1,0:T(8,128)(2,1)S(1)}, u32[]{:S(2)}, u32[]{:S(2)}) %collective-permute-start.46) | collective-permute-done | bytes 131104 | tf_op jit(solution)/shard_map/ppermute | solution.py:774
  557.6 10.9 %multiply_subtract_fusion = (f32[256,6144]{1,0:T(8,128)}, f32[256,6144]{1,0:T(8,128)}, f32[256,6144]{1,0:T(8,128)}) fusion(f32[256,6144]{1,0:T(8,128)S(1)} %bitcast.171, bf16[256,6144]{1,0:T(8,128)(2,1)} %slice_dynamic-update-slice_fusion, f32[256,6144]{1,0:T(8,128)S(1)} %bitcast.173, f32[256,6144]{1,0:T(8,128)} %param.31), kind=kLoop, calls=%fused_computation.5 | loop fusion | flops 25165824 | bytes 40894464 | tf_op jit(solution)/shard_map/sub | solution.py:93
  572.0 10.5 %collective-permute-done.54 = bf16[128,1024]{1,0:T(8,128)(2,1)S(1)} collective-permute-done((bf16[128,1024]{1,0:T(8,128)(2,1)}, bf16[128,1024]{1,0:T(8,128)(2,1)S(1)}, u32[]{:S(2)}, u32[]{:S(2)}) %collective-permute-start.54) | collective-permute-done | bytes 262176 | tf_op jit(solution)/shard_map/ppermute | solution.py:774
  587.8 6.7 %multiply_subtract_fusion.3 = (f32[512,1024]{1,0:T(8,128)}, f32[512,1024]{1,0:T(8,128)}, f32[512,1024]{1,0:T(8,128)}) fusion(f32[512,1024]{1,0:T(8,128)S(1)} %copy-done.3, bf16[512,1024]{1,0:T(8,128)(2,1)} %all-reduce.14.cloned.1.call-done, f32[512,1024]{1,0:T(8,128)} %param.27, f32[512,1024]{1,0:T(8,128)} %param.28), kind=kLoop, calls=%fused_computation.70 | loop fusion | flops 8388608 | bytes 13631488 | tf_op jit(solution)/shard_map/sub | solution.py:93
  604.5 5.8 multiply_subtract_fusion.1
  (511 shorter events, 275.8 us)
Async XLA Ops:
  7.2 431.2 %all-reduce.12.cloned.1.call-start = ((), (), s32[]{:S(2)}) async-start(), calls=%async_computation | async-start | bytes 3145728 | tf_op jit(solution)/shard_map/psum | solution.py:1073
  20.6 28.9 %collective-permute-start.4 = (bf16[2,256,1024]{2,1,0:T(8,128)(2,1)}, bf16[2,256,1024]{2,1,0:T(8,128)(2,1)}, u32[]{:S(2)}, u32[]{:S(2)}) collective-permute-start(bf16[2,256,1024]{2,1,0:T(8,128)(2,1)} %pad_maximum_fusion.13), channel_id=1, source_target_pairs={{0,2},{1,3},{2,0},{3,1},{4,6},{5,7},{6,4},{7,5},{8,10},{9,11},{10,... | collective-permute-start | bytes 3145736 | tf_op jit(solution)/shard_map/ppermute | solution.py:774
  29.9 47.1 %collective-permute-start.1 = (bf16[544,1024]{1,0:T(8,128)(2,1)}, bf16[544,1024]{1,0:T(8,128)(2,1)}, u32[]{:S(2)}, u32[]{:S(2)}) collective-permute-start(bf16[544,1024]{1,0:T(8,128)(2,1)} %pad_maximum_fusion.12.mine_ref), channel_id=1, source_target_pairs={{0,1},{1,0},{2,3},{3,2},{4,5},{5,4},{6,7},{7,6},{8,9},{9,8},{10,11... | collective-permute-start | bytes 3342344 | tf_op jit(solution)/shard_map/ppermute | solution.py:774
  29.9 57.4 %collective-permute-start.3 = (bf16[2,256,1024]{2,1,0:T(8,128)(2,1)}, bf16[2,256,1024]{2,1,0:T(8,128)(2,1)}, u32[]{:S(2)}, u32[]{:S(2)}) collective-permute-start(bf16[2,256,1024]{2,1,0:T(8,128)(2,1)} %get-tuple-element.136), channel_id=1, source_target_pairs={{0,1},{1,0},{2,3},{3,2},{4,5},{5,4},{6,7},{7,6},{8,9},{9,8},{10,11... | collective-permute-start | bytes 3145736 | tf_op jit(solution)/shard_map/ppermute | solution.py:774
  30.5 29.9 %collective-permute-start.5 = (bf16[256,1024]{1,0:T(8,128)(2,1)}, bf16[256,1024]{1,0:T(8,128)(2,1)}, u32[]{:S(2)}, u32[]{:S(2)}) collective-permute-start(bf16[256,1024]{1,0:T(8,128)(2,1)} %get-tuple-element.130), channel_id=1, source_target_pairs={{0,3},{1,2},{2,1},{3,0},{4,7},{5,6},{6,5},{7,4},{8,11},{9,10},{10,... | collective-permute-start | bytes 1572872 | tf_op jit(solution)/shard_map/ppermute | solution.py:774
  42.1 34.6 %collective-permute-start.2 = (bf16[256,1536]{1,0:T(8,128)(2,1)}, bf16[256,1536]{1,0:T(8,128)(2,1)}, u32[]{:S(2)}, u32[]{:S(2)}) collective-permute-start(bf16[256,1536]{1,0:T(8,128)(2,1)} %get-tuple-element.133), channel_id=1, source_target_pairs={{0,2},{1,3},{2,0},{3,1},{4,6},{5,7},{6,4},{7,5},{8,10},{9,11},{10,... | collective-permute-start | bytes 2359304 | tf_op jit(solution)/shard_map/ppermute | solution.py:774
  49.5 36.1 %collective-permute-start.6 = (bf16[2,256,1024]{2,1,0:T(8,128)(2,1)}, bf16[2,256,1024]{2,1,0:T(8,128)(2,1)}, u32[]{:S(2)}, u32[]{:S(2)}) collective-permute-start(bf16[2,256,1024]{2,1,0:T(8,128)(2,1)} %collective-permute-done.4), channel_id=1, source_target_pairs={{0,4},{1,5},{2,6},{3,7},{4,0},{5,1},{6,2},{7,3},{8,12},{9,13},{10,... | collective-permute-start | bytes 3145736 | tf_op jit(solution)/shard_map/ppermute | solution.py:774
  60.3 27.1 %collective-permute-start.7 = (bf16[256,1024]{1,0:T(8,128)(2,1)}, bf16[256,1024]{1,0:T(8,128)(2,1)S(1)}, u32[]{:S(2)}, u32[]{:S(2)}) collective-permute-start(bf16[256,1024]{1,0:T(8,128)(2,1)} %collective-permute-done.5.diag_ref), channel_id=1, source_target_pairs={{0,4},{1,5},{2,6},{3,7},{4,0},{5,1},{6,2},{7,3},{8,12},{9,13},{10,... | collective-permute-start | bytes 1572872 | tf_op jit(solution)/shard_map/ppermute | solution.py:774
  76.8 24.5 %collective-permute-start.8 = (bf16[256,1536]{1,0:T(8,128)(2,1)}, bf16[256,1536]{1,0:T(8,128)(2,1)}, u32[]{:S(2)}, u32[]{:S(2)}) collective-permute-start(bf16[256,1536]{1,0:T(8,128)(2,1)} %get-tuple-element.139), channel_id=1, source_target_pairs={{0,3},{1,2},{2,1},{3,0},{4,7},{5,6},{6,5},{7,4},{8,11},{9,10},{10,... | collective-permute-start | bytes 2359304 | tf_op jit(solution)/shard_map/ppermute | solution.py:774
  127.2 61.1 %collective-permute-start.9 = (bf16[1024,1024]{1,0:T(8,128)(2,1)}, bf16[1024,1024]{1,0:T(8,128)(2,1)}, u32[]{:S(2)}, u32[]{:S(2)}) collective-permute-start(bf16[1024,1024]{1,0:T(8,128)(2,1)} %convolution_convert_fusion.5), channel_id=1, source_target_pairs={{0,1},{1,0},{2,3},{3,2},{4,5},{5,4},{6,7},{7,6},{8,9},{9,8},{10,11... | collective-permute-start | bytes 6291464 | tf_op jit(solution)/shard_map/ppermute | solution.py:774
  129.1 41.0 %collective-permute-start.10 = (bf16[2,256,1536]{2,1,0:T(8,128)(2,1)}, bf16[2,256,1536]{2,1,0:T(8,128)(2,1)}, u32[]{:S(2)}, u32[]{:S(2)}) collective-permute-start(bf16[2,256,1536]{2,1,0:T(8,128)(2,1)} %get-tuple-element.145), channel_id=1, source_target_pairs={{0,1},{1,0},{2,3},{3,2},{4,5},{5,4},{6,7},{7,6},{8,9},{9,8},{10,11... | collective-permute-start | bytes 4718600 | tf_op jit(solution)/shard_map/ppermute | solution.py:774
  130.9 28.8 %collective-permute-start.13 = (bf16[384,1024]{1,0:T(8,128)(2,1)S(1)}, bf16[384,1024]{1,0:T(8,128)(2,1)}, u32[]{:S(2)}, u32[]{:S(2)}) collective-permute-start(bf16[384,1024]{1,0:T(8,128)(2,1)S(1)} %copy-done.20), channel_id=1, source_target_pairs={{0,2},{1,3},{2,0},{3,1},{4,6},{5,7},{6,4},{7,5},{8,10},{9,11},{10,... | collective-permute-start | bytes 2359304 | tf_op jit(solution)/shard_map/ppermute | solution.py:774
  144.7 32.0 %collective-permute-start.16 = (bf16[512,1024]{1,0:T(8,128)(2,1)}, bf16[512,1024]{1,0:T(8,128)(2,1)}, u32[]{:S(2)}, u32[]{:S(2)}) collective-permute-start(bf16[512,1024]{1,0:T(8,128)(2,1)} %pad_maximum_fusion.14.mine_ref), channel_id=1, source_target_pairs={{0,1},{1,0},{2,3},{3,2},{4,5},{5,4},{6,7},{7,6},{8,9},{9,8},{10,11... | collective-permute-start | bytes 3145736 | tf_op jit(solution)/shard_map/ppermute | solution.py:774
  150.2 20.7 %collective-permute-start.12 = (bf16[256,1536]{1,0:T(8,128)(2,1)}, bf16[256,1536]{1,0:T(8,128)(2,1)}, u32[]{:S(2)}, u32[]{:S(2)}) collective-permute-start(bf16[256,1536]{1,0:T(8,128)(2,1)} %collective-permute-done.8.diag_ref), channel_id=1, source_target_pairs={{0,4},{1,5},{2,6},{3,7},{4,0},{5,1},{6,2},{7,3},{8,12},{9,13},{10,... | collective-permute-start | bytes 2359304 | tf_op jit(solution)/shard_map/ppermute | solution.py:774
  159.7 26.9 %collective-permute-start.14 = (bf16[384,1024]{1,0:T(8,128)(2,1)}, bf16[384,1024]{1,0:T(8,128)(2,1)}, u32[]{:S(2)}, u32[]{:S(2)}) collective-permute-start(bf16[384,1024]{1,0:T(8,128)(2,1)} %collective-permute-done.13), channel_id=1, source_target_pairs={{0,4},{1,5},{2,6},{3,7},{4,0},{5,1},{6,2},{7,3},{8,12},{9,13},{10,... | collective-permute-start | bytes 2359304 | tf_op jit(solution)/shard_map/ppermute | solution.py:774
  246.6 37.4 %collective-permute-start.18 = (bf16[768,1024]{1,0:T(8,128)(2,1)}, bf16[768,1024]{1,0:T(8,128)(2,1)S(1)}, u32[]{:S(2)}, u32[]{:S(2)}) collective-permute-start(bf16[768,1024]{1,0:T(8,128)(2,1)} %convolution_convert_fusion.7), channel_id=1, source_target_pairs={{0,2},{1,3},{2,0},{3,1},{4,6},{5,7},{6,4},{7,5},{8,10},{9,11},{10,... | collective-permute-start | bytes 4718600 | tf_op jit(solution)/shard_map/ppermute | solution.py:774
  248.4 83.6 %collective-permute-start.20 = (bf16[512,1536]{1,0:T(8,128)(2,1)}, bf16[512,1536]{1,0:T(8,128)(2,1)}, u32[]{:S(2)}, u32[]{:S(2)}) collective-permute-start(bf16[512,1536]{1,0:T(8,128)(2,1)} %convolution_convert_fusion.2), channel_id=1, source_target_pairs={{0,2},{1,3},{2,0},{3,1},{4,6},{5,7},{6,4},{7,5},{8,10},{9,11},{10,... | collective-permute-start | bytes 4718600 | tf_op jit(solution)/shard_map/ppermute | solution.py:774
  248.7 116.8 %collective-permute-start.24 = (bf16[512,1536]{1,0:T(8,128)(2,1)}, bf16[512,1536]{1,0:T(8,128)(2,1)}, u32[]{:S(2)}, u32[]{:S(2)}) collective-permute-start(bf16[512,1536]{1,0:T(8,128)(2,1)} %convolution_convert_fusion), channel_id=1, source_target_pairs={{0,2},{1,3},{2,0},{3,1},{4,6},{5,7},{6,4},{7,5},{8,10},{9,11},{10,... | collective-permute-start | bytes 4718600 | tf_op jit(solution)/shard_map/ppermute | solution.py:774
  332.1 255.7 %all-reduce.14.cloned.1.call-start = ((), (), s32[]{:S(2)}) async-start(), calls=%async_computation.1 | async-start | bytes 2097152 | tf_op jit(solution)/shard_map/psum | solution.py:1073
  335.7 68.2 %collective-permute-start.19 = (bf16[512,1024]{1,0:T(8,128)(2,1)S(1)}, bf16[512,1024]{1,0:T(8,128)(2,1)S(1)}, u32[]{:S(2)}, u32[]{:S(2)}) collective-permute-start(bf16[512,1024]{1,0:T(8,128)(2,1)S(1)} %convolution_convert_fusion.13), channel_id=1, source_target_pairs={{0,2},{1,3},{2,0},{3,1},{4,6},{5,7},{6,4},{7,5},{8,10},{9,11},{10,... | collective-permute-start | bytes 3145736 | tf_op jit(solution)/shard_map/ppermute | solution.py:774
  337.5 152.0 %collective-permute-start.38 = (bf16[512,1024]{1,0:T(8,128)(2,1)}, bf16[512,1024]{1,0:T(8,128)(2,1)}, u32[]{:S(2)}, u32[]{:S(2)}) collective-permute-start(bf16[512,1024]{1,0:T(8,128)(2,1)} %convolution_convert_fusion.9), channel_id=1, source_target_pairs={{0,2},{1,3},{2,0},{3,1},{4,6},{5,7},{6,4},{7,5},{8,10},{9,11},{10,... | collective-permute-start | bytes 3145736 | tf_op jit(solution)/shard_map/ppermute | solution.py:774
  337.8 126.1 %collective-permute-start.33 = (bf16[512,1024]{1,0:T(8,128)(2,1)}, bf16[512,1024]{1,0:T(8,128)(2,1)}, u32[]{:S(2)}, u32[]{:S(2)}) collective-permute-start(bf16[512,1024]{1,0:T(8,128)(2,1)} %convolution_convert_fusion.11), channel_id=1, source_target_pairs={{0,2},{1,3},{2,0},{3,1},{4,6},{5,7},{6,4},{7,5},{8,10},{9,11},{10,... | collective-permute-start | bytes 3145736 | tf_op jit(solution)/shard_map/ppermute | solution.py:774
  378.4 22.6 %collective-permute-start.27 = (bf16[256,1536]{1,0:T(8,128)(2,1)S(1)}, bf16[256,1536]{1,0:T(8,128)(2,1)S(1)}, u32[]{:S(2)}, u32[]{:S(2)}) collective-permute-start(bf16[256,1536]{1,0:T(8,128)(2,1)S(1)} %get-tuple-element.316), channel_id=1, source_target_pairs={{0,4},{1,5},{2,6},{3,7},{4,0},{5,1},{6,2},{7,3},{8,12},{9,13},{10,... | collective-permute-start | bytes 2359304 | tf_op jit(solution)/shard_map/ppermute | solution.py:774
  405.5 38.8 %collective-permute-start.28 = (bf16[256,1024]{1,0:T(8,128)(2,1)}, bf16[256,1024]{1,0:T(8,128)(2,1)}, u32[]{:S(2)}, u32[]{:S(2)}) collective-permute-start(bf16[256,1024]{1,0:T(8,128)(2,1)} %get-tuple-element.300), channel_id=1, source_target_pairs={{0,1},{1,0},{2,3},{3,2},{4,5},{5,4},{6,7},{7,6},{8,9},{9,8},{10,11... | collective-permute-start | bytes 1572872 | tf_op jit(solution)/shard_map/ppermute | solution.py:774
  405.6 30.9 %collective-permute-start.30 = (bf16[128,1536]{1,0:T(8,128)(2,1)S(1)}, bf16[128,1536]{1,0:T(8,128)(2,1)S(1)}, u32[]{:S(2)}, u32[]{:S(2)}) collective-permute-start(bf16[128,1536]{1,0:T(8,128)(2,1)S(1)} %get-tuple-element.362), channel_id=1, source_target_pairs={{0,8},{1,9},{2,10},{3,11},{4,12},{5,13},{6,14},{7,15},{8,0},{9,1},... | collective-permute-start | bytes 1179656 | tf_op jit(solution)/shard_map/ppermute | solution.py:774
  419.9 39.4 %collective-permute-start.35 = (bf16[128,1536]{1,0:T(8,128)(2,1)S(1)}, bf16[128,1536]{1,0:T(8,128)(2,1)}, u32[]{:S(2)}, u32[]{:S(2)}) collective-permute-start(bf16[128,1536]{1,0:T(8,128)(2,1)S(1)} %pad_maximum_fusion.34), channel_id=1, source_target_pairs={{0,8},{1,9},{2,10},{3,11},{4,12},{5,13},{6,14},{7,15},{8,0},{9,1},... | collective-permute-start | bytes 1179656 | tf_op jit(solution)/shard_map/ppermute | solution.py:774
  439.4 22.5 %collective-permute-start.34 = (bf16[64,1536]{1,0:T(8,128)(2,1)S(1)}, bf16[64,1536]{1,0:T(8,128)(2,1)S(1)}, u32[]{:S(2)}, u32[]{:S(2)}) collective-permute-start(bf16[64,1536]{1,0:T(8,128)(2,1)S(1)} %get-tuple-element.386), channel_id=1, source_target_pairs={{0,16},{1,17},{2,18},{3,19},{4,20},{5,21},{6,22},{7,23},{8,24},{9,... | collective-permute-start | bytes 589832 | tf_op jit(solution)/shard_map/ppermute | solution.py:774
  468.1 24.0 %collective-permute-start.37 = (bf16[64,1024]{1,0:T(8,128)(2,1)S(1)}, bf16[64,1024]{1,0:T(8,128)(2,1)S(1)}, u32[]{:S(2)}, u32[]{:S(2)}) collective-permute-start(bf16[64,1024]{1,0:T(8,128)(2,1)S(1)} %get-tuple-element.398), channel_id=1, source_target_pairs={{0,16},{1,17},{2,18},{3,19},{4,20},{5,21},{6,22},{7,23},{8,24},{9,... | collective-permute-start | bytes 393224 | tf_op jit(solution)/shard_map/ppermute | solution.py:774
  522.6 26.7 %collective-permute-start.53 = (bf16[64,1024]{1,0:T(8,128)(2,1)S(1)}, bf16[64,1024]{1,0:T(8,128)(2,1)S(1)}, u32[]{:S(2)}, u32[]{:S(2)}) collective-permute-start(bf16[64,1024]{1,0:T(8,128)(2,1)S(1)} %add_convert_fusion.22), channel_id=1, source_target_pairs={{0,16},{1,17},{2,18},{3,19},{4,20},{5,21},{6,22},{7,23},{8,24},{9,... | collective-permute-start | bytes 393224 | tf_op jit(solution)/shard_map/ppermute | solution.py:774
  526.9 42.9 %collective-permute-start.52 = (bf16[256,1024]{1,0:T(8,128)(2,1)S(1)}, bf16[256,1024]{1,0:T(8,128)(2,1)}, u32[]{:S(2)}, u32[]{:S(2)}) collective-permute-start(bf16[256,1024]{1,0:T(8,128)(2,1)S(1)} %pad_maximum_fusion.32), channel_id=1, source_target_pairs={{0,4},{1,5},{2,6},{3,7},{4,0},{5,1},{6,2},{7,3},{8,12},{9,13},{10,... | collective-permute-start | bytes 1572872 | tf_op jit(solution)/shard_map/ppermute | solution.py:774
  529.7 80.6 %collective-permute-start.51 = (bf16[256,1024]{1,0:T(8,128)(2,1)}, bf16[256,1024]{1,0:T(8,128)(2,1)}, u32[]{:S(2)}, u32[]{:S(2)}) collective-permute-start(bf16[256,1024]{1,0:T(8,128)(2,1)} %slice.447), channel_id=1, source_target_pairs={{0,2},{1,3},{2,0},{3,1},{4,6},{5,7},{6,4},{7,5},{8,10},{9,11},{10,... | collective-permute-start | bytes 1572872 | tf_op jit(solution)/shard_map/ppermute | solution.py:774
  534.6 60.1 %collective-permute-start.48 = (bf16[512,1024]{1,0:T(8,128)(2,1)}, bf16[512,1024]{1,0:T(8,128)(2,1)}, u32[]{:S(2)}, u32[]{:S(2)}) collective-permute-start(bf16[512,1024]{1,0:T(8,128)(2,1)} %pad_maximum_fusion.17), channel_id=1, source_target_pairs={{0,1},{1,0},{2,3},{3,2},{4,5},{5,4},{6,7},{7,6},{8,9},{9,8},{10,11... | collective-permute-start | bytes 3145736 | tf_op jit(solution)/shard_map/ppermute | solution.py:774
  (129 other events, 1210.3 us)
Sparse Core Ops, SparseCore 0:
  332.2 106.1 all-reduce.11
  498.9 88.8 all-reduce.13

commit v5 on v4

--- a/solution.py
+++ b/solution.py
@@ -897,17 +897,19 @@
     tokens = hidden.astype(f32)
     qkv.near = tie(qkv.near, gateup.chip)
     w_qkv = qkv.joined()
-    mixed = split_product(normed_low, w_qkv, 1, 0)
+    mixed = split_product(tie(normed_low, gateup.peer), w_qkv, 1, 0)
     block = min(256, seq_len)
     attended, totals = attend_forward(
-        tie(mixed, gateup.diagonal), cosine, sine, gain_query, gain_key, heads, ratio, block
-    )
-    branch = split_product(attended, w_out, 1, 0).astype(bf16)
+        tie(mixed, gateup.diagonal, gateup.chip_side), cosine, sine, gain_query, gain_key, heads, ratio, block
+    )
+    pinned = tie(attended, gateup.diagonal_side, down_chip)
+    branch = split_product(pinned, w_out, 1, 0).astype(bf16)
     middle = tokens + (branch.astype(f32) + over_core(branch).astype(f32))
     second, pull_two = jax.vjp(rms_scale, middle, gain_two)
     second_low = second.astype(bf16)
+    gateup.near = tie(gateup.near, grad_far)
     w_gateup = gateup.joined()
-    gate_up = split_product(second_low, w_gateup, 1, 0)
+    gate_up = split_product(tie(second_low, down_side), w_gateup, 1, 0)
 
     def gated_part(values, part):
         pieces_here = []
@@ -976,6 +978,11 @@
     def passed(value):
         token[0] = value
 
+    def all_sum(near, received):
+        value = add(*event(near, received))
+        passed(value)
+        return lax.psum(value, "dp")
+
     w_down = join_rows(down_weight, down_chip, down_side)
     down_near, down_received = exchange(
         far_columns(inner_low, True), far_columns(inner_low, False), grad_result
@@ -983,10 +990,12 @@
     grad_inner = split_product(tie(grad_result, down_near), w_down, 1, 1)
     (grad_gate_up,) = pull_gate(grad_inner)
     grad_gate_low = grad_gate_up.astype(bf16)
+    down_sum = all_sum(down_near, down_received)
+    sent_low = tie(grad_gate_low, token[0])
     second_near, second_far = half_columns(second_low, False), half_columns(second_low, True)
     part_cols = grad_gate_low.shape[1] // parts
     gateup_sent = [
-        exchange(second_far, second_near, grad_gate_low[:, part * part_cols : (part + 1) * part_cols])
+        exchange(second_far, second_near, sent_low[:, part * part_cols : (part + 1) * part_cols])
         for part in range(parts)
     ]
     second_part = split_product(grad_gate_low, w_gateup, 1, 1).astype(bf16)
@@ -1067,20 +1076,14 @@
             if self.level >= 0:
                 self.send_back()
 
-    def all_sum(near, received):
-        value = add(*event(near, received))
-        passed(value)
-        return lax.psum(value, "dp")
-
-    down_sum = all_sum(down_near, tie(down_received, grad_att))
-    grad_att = tie(grad_att, token[0])
+    out_received = over_chip(out_far)
     back_0 = backward_part(0, grad_att)
     qkv_0 = exchange(normed_far, normed_near, back_0[0])
     back_1 = backward_part(1, tie(grad_att, qkv_0[0]))
-    qkv_1 = exchange(normed_far, normed_near, back_1[0])
-    out_far = tie(out_far, qkv_1[0])
-    out_received = over_chip(tie(out_far, gateup_sent[0][1]))
-    gateup_0 = Summed(gateup_sent[0][0], tie(gateup_sent[0][1], qkv_1[0]))
+    far_1 = split_product(normed_far, back_1[0], 0, 0).astype(bf16)
+    near_1 = split_product(normed_near, back_1[0], 0, 0).astype(bf16)
+    gateup_0 = Summed(gateup_sent[0][0], tie(gateup_sent[0][1], near_1))
+    qkv_1 = (near_1, over_chip(tie(far_1, token[0])))
     normed_part = split_product(
         tie(back_0[0], token[0]), w_qkv[:, : 2 * wide], 1, 1
     ) + split_product(tie(back_1[0], token[0]), w_qkv[:, 2 * wide :], 1, 1)
@@ -1093,53 +1096,70 @@
     unused, pull_one = jax.vjp(rms_scale, own_tokens, gain_one)
     grad_token_part, grad_gain_one = pull_one(grad_normed)
     input_rows = (take_rows(grad_middle, own_targets, chunk) + grad_token_part).astype(bf16)
+    counted = jnp.where(rank == 0, 1.0, 0.0).astype(f32)
+    gain_state = [
+        jnp.concatenate(
+            [
+                grad_gain_one,
+                grad_gain_two * counted,
+                back_0[1] + back_1[1],
+                back_0[2] + back_1[2],
+            ]
+        )
+    ]
+    gain_moves = [over_core, over_chip] + [move for bit, move in levels]
+
+    def gain_step():
+        if len(gain_state) > 1:
+            value, received = event(*gain_state)
+            gain_state[:] = [value + received]
+            passed(gain_state[0])
+        if gain_moves:
+            gain_state.append(gain_moves.pop(0)(gain_state[0]))
+
     gateup_0.step()
     gateup_1.step()
     gateup_0.step()
-    summed_0 = Summed(*qkv_0)
+    gain_step()
     gateup_0.step()
     gateup_1.step()
     (down_sum,) = event(down_sum)
     passed(down_sum)
-    summed_0.step()
+    out_sum = all_sum(out_near, out_received)
+    summed_0 = Summed(*qkv_0)
+    gain_step()
     gateup_0.step()
     gateup_1.step()
+    summed_0.step()
+    gain_step()
+    gateup_1.step()
     summed_1 = Summed(*qkv_1)
+    layer_out = to_stored(
+        take_rows(middle, own_targets, chunk) + share_rows(tie(result_part, back_0[0]))
+    )
+    input_grad = to_stored(tie(input_rows, token[0]))
+    gateup_0.step()
+    gateup_1.step()
     summed_0.step()
-    gateup_1.step()
-    gateup_0.step()
-    summed_1.step()
-    out_sum = all_sum(out_near, out_received)
-    summed_0.step()
-    gateup_1.step()
+    gain_step()
     summed_1.step()
     summed_0.step()
     gateup_1.step()
     summed_1.step()
-    summed_0.step()
-    counted = jnp.where(rank == 0, 1.0, 0.0).astype(f32)
-    total_gains = jnp.concatenate(
-        [
-            grad_gain_one,
-            grad_gain_two * counted,
-            back_0[1] + back_1[1],
-            back_0[2] + back_1[2],
-        ]
-    )
-    layer_out = to_stored(
-        take_rows(middle, own_targets, chunk) + share_rows(tie(result_part, token[0]))
-    )
-    input_grad = to_stored(tie(input_rows, token[0]))
-    for move in (over_core, over_chip):
-        total_gains = total_gains + move(tie(total_gains, token[0]))
-    summed_1.step()
-    for bit, move in levels:
-        total_gains = total_gains + move(tie(total_gains, token[0]))
+    gain_step()
     summed_0.step()
     summed_1.step()
+    gain_step()
+    summed_0.step()
+    summed_1.step()
+    summed_1.step()
+    summed_0.step()
     for summed in (gateup_0, gateup_1, summed_0, summed_1):
         while summed.level >= 0:
             summed.step()
+    while len(gain_state) > 1:
+        gain_step()
+    total_gains = gain_state[0]
     gateup_sums = [gateup_0.value, gateup_1.value]
     qkv_sums = [summed_0.value, summed_1.value]
     total_down = down_sum.astype(f32)

time: 631 us -> 696 us (1.10)
  waiting for transfers between devices: 206 us -> 274 us
  local copies, waits for them, and re-layouts: 46 us -> 37.2 us
    psum x2, waiting for transfers between devices: 4.55 us -> 52.1 us  [all_sum(): return lax.psum(value, 'dp')]
    ppermute x61, waiting for transfers between devices: 202 us -> 222 us  [permute(): return lax.ppermute(value, ALL, pairs)]
    unnamed x239 -> x271, local copies, waits for them, and re-layouts: 28.2 us -> 20.9 us
  transfers between devices with their start and end apart: 63 -> 63, of which waited for: 32 -> 27; matrix products, arithmetic and copies ran while one was open for 25% -> 24% of each run, Pallas kernels for 12% -> 14%
where the time goes in v5:
time: 696 us; the launch traced here: 686 us
  waiting for transfers between devices  274 us (39%)
  other arithmetic  110 us (16%)
  Pallas kernels  95.5 us (14%)
  matrix products  84.9 us (12%)
  starting transfers between devices  61.2 us (9%)
  local copies, waits for them, and re-layouts  37.2 us (5%)
  between operations  22.7 us (3%)
    ppermute x61, waiting for transfers between devices, permute(): return lax.ppermute(value, ALL, pairs)  222 us
    dot_general x21, matrix products, split_product(): lax.dot_general(left, right, (((left_dim,), (right_dim,)), ((), ())), pre...  84.9 us
    ppermute x61, starting transfers between devices, permute(): return lax.ppermute(value, ALL, pairs)  61.1 us
    psum x2, waiting for transfers between devices, all_sum(): return lax.psum(value, 'dp')  52.1 us
    pallas_call x2, Pallas kernels, attend_backward(): pl.pallas_call(kernel, grid=(heads,), in_specs=[pl.BlockSpec((rows, wide)...  36.2 us
    sub x5, other arithmetic, adam_step(): return (weight - rate * (ratio + decay * weight), moment_new, square_new)  29.9 us
    pallas_call x1, Pallas kernels, attend_forward(): pl.pallas_call(kernel, grid=(heads,), in_specs=[pl.BlockSpec((rows, wide)...  22 us
    unnamed x271, local copies, waits for them, and re-layouts  20.9 us
  transfers between devices with their start and end apart: 63, of which 27 were waited for; matrix products, arithmetic and copies ran while one was open for 24% of the time, Pallas kernels for 14%

profile of v5, /device:TPU:0, one launch (start us, length us, event | category | flops | bytes accessed | tf_op | source)
XLA Modules:
  0.0 685.7 jit_solution(14464332379237524703)
XLA Ops:
  14.1 6.1 cut_columns.2
  21.4 6.4 collective-permute-done
  32.9 7.7 %cut_columns.3 = (bf16[256,1536]{1,0:T(8,128)(2,1)}, bf16[256,1536]{1,0:T(8,128)(2,1)}, bf16[2,256,1536]{2,1,0:T(8,128)(2,1)S(1)}, bf16[256,1536]{1,0:T(8,128)(2...) custom-call(s32[3]{0:T(128)S(1)} %pad_add_fusion.at_ref, f32[256,6144]{1,0:T(8,128)} %refs_1_.1, ...), custom_call_target="tpu_custom_call" | custom-call | flops 1000000 | bytes 100000 | tf_op jit(solution)/shard_map/cut_columns/pallas_call | solution.py:437
  53.7 7.4 %collective-permute-done.6.diag_ref = bf16[256,1024]{1,0:T(8,128)(2,1)} collective-permute-done((bf16[256,1024]{1,0:T(8,128)(2,1)}, bf16[256,1024]{1,0:T(8,128)(2,1)}, u32[]{:S(2)}, u32[]{:S(2)}) %collective-permute-start.6) | collective-permute-done | bytes 524320 | tf_op jit(solution)/shard_map/ppermute | solution.py:774
  62.6 14.9 %collective-permute-done.4.chip_ref = bf16[256,1536]{1,0:T(8,128)(2,1)} collective-permute-done((bf16[256,1536]{1,0:T(8,128)(2,1)}, bf16[256,1536]{1,0:T(8,128)(2,1)}, u32[]{:S(2)}, u32[]{:S(2)}) %collective-permute-start.4) | collective-permute-done | bytes 786464 | tf_op jit(solution)/shard_map/ppermute | solution.py:774
  80.9 7.0 %place_rows.2 = (bf16[1024,1024]{1,0:T(8,128)(2,1)}, bf16[1024,1024]{1,0:T(8,128)(2,1)}) custom-call(s32[8]{0:T(128)} %copy-done.93, bf16[544,1024]{1,0:T(8,128)(2,1)} %pad_maximum_fusion.12.mine_ref, bf16[544,1024]{1,0:T(8,128)(2,1)} %collective-permute-done.1.theirs_ref, f32[1,1024]{1,0:T(1,128)} %bitcast.200), custom_call_target="tpu_custom_call" | custom-call | flops 1000000 | bytes 100000 | tf_op jit(solution)/shard_map/place_rows/pallas_call | solution.py:375
  87.9 9.5 %collective-permute-done.9.diag_ref = bf16[256,1536]{1,0:T(8,128)(2,1)} collective-permute-done((bf16[256,1536]{1,0:T(8,128)(2,1)}, bf16[256,1536]{1,0:T(8,128)(2,1)}, u32[]{:S(2)}, u32[]{:S(2)}) %collective-permute-start.9) | collective-permute-done | bytes 786464 | tf_op jit(solution)/shard_map/ppermute | solution.py:774
  106.4 8.9 %fusion.112.mixed_ref = f32[1024,2048]{1,0:T(8,128)} fusion(bf16[1024,1024]{1,0:T(8,128)(2,1)S(1)} %copy-done.101, bf16[1024,2048]{1,0:T(8,128)(2,1)} %join_columns.2), kind=kOutput, calls=%fused_computation.424 | convolution fusion | flops 4294967296 | bytes 14680064 | tf_op jit(solution)/shard_map/dot_general | solution.py:339
  116.2 22.0 %attend_forward.1 = (bf16[1024,1024]{1,0:T(8,128)(2,1)S(1)}, f32[1024,512]{1,0:T(8,128)S(1)}) custom-call(f32[1024,2048]{1,0:T(8,128)} %fusion.112.mixed_ref, f32[1024,128]{1,0:T(8,128)S(1)} %pad_maximum_fusion.30.cos_ref, f32[1024,128]{1,0:T(8,128)S(1)} %pad_maximum_fusion.31.sin_ref, f32[1,128]{1,0:T(1,128)S(1)} %get-tuple-element.419.gq_ref, ...), custom_call_target="tpu_custom_call" | custom-call | flops 1000000 | bytes 100000 | tf_op jit(solution)/shard_map/attend_forward/pallas_call | solution.py:578
  143.4 13.0 %collective-permute-done.15 = bf16[256,1024]{1,0:T(8,128)(2,1)S(1)} collective-permute-done((bf16[256,1024]{1,0:T(8,128)(2,1)S(1)}, bf16[256,1024]{1,0:T(8,128)(2,1)S(1)}, u32[]{:S(2)}, u32[]{:S(2)}) %collective-permute-start.15) | collective-permute-done | bytes 524320 | tf_op jit(solution)/shard_map/ppermute | solution.py:774
  174.6 6.5 place_rows.3
  189.6 6.7 fusion.113
  210.0 7.6 %slice_multiply_fusion.3 = (f32[1024,384]{1,0:T(8,128)}, f32[1024,384]{1,0:T(8,128)}, f32[1024,384]{1,0:T(8,128)}, f32[1024,384]{1,0:T(8,128)}, f32[1024,384]{1,...) fusion(f32[1024,1536]{1,0:T(8,128)} %copy-done.28, f32[1024,3072]{1,0:T(8,128)S(1)} %fusion.113), kind=kLoop, calls=%fused_computation.135 | loop fusion | flops 18087936 | bytes 29884416 | tf_op jit(solution)/shard_map/transpose(jvp())/mul | solution.py:919
  227.2 11.9 %convolution_convert_fusion.6 = bf16[1024,1024]{1,0:T(8,128)(2,1)} fusion(bf16[1024,3072]{1,0:T(8,128)(2,1)} %add_convert_fusion, bf16[1024,3072]{1,0:T(8,128)(2,1)} %join_columns.3), kind=kOutput, calls=%fused_computation.87 | convolution fusion | flops 6443499520 | bytes 14680064 | tf_op jit(solution)/shard_map/dot_general | solution.py:339
  246.7 10.7 %collective-permute-done.20 = bf16[768,1024]{1,0:T(8,128)(2,1)S(1)} collective-permute-done((bf16[768,1024]{1,0:T(8,128)(2,1)}, bf16[768,1024]{1,0:T(8,128)(2,1)S(1)}, u32[]{:S(2)}, u32[]{:S(2)}) %collective-permute-start.20) | collective-permute-done | bytes 1572896 | tf_op jit(solution)/shard_map/ppermute | solution.py:774
  289.1 18.2 %attend_backward.2 = (bf16[1024,1024]{1,0:T(8,128)(2,1)S(1)}, f32[1,128]{1,0:T(1,128)S(1)}, f32[1,128]{1,0:T(1,128)S(1)}) custom-call(f32[1024,2048]{1,0:T(8,128)} %fusion.112.mixed_ref, f32[1024,128]{1,0:T(8,128)S(1)} %pad_maximum_fusion.30.cos_ref, f32[1024,128]{1,0:T(8,128)S(1)} %pad_maximum_fusion.31.sin_ref, f32[1,128]{1,0:T(1,128)S(1)} %get-tuple-element.419.gq_ref, ...), custom_call_target="tpu_custom_call" | custom-call | flops 1000000 | bytes 100000 | tf_op jit(solution)/shard_map/attend_backward/pallas_call | solution.py:698
  316.3 18.0 %attend_backward.3 = (bf16[1024,1024]{1,0:T(8,128)(2,1)S(1)}, f32[1,128]{1,0:T(1,128)S(1)}, f32[1,128]{1,0:T(1,128)S(1)}) custom-call(f32[1024,2048]{1,0:T(8,128)} %fusion.112.mixed_ref, f32[1024,128]{1,0:T(8,128)S(1)} %pad_maximum_fusion.30.cos_ref, f32[1024,128]{1,0:T(8,128)S(1)} %pad_maximum_fusion.31.sin_ref, f32[1,128]{1,0:T(1,128)S(1)} %get-tuple-element.419.gq_ref, ...), custom_call_target="tpu_custom_call" | custom-call | flops 1000000 | bytes 100000 | tf_op jit(solution)/shard_map/attend_backward/pallas_call | solution.py:698
  348.2 45.6 %collective-permute-done.19 = bf16[256,1024]{1,0:T(8,128)(2,1)} collective-permute-done((bf16[256,1024]{1,0:T(8,128)(2,1)}, bf16[256,1024]{1,0:T(8,128)(2,1)}, u32[]{:S(2)}, u32[]{:S(2)}) %collective-permute-start.19) | collective-permute-done | bytes 524320 | tf_op jit(solution)/shard_map/ppermute | solution.py:774
  406.3 17.4 %collective-permute-done.26 = bf16[256,1536]{1,0:T(8,128)(2,1)S(1)} collective-permute-done((bf16[256,1536]{1,0:T(8,128)(2,1)S(1)}, bf16[256,1536]{1,0:T(8,128)(2,1)S(1)}, u32[]{:S(2)}, u32[]{:S(2)}) %collective-permute-start.26) | collective-permute-done | bytes 786464 | tf_op jit(solution)/shard_map/ppermute | solution.py:774
  439.5 6.1 collective-permute-done.29
  455.8 8.9 %collective-permute-done.31 = bf16[64,1536]{1,0:T(8,128)(2,1)S(1)} collective-permute-done((bf16[64,1536]{1,0:T(8,128)(2,1)S(1)}, bf16[64,1536]{1,0:T(8,128)(2,1)S(1)}, u32[]{:S(2)}, u32[]{:S(2)}) %collective-permute-start.31) | collective-permute-done | bytes 196640 | tf_op jit(solution)/shard_map/ppermute | solution.py:774
  464.9 10.9 %collective-permute-done.32 = bf16[64,1536]{1,0:T(8,128)(2,1)S(1)} collective-permute-done((bf16[64,1536]{1,0:T(8,128)(2,1)S(1)}, bf16[64,1536]{1,0:T(8,128)(2,1)S(1)}, u32[]{:S(2)}, u32[]{:S(2)}) %collective-permute-start.32) | collective-permute-done | bytes 196640 | tf_op jit(solution)/shard_map/ppermute | solution.py:774
  476.0 11.0 %collective-permute-done.30 = bf16[128,1536]{1,0:T(8,128)(2,1)S(1)} collective-permute-done((bf16[128,1536]{1,0:T(8,128)(2,1)S(1)}, bf16[128,1536]{1,0:T(8,128)(2,1)S(1)}, u32[]{:S(2)}, u32[]{:S(2)}) %collective-permute-start.30) | collective-permute-done | bytes 393248 | tf_op jit(solution)/shard_map/ppermute | solution.py:774
  496.9 6.3 multiply_subtract_fusion.2
  512.5 8.6 %collective-permute-done.41 = bf16[256,1024]{1,0:T(8,128)(2,1)S(1)} collective-permute-done((bf16[256,1024]{1,0:T(8,128)(2,1)S(1)}, bf16[256,1024]{1,0:T(8,128)(2,1)S(1)}, u32[]{:S(2)}, u32[]{:S(2)}) %collective-permute-start.41) | collective-permute-done | bytes 524320 | tf_op jit(solution)/shard_map/ppermute | solution.py:774
  525.2 52.1 %all-reduce.14.cloned.1.call-done = bf16[512,1024]{1,0:T(8,128)(2,1)} async-done(((bf16[512,1024]{1,0:T(8,128)(2,1)}), bf16[512,1024]{1,0:T(8,128)(2,1)}) %all-reduce.14.cloned.1.call-update) | async-done | bytes 1048592 | tf_op jit(solution)/shard_map/psum | solution.py:984
  577.3 6.7 multiply_subtract_fusion.3
  611.3 8.2 %collective-permute-done.53 = bf16[256,1536]{1,0:T(8,128)(2,1)S(1)} collective-permute-done((bf16[256,1536]{1,0:T(8,128)(2,1)S(1)}, bf16[256,1536]{1,0:T(8,128)(2,1)S(1)}, u32[]{:S(2)}, u32[]{:S(2)}) %collective-permute-start.53) | collective-permute-done | bytes 786464 | tf_op jit(solution)/shard_map/ppermute | solution.py:774
  635.1 10.5 %multiply_subtract_fusion = (f32[256,6144]{1,0:T(8,128)}, f32[256,6144]{1,0:T(8,128)}, f32[256,6144]{1,0:T(8,128)}) fusion(f32[256,6144]{1,0:T(8,128)S(1)} %bitcast.171, bf16[256,6144]{1,0:T(8,128)(2,1)S(1)} %slice_dynamic-update-slice_fusion, f32[256,6144]{1,0:T(8,128)S(1)} %bitcast.173, f32[256,6144]{1,0:T(8,128)} %param.31), kind=kLoop, calls=%fused_computation.5 | loop fusion | flops 25165824 | bytes 40894464 | tf_op jit(solution)/shard_map/sub | solution.py:93
  649.6 11.2 %collective-permute-done.57 = bf16[256,1024]{1,0:T(8,128)(2,1)S(1)} collective-permute-done((bf16[256,1024]{1,0:T(8,128)(2,1)}, bf16[256,1024]{1,0:T(8,128)(2,1)S(1)}, u32[]{:S(2)}, u32[]{:S(2)}) %collective-permute-start.57) | collective-permute-done | bytes 524320 | tf_op jit(solution)/shard_map/ppermute | solution.py:774
  661.0 6.7 collective-permute-done.60
  672.6 5.8 multiply_subtract_fusion.1
  (547 shorter events, 264.3 us)
Async XLA Ops:
  7.2 480.1 %all-reduce.12.cloned.1.call-start = ((), (), s32[]{:S(2)}) async-start(), calls=%async_computation | async-start | bytes 3145728 | tf_op jit(solution)/shard_map/psum | solution.py:984
  20.2 26.1 %collective-permute-start.2 = (bf16[2,256,1024]{2,1,0:T(8,128)(2,1)}, bf16[2,256,1024]{2,1,0:T(8,128)(2,1)S(1)}, u32[]{:S(2)}, u32[]{:S(2)}) collective-permute-start(bf16[2,256,1024]{2,1,0:T(8,128)(2,1)} %get-tuple-element.139), channel_id=1, source_target_pairs={{0,1},{1,0},{2,3},{3,2},{4,5},{5,4},{6,7},{7,6},{8,9},{9,8},{10,11... | collective-permute-start | bytes 3145736 | tf_op jit(solution)/shard_map/ppermute | solution.py:774
  21.4 28.9 %collective-permute-start.5 = (bf16[2,256,1024]{2,1,0:T(8,128)(2,1)}, bf16[2,256,1024]{2,1,0:T(8,128)(2,1)}, u32[]{:S(2)}, u32[]{:S(2)}) collective-permute-start(bf16[2,256,1024]{2,1,0:T(8,128)(2,1)} %pad_maximum_fusion.13), channel_id=1, source_target_pairs={{0,2},{1,3},{2,0},{3,1},{4,6},{5,7},{6,4},{7,5},{8,10},{9,11},{10,... | collective-permute-start | bytes 3145736 | tf_op jit(solution)/shard_map/ppermute | solution.py:774
  30.7 47.1 %collective-permute-start.1 = (bf16[544,1024]{1,0:T(8,128)(2,1)}, bf16[544,1024]{1,0:T(8,128)(2,1)}, u32[]{:S(2)}, u32[]{:S(2)}) collective-permute-start(bf16[544,1024]{1,0:T(8,128)(2,1)} %pad_maximum_fusion.12.mine_ref), channel_id=1, source_target_pairs={{0,1},{1,0},{2,3},{3,2},{4,5},{5,4},{6,7},{7,6},{8,9},{9,8},{10,11... | collective-permute-start | bytes 3342344 | tf_op jit(solution)/shard_map/ppermute | solution.py:774
  30.7 30.4 %collective-permute-start.6 = (bf16[256,1024]{1,0:T(8,128)(2,1)}, bf16[256,1024]{1,0:T(8,128)(2,1)}, u32[]{:S(2)}, u32[]{:S(2)}) collective-permute-start(bf16[256,1024]{1,0:T(8,128)(2,1)} %get-tuple-element.136), channel_id=1, source_target_pairs={{0,3},{1,2},{2,1},{3,0},{4,7},{5,6},{6,5},{7,4},{8,11},{9,10},{10,... | collective-permute-start | bytes 1572872 | tf_op jit(solution)/shard_map/ppermute | solution.py:774
  43.7 33.8 %collective-permute-start.4 = (bf16[256,1536]{1,0:T(8,128)(2,1)}, bf16[256,1536]{1,0:T(8,128)(2,1)}, u32[]{:S(2)}, u32[]{:S(2)}) collective-permute-start(bf16[256,1536]{1,0:T(8,128)(2,1)} %get-tuple-element.144), channel_id=1, source_target_pairs={{0,2},{1,3},{2,0},{3,1},{4,6},{5,7},{6,4},{7,5},{8,10},{9,11},{10,... | collective-permute-start | bytes 2359304 | tf_op jit(solution)/shard_map/ppermute | solution.py:774
  46.4 60.0 %collective-permute-start.3 = (bf16[2,256,1536]{2,1,0:T(8,128)(2,1)}, bf16[2,256,1536]{2,1,0:T(8,128)(2,1)}, u32[]{:S(2)}, u32[]{:S(2)}) collective-permute-start(bf16[2,256,1536]{2,1,0:T(8,128)(2,1)} %copy-done.23), channel_id=1, source_target_pairs={{0,1},{1,0},{2,3},{3,2},{4,5},{5,4},{6,7},{7,6},{8,9},{9,8},{10,11... | collective-permute-start | bytes 4718600 | tf_op jit(solution)/shard_map/ppermute | solution.py:774
  50.3 49.1 %collective-permute-start.7 = (bf16[2,256,1024]{2,1,0:T(8,128)(2,1)}, bf16[2,256,1024]{2,1,0:T(8,128)(2,1)}, u32[]{:S(2)}, u32[]{:S(2)}) collective-permute-start(bf16[2,256,1024]{2,1,0:T(8,128)(2,1)} %collective-permute-done.5), channel_id=1, source_target_pairs={{0,4},{1,5},{2,6},{3,7},{4,0},{5,1},{6,2},{7,3},{8,12},{9,13},{10,... | collective-permute-start | bytes 3145736 | tf_op jit(solution)/shard_map/ppermute | solution.py:774
  61.1 40.7 %collective-permute-start.8 = (bf16[256,1024]{1,0:T(8,128)(2,1)}, bf16[256,1024]{1,0:T(8,128)(2,1)S(1)}, u32[]{:S(2)}, u32[]{:S(2)}) collective-permute-start(bf16[256,1024]{1,0:T(8,128)(2,1)} %collective-permute-done.6.diag_ref), channel_id=1, source_target_pairs={{0,4},{1,5},{2,6},{3,7},{4,0},{5,1},{6,2},{7,3},{8,12},{9,13},{10,... | collective-permute-start | bytes 1572872 | tf_op jit(solution)/shard_map/ppermute | solution.py:774
  77.9 37.5 %collective-permute-start.10 = (bf16[256,1536]{1,0:T(8,128)(2,1)}, bf16[256,1536]{1,0:T(8,128)(2,1)S(1)}, u32[]{:S(2)}, u32[]{:S(2)}) collective-permute-start(bf16[256,1536]{1,0:T(8,128)(2,1)} %collective-permute-done.4.chip_ref), channel_id=1, source_target_pairs={{0,4},{1,5},{2,6},{3,7},{4,0},{5,1},{6,2},{7,3},{8,12},{9,13},{10,... | collective-permute-start | bytes 2359304 | tf_op jit(solution)/shard_map/ppermute | solution.py:774
  97.4 40.8 %collective-permute-start.11 = (bf16[256,1536]{1,0:T(8,128)(2,1)}, bf16[256,1536]{1,0:T(8,128)(2,1)S(1)}, u32[]{:S(2)}, u32[]{:S(2)}) collective-permute-start(bf16[256,1536]{1,0:T(8,128)(2,1)} %collective-permute-done.9.diag_ref), channel_id=1, source_target_pairs={{0,4},{1,5},{2,6},{3,7},{4,0},{5,1},{6,2},{7,3},{8,12},{9,13},{10,... | collective-permute-start | bytes 2359304 | tf_op jit(solution)/shard_map/ppermute | solution.py:774
  99.4 38.9 %collective-permute-start.12 = (bf16[384,1024]{1,0:T(8,128)(2,1)}, bf16[384,1024]{1,0:T(8,128)(2,1)}, u32[]{:S(2)}, u32[]{:S(2)}) collective-permute-start(bf16[384,1024]{1,0:T(8,128)(2,1)} %get-tuple-element.153), channel_id=1, source_target_pairs={{0,2},{1,3},{2,0},{3,1},{4,6},{5,7},{6,4},{7,5},{8,10},{9,11},{10,... | collective-permute-start | bytes 2359304 | tf_op jit(solution)/shard_map/ppermute | solution.py:774
  141.9 40.9 %collective-permute-start.13 = (bf16[1024,1024]{1,0:T(8,128)(2,1)}, bf16[1024,1024]{1,0:T(8,128)(2,1)}, u32[]{:S(2)}, u32[]{:S(2)}) collective-permute-start(bf16[1024,1024]{1,0:T(8,128)(2,1)} %convolution_convert_fusion.5), channel_id=1, source_target_pairs={{0,1},{1,0},{2,3},{3,2},{4,5},{5,4},{6,7},{7,6},{8,9},{9,8},{10,11... | collective-permute-start | bytes 6291464 | tf_op jit(solution)/shard_map/ppermute | solution.py:774
  157.5 23.7 %collective-permute-start.14 = (bf16[384,1024]{1,0:T(8,128)(2,1)}, bf16[384,1024]{1,0:T(8,128)(2,1)}, u32[]{:S(2)}, u32[]{:S(2)}) collective-permute-start(bf16[384,1024]{1,0:T(8,128)(2,1)} %collective-permute-done.12), channel_id=1, source_target_pairs={{0,4},{1,5},{2,6},{3,7},{4,0},{5,1},{6,2},{7,3},{8,12},{9,13},{10,... | collective-permute-start | bytes 2359304 | tf_op jit(solution)/shard_map/ppermute | solution.py:774
  220.6 36.7 %collective-permute-start.20 = (bf16[768,1024]{1,0:T(8,128)(2,1)}, bf16[768,1024]{1,0:T(8,128)(2,1)S(1)}, u32[]{:S(2)}, u32[]{:S(2)}) collective-permute-start(bf16[768,1024]{1,0:T(8,128)(2,1)} %convolution_convert_fusion.7), channel_id=1, source_target_pairs={{0,2},{1,3},{2,0},{3,1},{4,6},{5,7},{6,4},{7,5},{8,10},{9,11},{10,... | collective-permute-start | bytes 4718600 | tf_op jit(solution)/shard_map/ppermute | solution.py:774
  239.2 37.5 %collective-permute-start.17 = (bf16[1024,1024]{1,0:T(8,128)(2,1)}, bf16[1024,1024]{1,0:T(8,128)(2,1)}, u32[]{:S(2)}, u32[]{:S(2)}) collective-permute-start(bf16[1024,1024]{1,0:T(8,128)(2,1)} %convolution_convert_fusion.6), channel_id=1, source_target_pairs={{0,1},{1,0},{2,3},{3,2},{4,5},{5,4},{6,7},{7,6},{8,9},{9,8},{10,11... | collective-permute-start | bytes 6291464 | tf_op jit(solution)/shard_map/ppermute | solution.py:774
  264.9 78.6 %collective-permute-start.21 = (bf16[512,1536]{1,0:T(8,128)(2,1)}, bf16[512,1536]{1,0:T(8,128)(2,1)S(1)}, u32[]{:S(2)}, u32[]{:S(2)}) collective-permute-start(bf16[512,1536]{1,0:T(8,128)(2,1)} %convolution_convert_fusion.2), channel_id=1, source_target_pairs={{0,2},{1,3},{2,0},{3,1},{4,6},{5,7},{6,4},{7,5},{8,10},{9,11},{10,... | collective-permute-start | bytes 4718600 | tf_op jit(solution)/shard_map/ppermute | solution.py:774
  270.8 153.1 %collective-permute-start.25 = (bf16[512,1536]{1,0:T(8,128)(2,1)}, bf16[512,1536]{1,0:T(8,128)(2,1)}, u32[]{:S(2)}, u32[]{:S(2)}) collective-permute-start(bf16[512,1536]{1,0:T(8,128)(2,1)} %convolution_convert_fusion), channel_id=1, source_target_pairs={{0,2},{1,3},{2,0},{3,1},{4,6},{5,7},{6,4},{7,5},{8,10},{9,11},{10,... | collective-permute-start | bytes 4718600 | tf_op jit(solution)/shard_map/ppermute | solution.py:774
  316.3 24.8 %collective-permute-start.18 = (bf16[512,1024]{1,0:T(8,128)(2,1)}, bf16[512,1024]{1,0:T(8,128)(2,1)S(1)}, u32[]{:S(2)}, u32[]{:S(2)}) collective-permute-start(bf16[512,1024]{1,0:T(8,128)(2,1)} %pad_maximum_fusion.15), channel_id=1, source_target_pairs={{0,1},{1,0},{2,3},{3,2},{4,5},{5,4},{6,7},{7,6},{8,9},{9,8},{10,11... | collective-permute-start | bytes 3145736 | tf_op jit(solution)/shard_map/ppermute | solution.py:774
  334.3 158.5 %collective-permute-start.36 = (bf16[512,1024]{1,0:T(8,128)(2,1)}, bf16[512,1024]{1,0:T(8,128)(2,1)}, u32[]{:S(2)}, u32[]{:S(2)}) collective-permute-start(bf16[512,1024]{1,0:T(8,128)(2,1)} %convolution_convert_fusion.11), channel_id=1, source_target_pairs={{0,2},{1,3},{2,0},{3,1},{4,6},{5,7},{6,4},{7,5},{8,10},{9,11},{10,... | collective-permute-start | bytes 3145736 | tf_op jit(solution)/shard_map/ppermute | solution.py:774
  335.4 152.0 %collective-permute-start.37 = (bf16[512,1024]{1,0:T(8,128)(2,1)}, bf16[512,1024]{1,0:T(8,128)(2,1)}, u32[]{:S(2)}, u32[]{:S(2)}) collective-permute-start(bf16[512,1024]{1,0:T(8,128)(2,1)} %convolution_convert_fusion.9), channel_id=1, source_target_pairs={{0,2},{1,3},{2,0},{3,1},{4,6},{5,7},{6,4},{7,5},{8,10},{9,11},{10,... | collective-permute-start | bytes 3145736 | tf_op jit(solution)/shard_map/ppermute | solution.py:774
  342.4 51.3 %collective-permute-start.19 = (bf16[256,1024]{1,0:T(8,128)(2,1)}, bf16[256,1024]{1,0:T(8,128)(2,1)}, u32[]{:S(2)}, u32[]{:S(2)}) collective-permute-start(bf16[256,1024]{1,0:T(8,128)(2,1)} %slice.525), channel_id=1, source_target_pairs={{0,2},{1,3},{2,0},{3,1},{4,6},{5,7},{6,4},{7,5},{8,10},{9,11},{10,... | collective-permute-start | bytes 1572872 | tf_op jit(solution)/shard_map/ppermute | solution.py:774
  345.3 50.7 %collective-permute-start.22 = (bf16[256,1536]{1,0:T(8,128)(2,1)}, bf16[256,1536]{1,0:T(8,128)(2,1)}, u32[]{:S(2)}, u32[]{:S(2)}) collective-permute-start(bf16[256,1536]{1,0:T(8,128)(2,1)} %get-tuple-element.291), channel_id=1, source_target_pairs={{0,1},{1,0},{2,3},{3,2},{4,5},{5,4},{6,7},{7,6},{8,9},{9,8},{10,11... | collective-permute-start | bytes 2359304 | tf_op jit(solution)/shard_map/ppermute | solution.py:774
  348.1 229.2 %all-reduce.14.cloned.1.call-start = ((), (), s32[]{:S(2)}) async-start(), calls=%async_computation.1 | async-start | bytes 2097152 | tf_op jit(solution)/shard_map/psum | solution.py:984
  406.2 22.7 %collective-permute-start.23 = (bf16[512,1024]{1,0:T(8,128)(2,1)S(1)}, bf16[512,1024]{1,0:T(8,128)(2,1)S(1)}, u32[]{:S(2)}, u32[]{:S(2)}) collective-permute-start(bf16[512,1024]{1,0:T(8,128)(2,1)S(1)} %pad_maximum_fusion.18), channel_id=1, source_target_pairs={{0,1},{1,0},{2,3},{3,2},{4,5},{5,4},{6,7},{7,6},{8,9},{9,8},{10,11... | collective-permute-start | bytes 3145736 | tf_op jit(solution)/shard_map/ppermute | solution.py:774
  438.3 83.9 %collective-permute-start.24 = (bf16[512,1024]{1,0:T(8,128)(2,1)}, bf16[512,1024]{1,0:T(8,128)(2,1)}, u32[]{:S(2)}, u32[]{:S(2)}) collective-permute-start(bf16[512,1024]{1,0:T(8,128)(2,1)} %convolution_convert_fusion.12), channel_id=1, source_target_pairs={{0,2},{1,3},{2,0},{3,1},{4,6},{5,7},{6,4},{7,5},{8,10},{9,11},{10,... | collective-permute-start | bytes 3145736 | tf_op jit(solution)/shard_map/ppermute | solution.py:774
  445.6 76.5 %collective-permute-start.40 = (f32[2304]{0:T(1024)S(1)}, f32[2304]{0:T(1024)S(1)}, u32[]{:S(2)}, u32[]{:S(2)}) collective-permute-start(f32[2304]{0:T(1024)S(1)} %add.532), channel_id=1, source_target_pairs={{0,2},{1,3},{2,0},{3,1},{4,6},{5,7},{6,4},{7,5},{8,10},{9,11},{10,... | collective-permute-start | bytes 27656 | tf_op jit(solution)/shard_map/ppermute | solution.py:774
  487.4 21.8 %collective-permute-start.33 = (bf16[64,1536]{1,0:T(8,128)(2,1)S(1)}, bf16[64,1536]{1,0:T(8,128)(2,1)}, u32[]{:S(2)}, u32[]{:S(2)}) collective-permute-start(bf16[64,1536]{1,0:T(8,128)(2,1)S(1)} %get-tuple-element.400), channel_id=1, source_target_pairs={{0,16},{1,17},{2,18},{3,19},{4,20},{5,21},{6,22},{7,23},{8,24},{9,... | collective-permute-start | bytes 589832 | tf_op jit(solution)/shard_map/ppermute | solution.py:774
  509.2 81.2 %collective-permute-start.46 = (bf16[256,1536]{1,0:T(8,128)(2,1)}, bf16[256,1536]{1,0:T(8,128)(2,1)}, u32[]{:S(2)}, u32[]{:S(2)}) collective-permute-start(bf16[256,1536]{1,0:T(8,128)(2,1)} %pad_maximum_fusion.27), channel_id=1, source_target_pairs={{0,4},{1,5},{2,6},{3,7},{4,0},{5,1},{6,2},{7,3},{8,12},{9,13},{10,... | collective-permute-start | bytes 2359304 | tf_op jit(solution)/shard_map/ppermute | solution.py:774
  525.2 62.2 %collective-permute-start.42 = (bf16[256,1024]{1,0:T(8,128)(2,1)}, bf16[256,1024]{1,0:T(8,128)(2,1)}, u32[]{:S(2)}, u32[]{:S(2)}) collective-permute-start(bf16[256,1024]{1,0:T(8,128)(2,1)} %get-tuple-element.293), channel_id=1, source_target_pairs={{0,1},{1,0},{2,3},{3,2},{4,5},{5,4},{6,7},{7,6},{8,9},{9,8},{10,11... | collective-permute-start | bytes 1572872 | tf_op jit(solution)/shard_map/ppermute | solution.py:774
  587.4 22.7 %collective-permute-start.43 = (bf16[256,1024]{1,0:T(8,128)(2,1)S(1)}, bf16[256,1024]{1,0:T(8,128)(2,1)S(1)}, u32[]{:S(2)}, u32[]{:S(2)}) collective-permute-start(bf16[256,1024]{1,0:T(8,128)(2,1)S(1)} %slice.447), channel_id=1, source_target_pairs={{0,2},{1,3},{2,0},{3,1},{4,6},{5,7},{6,4},{7,5},{8,10},{9,11},{10,... | collective-permute-start | bytes 1572872 | tf_op jit(solution)/shard_map/ppermute | solution.py:774
  597.4 22.1 %collective-permute-start.53 = (bf16[256,1536]{1,0:T(8,128)(2,1)S(1)}, bf16[256,1536]{1,0:T(8,128)(2,1)S(1)}, u32[]{:S(2)}, u32[]{:S(2)}) collective-permute-start(bf16[256,1536]{1,0:T(8,128)(2,1)S(1)} %pad_maximum_fusion.28), channel_id=1, source_target_pairs={{0,4},{1,5},{2,6},{3,7},{4,0},{5,1},{6,2},{7,3},{8,12},{9,13},{10,... | collective-permute-start | bytes 2359304 | tf_op jit(solution)/shard_map/ppermute | solution.py:774
  (145 other events, 1311.3 us)
Sparse Core Ops, SparseCore 0:
  348.2 92.8 all-reduce.11
  492.9 84.3 all-reduce.13
